TPU v7x, 32 devices: a whole 2x2x4 slice. The times are simulated.
32 devices in a mesh: rows: 4 (over z), cols: 8 (over y, x, core).
Axes of the slice: x: 2, y: 2, z: 4, core: 2. Of those that a mesh axis runs over, the one named last changes fastest.
Arguments:
- observed: float32 [426, 64, 1024], P(None, 'rows', 'cols'), may hold values from 0.05 to 3
- nonlin: float32 [64, 1024], P('rows', 'cols'), may hold values from -0.3 to 0.3
- abundance: float32 [64, 64, 1024], P(None, 'rows', 'cols'), may hold values from 0 to 2
- spectra: float32 [426, 64], replicated, may hold values from 0.1 to 1
- kernels: float32 [8, 9, 9], replicated, may hold values from 0.003 to 0.03
- tile_family: int32 [4, 8], P('rows', 'cols'), may hold values from 0 to 7
Outputs:
- abundance_out: float32 [64, 64, 1024], P(None, 'rows', 'cols')
- spectra_out: float32 [426, 64], replicated
All inputs are finite; a program needn't handle non-finite values.
Results may differ from a plain program's by a relative error of at most 0.0003.
Values sent between devices are 32-bit elements; how exact they have to be, the bound alone decides.
No kernel may reach another device: no remote copies, remote signals or barrier semaphores. Data moves between devices by JAX's collectives and lax.ppermute only.
A program may use at most 64 MiB of HBM per device.

v0:
```python
import jax
import jax.numpy as jnp
from jax import lax
from jax.sharding import PartitionSpec as P

KS = 9
ITERS = 3


def padded_2(block, sides, width):
    for axis, dim in sides:
        count = lax.axis_size(axis)
        forward = [(i, i + 1) for i in range(count - 1)]
        backward = [(target, source) for source, target in forward]
        low = lax.ppermute(
            lax.slice_in_dim(block, block.shape[dim] - width, None, axis=dim), axis, forward
        )
        high = lax.ppermute(lax.slice_in_dim(block, 0, width, axis=dim), axis, backward)
        block = jnp.concatenate([low, block, high], axis=dim)
    return block


def shifted(block, axis, distance):
    devices = range(lax.axis_size(axis))
    route = [(i - distance, i) for i in devices if i - distance in devices]
    return lax.ppermute(block, axis, route)


def offset_table(width, radius):
    padded_cols = jnp.arange(width + 2 * radius, dtype=jnp.int32)[:, None]
    out_cols = jnp.arange(width, dtype=jnp.int32)[None, :]
    offset = padded_cols - out_cols
    return (offset[None] == jnp.arange(KS, dtype=jnp.int32)[:, None, None]).astype(jnp.float32)


def on_device(observed, nonlin, abundance, spectra, kernels, tile_family):
    highest = lax.Precision.HIGHEST
    bands, height, width = observed.shape
    channels = abundance.shape[0]
    radius = KS // 2
    pixel_count = height * width * lax.axis_size("rows") * lax.axis_size("cols")
    table = kernels.reshape(kernels.shape[0], KS * KS)
    family_ids = jnp.arange(table.shape[0], dtype=jnp.int32)
    own_pick = (family_ids == tile_family[0, 0]).astype(jnp.float32)
    own_kernel = jnp.dot(
        own_pick, table, precision=highest, preferred_element_type=jnp.float32
    ).reshape(KS, KS)
    forward_bands = jnp.einsum(
        "uv,vpj->upj", own_kernel, offset_table(width, radius), precision=highest
    )
    flat_pixels = observed.reshape(bands, height * width)
    bend = nonlin.reshape(1, height * width)
    current = abundance
    endmembers = spectra
    for step in range(ITERS):
        padded = padded_2(current, (("rows", 1), ("cols", 2)), radius)
        blurred = jnp.zeros((channels, height, width), jnp.float32)
        for row_shift in range(KS):
            blurred = blurred + jnp.dot(
                padded[:, row_shift : row_shift + height, :],
                forward_bands[row_shift],
                precision=highest,
                preferred_element_type=jnp.float32,
            )
        flat_blur = blurred.reshape(channels, height * width)
        linear = (
            jnp.dot(endmembers, flat_blur, precision=highest, preferred_element_type=jnp.float32)
            / channels
        )
        resid = linear + bend * linear * linear - flat_pixels
        weighted = resid * (1.0 + 2.0 * bend * linear)
        grad_flat = (
            lax.dot_general(
                endmembers,
                weighted,
                (((0,), (0,)), ((), ())),
                precision=highest,
                preferred_element_type=jnp.float32,
            )
            / channels
        )
        grad_local = (
            lax.dot_general(
                weighted,
                flat_blur,
                (((1,), (1,)), ((), ())),
                precision=highest,
                preferred_element_type=jnp.float32,
            )
            / channels
        )
        grad_blur = grad_flat.reshape(channels, height, width)
        spread = jnp.zeros((channels, height + 2 * radius, width + 2 * radius), jnp.float32)
        for row_shift in range(KS):
            contrib = lax.dot_general(
                grad_blur,
                forward_bands[row_shift],
                (((2,), (1,)), ((), ())),
                precision=highest,
                preferred_element_type=jnp.float32,
            )
            spread = spread + jnp.pad(
                contrib, ((0, 0), (row_shift, 2 * radius - row_shift), (0, 0))
            )
        middle = spread[:, radius : radius + height, :]
        from_above = shifted(spread[:, radius + height :, :], "rows", 1)
        from_below = shifted(spread[:, :radius, :], "rows", -1)
        middle = middle.at[:, :radius, :].add(from_above)
        middle = middle.at[:, height - radius :, :].add(from_below)
        grad_abund = middle[:, :, radius : radius + width]
        from_left = shifted(middle[:, :, radius + width :], "cols", 1)
        from_right = shifted(middle[:, :, :radius], "cols", -1)
        grad_abund = grad_abund.at[:, :, :radius].add(from_left)
        grad_abund = grad_abund.at[:, :, width - radius :].add(from_right)
        share = lax.psum_scatter(grad_local, "cols", scatter_dimension=1, tiled=True)
        share = lax.psum(share, "rows")
        share_width = share.shape[1]
        start = lax.axis_index("cols") * share_width
        own_spectra = lax.dynamic_slice_in_dim(endmembers, start, share_width, 1)
        updated = jnp.maximum(own_spectra - 40.0 * (share / pixel_count), 0.0)
        new_spectra = lax.all_gather(updated, "cols", axis=1, tiled=True)
        current = jnp.maximum(current - 0.5 * grad_abund, 0.0)
        endmembers = new_spectra
    return (current, endmembers)


def solution(mesh):
    placed = (
        P(None, "rows", "cols"),
        P("rows", "cols"),
        P(None, "rows", "cols"),
        P(),
        P(),
        P("rows", "cols"),
    )
    return jax.shard_map(
        on_device,
        mesh=mesh,
        in_specs=placed,
        out_specs=(P(None, "rows", "cols"), P()),
        check_vma=False,
    )
```

profile of v0, /device:TPU:1, one launch (start us, length us, event | category | flops | bytes accessed | tf_op | source)
XLA Modules:
  0.0 379.6 jit_solution(1648783574571566477)
XLA Ops:
  8.3 4.0 %collective-permute-start = (f32[64,4,128]{2,1,0:T(4,128)S(1)}, f32[64,4,128]{2,1,0:T(4,128)S(1)}, u32[]{:S(2)}, u32[]{:S(2)}) collective-permute-start(f32[64,4,128]{2,1,0:T(4,128)S(1)} %get-tuple-element.177), channel_id=1, source_target_pairs={{0,8},{8,16},{16,24},{1,9},{9,17},{17,25},{2,10},{10,18},{18,26},{... | collective-permute-start | bytes 393224 | tf_op jit(solution)/shard_map/ppermute | solution.py:15
  19.1 4.0 %collective-permute-start.3 = (f32[64,24,4]{0,1,2:T(8,128)S(1)}, f32[64,24,4]{0,1,2:T(8,128)S(1)}, u32[]{:S(2)}, u32[]{:S(2)}) collective-permute-start(f32[64,24,4]{0,1,2:T(8,128)S(1)} %copy.10), channel_id=1, source_target_pairs={{1,0},{2,1},{3,2},{4,3},{5,4},{6,5},{7,6},{9,8},{10,9},{11,10},{12... | collective-permute-start | bytes 73736 | tf_op jit(solution)/shard_map/ppermute | solution.py:18
  65.7 4.6 %collective-permute-done.4 = f32[64,4,136]{2,1,0:T(4,128)S(1)} collective-permute-done((f32[64,4,136]{2,1,0:T(4,128)S(1)}, f32[64,4,136]{2,1,0:T(4,128)S(1)}, u32[]{:S(2)}, u32[]{:S(2)}) %collective-permute-start.4) | collective-permute-done | bytes 139296 | tf_op jit(solution)/shard_map/ppermute | solution.py:26
  70.4 4.1 %collective-permute-done.5 = f32[64,4,136]{2,1,0:T(4,128)S(1)} collective-permute-done((f32[64,4,136]{2,1,0:T(4,128)S(1)}, f32[64,4,136]{2,1,0:T(4,128)S(1)}, u32[]{:S(2)}, u32[]{:S(2)}) %collective-permute-start.5) | collective-permute-done | bytes 139296 | tf_op jit(solution)/shard_map/ppermute | solution.py:26
  79.1 4.1 %convolution_multiply_fusion.5 = f32[426,64]{0,1:T(8,128)} fusion(f32[426,2048]{1,0:T(8,128)S(1)} %fusion.1, f32[8,8,16,128]{3,2,1,0:T(8,128)S(1)} %bitcast.240), kind=kOutput, calls=%fused_computation.47 | convolution fusion | flops 670067328 | bytes 4123136 | tf_op jit(solution)/shard_map/dot_general | solution.py:83
  88.8 5.5 %collective-permute-done.7 = f32[64,16,4]{2,1,0:T(8,128)} collective-permute-done((f32[64,16,4]{2,1,0:T(8,128)}, f32[64,16,4]{2,1,0:T(8,128)}, u32[]{:S(2)}, u32[]{:S(2)}) %collective-permute-start.7) | collective-permute-done | bytes 16416 | tf_op jit(solution)/shard_map/ppermute | solution.py:26
  95.5 10.6 %scatter-add.45 = f32[64,16,128]{2,1,0:T(8,128)S(1)} dynamic-update-slice(f32[64,16,128]{2,1,0:T(8,128)S(1)} %scatter-add.44, f32[64,16,4]{2,1,0:T(8,128)S(1)} %slice_add_fusion.4, s32[]{:T(128)} %constant.302.clone.1, s32[]{:T(128)} %constant.302.clone.1, s32[]{:T(128)} %constant.304.clone.1) | dynamic-update-slice | bytes 32772 | tf_op jit(solution)/shard_map/scatter-add | solution.py:114
  114.3 15.6 %psum.21 = f32[426,8]{0,1:T(8,128)S(1)} all-reduce(f32[426,8]{0,1:T(8,128)} %reduce-scatter.4.cloned.1.call-done), channel_id=1, replica_groups=mesh['rows'=4,'cols'=8] {'rows'}, use_global_device_ids=true, to_apply=%region_1.2 | all-reduce | flops 3408 | bytes 27264 | tf_op jit(solution)/shard_map/psum | solution.py:116
  130.9 6.8 %collective-permute-start.11 = (f32[64,24,4]{0,1,2:T(8,128)S(1)}, f32[64,24,4]{0,1,2:T(8,128)S(1)}, u32[]{:S(2)}, u32[]{:S(2)}) collective-permute-start(f32[64,24,4]{0,1,2:T(8,128)S(1)} %copy.15), channel_id=1, source_target_pairs={{1,0},{2,1},{3,2},{4,3},{5,4},{6,5},{7,6},{9,8},{10,9},{11,10},{12... | collective-permute-start | bytes 73736 | tf_op jit(solution)/shard_map/ppermute | solution.py:18
  140.8 8.9 %all_gather.9 = f32[426,64]{0,1:T(8,128)S(1)} all-gather(f32[426,8]{0,1:T(8,128)S(1)} %subtract_maximum_fusion.5), channel_id=1, replica_groups=mesh['rows'=4,'cols'=8] {'cols'}, dimensions={1}, use_global_device_ids=true | all-gather | bytes 122688 | tf_op jit(solution)/shard_map/all_gather | solution.py:121
  181.3 4.4 %collective-permute-done.12 = f32[64,4,136]{2,1,0:T(4,128)S(1)} collective-permute-done((f32[64,4,136]{2,1,0:T(4,128)S(1)}, f32[64,4,136]{2,1,0:T(4,128)S(1)}, u32[]{:S(2)}, u32[]{:S(2)}) %collective-permute-start.12) | collective-permute-done | bytes 139296 | tf_op jit(solution)/shard_map/ppermute | solution.py:26
  194.2 4.1 %convolution_multiply_fusion.4 = f32[426,64]{0,1:T(8,128)} fusion(f32[426,2048]{1,0:T(8,128)S(1)} %fusion.3, f32[8,8,16,128]{3,2,1,0:T(8,128)S(1)} %bitcast.242), kind=kOutput, calls=%fused_computation.46 | convolution fusion | flops 670067328 | bytes 4123136 | tf_op jit(solution)/shard_map/dot_general | solution.py:83
  203.9 5.5 %collective-permute-done.15 = f32[64,16,4]{2,1,0:T(8,128)} collective-permute-done((f32[64,16,4]{2,1,0:T(8,128)}, f32[64,16,4]{2,1,0:T(8,128)}, u32[]{:S(2)}, u32[]{:S(2)}) %collective-permute-start.15) | collective-permute-done | bytes 16416 | tf_op jit(solution)/shard_map/ppermute | solution.py:26
  210.7 10.6 %scatter-add.51 = f32[64,16,128]{2,1,0:T(8,128)S(1)} dynamic-update-slice(f32[64,16,128]{2,1,0:T(8,128)S(1)} %scatter-add.50, f32[64,16,4]{2,1,0:T(8,128)S(1)} %slice_add_fusion.2, s32[]{:T(128)} %constant.302.clone.1, s32[]{:T(128)} %constant.302.clone.1, s32[]{:T(128)} %constant.304.clone.1) | dynamic-update-slice | bytes 32772 | tf_op jit(solution)/shard_map/scatter-add | solution.py:114
  228.4 15.6 %psum.22 = f32[426,8]{0,1:T(8,128)S(1)} all-reduce(f32[426,8]{0,1:T(8,128)} %reduce-scatter.6.cloned.1.call-done), channel_id=1, replica_groups=mesh['rows'=4,'cols'=8] {'rows'}, use_global_device_ids=true, to_apply=%region_3.4 | all-reduce | flops 3408 | bytes 27264 | tf_op jit(solution)/shard_map/psum | solution.py:116
  245.1 6.8 %collective-permute-start.19 = (f32[64,24,4]{0,1,2:T(8,128)S(1)}, f32[64,24,4]{0,1,2:T(8,128)S(1)}, u32[]{:S(2)}, u32[]{:S(2)}) collective-permute-start(f32[64,24,4]{0,1,2:T(8,128)S(1)} %copy.19), channel_id=1, source_target_pairs={{1,0},{2,1},{3,2},{4,3},{5,4},{6,5},{7,6},{9,8},{10,9},{11,10},{12... | collective-permute-start | bytes 73736 | tf_op jit(solution)/shard_map/ppermute | solution.py:18
  254.9 8.9 %all_gather.10 = f32[426,64]{0,1:T(8,128)S(1)} all-gather(f32[426,8]{0,1:T(8,128)S(1)} %subtract_maximum_fusion.4), channel_id=1, replica_groups=mesh['rows'=4,'cols'=8] {'cols'}, dimensions={1}, use_global_device_ids=true | all-gather | bytes 122688 | tf_op jit(solution)/shard_map/all_gather | solution.py:121
  295.4 4.4 %collective-permute-done.20 = f32[64,4,136]{2,1,0:T(4,128)S(1)} collective-permute-done((f32[64,4,136]{2,1,0:T(4,128)S(1)}, f32[64,4,136]{2,1,0:T(4,128)S(1)}, u32[]{:S(2)}, u32[]{:S(2)}) %collective-permute-start.20) | collective-permute-done | bytes 139296 | tf_op jit(solution)/shard_map/ppermute | solution.py:26
  308.4 4.1 %convolution_multiply_fusion.3 = f32[426,64]{0,1:T(8,128)} fusion(f32[426,2048]{1,0:T(8,128)S(1)} %fusion.5, f32[8,8,16,128]{3,2,1,0:T(8,128)S(1)} %bitcast.238), kind=kOutput, calls=%fused_computation.45 | convolution fusion | flops 670067328 | bytes 4123136 | tf_op jit(solution)/shard_map/dot_general | solution.py:83
  316.9 6.6 %collective-permute-done.23 = f32[64,16,4]{2,1,0:T(8,128)} collective-permute-done((f32[64,16,4]{2,1,0:T(8,128)}, f32[64,16,4]{2,1,0:T(8,128)}, u32[]{:S(2)}, u32[]{:S(2)}) %collective-permute-start.23) | collective-permute-done | bytes 16416 | tf_op jit(solution)/shard_map/ppermute | solution.py:26
  324.8 10.6 %scatter-add.59 = f32[64,16,128]{2,1,0:T(8,128)S(1)} dynamic-update-slice(f32[64,16,128]{2,1,0:T(8,128)S(1)} %scatter-add.56, f32[64,16,4]{2,1,0:T(8,128)S(1)} %slice_add_fusion, s32[]{:T(128)} %constant.302.clone.1, s32[]{:T(128)} %constant.302.clone.1, s32[]{:T(128)} %constant.304.clone.1) | dynamic-update-slice | bytes 32772 | tf_op jit(solution)/shard_map/scatter-add | solution.py:114
  336.3 6.4 %reduce-scatter.8.cloned.1.call-done = f32[426,8]{0,1:T(8,128)} async-done(((f32[426,64]{0,1:T(8,128)}), f32[426,8]{0,1:T(8,128)}) %reduce-scatter.8.cloned.1.call-update) | async-done | bytes 13648 | tf_op jit(solution)/shard_map/reduce_scatter | solution.py:115
  342.6 15.6 %psum.23 = f32[426,8]{0,1:T(8,128)S(1)} all-reduce(f32[426,8]{0,1:T(8,128)} %reduce-scatter.8.cloned.1.call-done), channel_id=1, replica_groups=mesh['rows'=4,'cols'=8] {'rows'}, use_global_device_ids=true, to_apply=%region_5.6 | all-reduce | flops 3408 | bytes 27264 | tf_op jit(solution)/shard_map/psum | solution.py:116
  358.2 13.9 %all_gather.11 = f32[426,64]{0,1:T(8,128)S(1)} all-gather(f32[426,8]{0,1:T(8,128)S(1)} %subtract_maximum_fusion.3), channel_id=1, replica_groups=mesh['rows'=4,'cols'=8] {'cols'}, dimensions={1}, use_global_device_ids=true | all-gather | bytes 122688 | tf_op jit(solution)/shard_map/all_gather | solution.py:121
  (191 shorter events, 178.1 us)
Async XLA Ops:
  7.2 107.2 %reduce-scatter.4.cloned.1.call-start = ((), (), s32[]{:S(2)}) async-start(), calls=%async_computation.3 | async-start | bytes 147456 | tf_op jit(solution)/shard_map/reduce_scatter | solution.py:115
  8.3 8.2 %collective-permute-start = (f32[64,4,128]{2,1,0:T(4,128)S(1)}, f32[64,4,128]{2,1,0:T(4,128)S(1)}, u32[]{:S(2)}, u32[]{:S(2)}) collective-permute-start(f32[64,4,128]{2,1,0:T(4,128)S(1)} %get-tuple-element.177), channel_id=1, source_target_pairs={{0,8},{8,16},{16,24},{1,9},{9,17},{17,25},{2,10},{10,18},{18,26},{... | collective-permute-start | bytes 393224 | tf_op jit(solution)/shard_map/ppermute | solution.py:15
  19.1 13.2 %collective-permute-start.3 = (f32[64,24,4]{0,1,2:T(8,128)S(1)}, f32[64,24,4]{0,1,2:T(8,128)S(1)}, u32[]{:S(2)}, u32[]{:S(2)}) collective-permute-start(f32[64,24,4]{0,1,2:T(8,128)S(1)} %copy.10), channel_id=1, source_target_pairs={{1,0},{2,1},{3,2},{4,3},{5,4},{6,5},{7,6},{9,8},{10,9},{11,10},{12... | collective-permute-start | bytes 73736 | tf_op jit(solution)/shard_map/ppermute | solution.py:18
  23.2 8.8 %collective-permute-start.2 = (f32[64,24,4]{0,1,2:T(8,128)S(1)}, f32[64,24,4]{0,1,2:T(8,128)S(1)}, u32[]{:S(2)}, u32[]{:S(2)}) collective-permute-start(f32[64,24,4]{0,1,2:T(8,128)S(1)} %copy.9), channel_id=1, source_target_pairs={{0,1},{1,2},{2,3},{3,4},{4,5},{5,6},{6,7},{8,9},{9,10},{10,11},{11... | collective-permute-start | bytes 73736 | tf_op jit(solution)/shard_map/ppermute | solution.py:15
  61.0 9.2 %collective-permute-start.4 = (f32[64,4,136]{2,1,0:T(4,128)S(1)}, f32[64,4,136]{2,1,0:T(4,128)S(1)}, u32[]{:S(2)}, u32[]{:S(2)}) collective-permute-start(f32[64,4,136]{2,1,0:T(4,128)S(1)} %get-tuple-element.151), channel_id=1, source_target_pairs={{0,8},{8,16},{16,24},{1,9},{9,17},{17,25},{2,10},{10,18},{18,26},{... | collective-permute-start | bytes 417800 | tf_op jit(solution)/shard_map/ppermute | solution.py:26
  64.4 10.1 %collective-permute-start.5 = (f32[64,4,136]{2,1,0:T(4,128)S(1)}, f32[64,4,136]{2,1,0:T(4,128)S(1)}, u32[]{:S(2)}, u32[]{:S(2)}) collective-permute-start(f32[64,4,136]{2,1,0:T(4,128)S(1)} %get-tuple-element.150), channel_id=1, source_target_pairs={{8,0},{16,8},{24,16},{9,1},{17,9},{25,17},{10,2},{18,10},{26,18},{... | collective-permute-start | bytes 417800 | tf_op jit(solution)/shard_map/ppermute | solution.py:26
  75.6 9.9 %collective-permute-start.6 = (f32[64,16,4]{2,1,0:T(8,128)S(1)}, f32[64,16,4]{2,1,0:T(8,128)}, u32[]{:S(2)}, u32[]{:S(2)}) collective-permute-start(f32[64,16,4]{2,1,0:T(8,128)S(1)} %get-tuple-element.166), channel_id=1, source_target_pairs={{0,1},{1,2},{2,3},{3,4},{4,5},{5,6},{6,7},{8,9},{9,10},{10,11},{11... | collective-permute-start | bytes 49160 | tf_op jit(solution)/shard_map/ppermute | solution.py:26
  83.2 145.2 %reduce-scatter.6.cloned.1.call-start = ((), (), s32[]{:S(2)}) async-start(), calls=%async_computation.4 | async-start | bytes 147456 | tf_op jit(solution)/shard_map/reduce_scatter | solution.py:115
  83.5 10.8 %collective-permute-start.7 = (f32[64,16,4]{2,1,0:T(8,128)}, f32[64,16,4]{2,1,0:T(8,128)}, u32[]{:S(2)}, u32[]{:S(2)}) collective-permute-start(f32[64,16,4]{2,1,0:T(8,128)} %get-tuple-element.165), channel_id=1, source_target_pairs={{1,0},{2,1},{3,2},{4,3},{5,4},{6,5},{7,6},{9,8},{10,9},{11,10},{12... | collective-permute-start | bytes 49160 | tf_op jit(solution)/shard_map/ppermute | solution.py:26
  106.3 23.6 %collective-permute-start.8 = (f32[64,4,128]{2,1,0:T(4,128)S(1)}, f32[64,4,128]{2,1,0:T(4,128)S(1)}, u32[]{:S(2)}, u32[]{:S(2)}) collective-permute-start(f32[64,4,128]{2,1,0:T(4,128)S(1)} %get-tuple-element.175), channel_id=1, source_target_pairs={{0,8},{8,16},{16,24},{1,9},{9,17},{17,25},{2,10},{10,18},{18,26},{... | collective-permute-start | bytes 393224 | tf_op jit(solution)/shard_map/ppermute | solution.py:15
  109.5 20.4 %collective-permute-start.9 = (f32[64,4,128]{2,1,0:T(4,128)S(1)}, f32[64,4,128]{2,1,0:T(4,128)S(1)}, u32[]{:S(2)}, u32[]{:S(2)}) collective-permute-start(f32[64,4,128]{2,1,0:T(4,128)S(1)} %get-tuple-element.176), channel_id=1, source_target_pairs={{8,0},{16,8},{24,16},{9,1},{17,9},{25,17},{10,2},{18,10},{26,18},{... | collective-permute-start | bytes 393224 | tf_op jit(solution)/shard_map/ppermute | solution.py:18
  130.9 19.1 %collective-permute-start.11 = (f32[64,24,4]{0,1,2:T(8,128)S(1)}, f32[64,24,4]{0,1,2:T(8,128)S(1)}, u32[]{:S(2)}, u32[]{:S(2)}) collective-permute-start(f32[64,24,4]{0,1,2:T(8,128)S(1)} %copy.15), channel_id=1, source_target_pairs={{1,0},{2,1},{3,2},{4,3},{5,4},{6,5},{7,6},{9,8},{10,9},{11,10},{12... | collective-permute-start | bytes 73736 | tf_op jit(solution)/shard_map/ppermute | solution.py:18
  137.8 11.9 %collective-permute-start.10 = (f32[64,24,4]{0,1,2:T(8,128)S(1)}, f32[64,24,4]{0,1,2:T(8,128)S(1)}, u32[]{:S(2)}, u32[]{:S(2)}) collective-permute-start(f32[64,24,4]{0,1,2:T(8,128)S(1)} %copy.14), channel_id=1, source_target_pairs={{0,1},{1,2},{2,3},{3,4},{4,5},{5,6},{6,7},{8,9},{9,10},{10,11},{11... | collective-permute-start | bytes 73736 | tf_op jit(solution)/shard_map/ppermute | solution.py:15
  180.0 9.6 %collective-permute-start.13 = (f32[64,4,136]{2,1,0:T(4,128)S(1)}, f32[64,4,136]{2,1,0:T(4,128)S(1)}, u32[]{:S(2)}, u32[]{:S(2)}) collective-permute-start(f32[64,4,136]{2,1,0:T(4,128)S(1)} %get-tuple-element.148), channel_id=1, source_target_pairs={{8,0},{16,8},{24,16},{9,1},{17,9},{25,17},{10,2},{18,10},{26,18},{... | collective-permute-start | bytes 417800 | tf_op jit(solution)/shard_map/ppermute | solution.py:26
  190.7 9.8 %collective-permute-start.14 = (f32[64,16,4]{2,1,0:T(8,128)S(1)}, f32[64,16,4]{2,1,0:T(8,128)}, u32[]{:S(2)}, u32[]{:S(2)}) collective-permute-start(f32[64,16,4]{2,1,0:T(8,128)S(1)} %get-tuple-element.164), channel_id=1, source_target_pairs={{0,1},{1,2},{2,3},{3,4},{4,5},{5,6},{6,7},{8,9},{9,10},{10,11},{11... | collective-permute-start | bytes 49160 | tf_op jit(solution)/shard_map/ppermute | solution.py:26
  198.3 144.3 %reduce-scatter.8.cloned.1.call-start = ((), (), s32[]{:S(2)}) async-start(), calls=%async_computation.5 | async-start | bytes 147456 | tf_op jit(solution)/shard_map/reduce_scatter | solution.py:115
  198.6 10.8 %collective-permute-start.15 = (f32[64,16,4]{2,1,0:T(8,128)}, f32[64,16,4]{2,1,0:T(8,128)}, u32[]{:S(2)}, u32[]{:S(2)}) collective-permute-start(f32[64,16,4]{2,1,0:T(8,128)} %get-tuple-element.163), channel_id=1, source_target_pairs={{1,0},{2,1},{3,2},{4,3},{5,4},{6,5},{7,6},{9,8},{10,9},{11,10},{12... | collective-permute-start | bytes 49160 | tf_op jit(solution)/shard_map/ppermute | solution.py:26
  221.4 22.6 %collective-permute-start.16 = (f32[64,4,128]{2,1,0:T(4,128)S(1)}, f32[64,4,128]{2,1,0:T(4,128)S(1)}, u32[]{:S(2)}, u32[]{:S(2)}) collective-permute-start(f32[64,4,128]{2,1,0:T(4,128)S(1)} %get-tuple-element.173), channel_id=1, source_target_pairs={{0,8},{8,16},{16,24},{1,9},{9,17},{17,25},{2,10},{10,18},{18,26},{... | collective-permute-start | bytes 393224 | tf_op jit(solution)/shard_map/ppermute | solution.py:15
  223.6 20.5 %collective-permute-start.17 = (f32[64,4,128]{2,1,0:T(4,128)S(1)}, f32[64,4,128]{2,1,0:T(4,128)S(1)}, u32[]{:S(2)}, u32[]{:S(2)}) collective-permute-start(f32[64,4,128]{2,1,0:T(4,128)S(1)} %get-tuple-element.174), channel_id=1, source_target_pairs={{8,0},{16,8},{24,16},{9,1},{17,9},{25,17},{10,2},{18,10},{26,18},{... | collective-permute-start | bytes 393224 | tf_op jit(solution)/shard_map/ppermute | solution.py:18
  245.1 19.1 %collective-permute-start.19 = (f32[64,24,4]{0,1,2:T(8,128)S(1)}, f32[64,24,4]{0,1,2:T(8,128)S(1)}, u32[]{:S(2)}, u32[]{:S(2)}) collective-permute-start(f32[64,24,4]{0,1,2:T(8,128)S(1)} %copy.19), channel_id=1, source_target_pairs={{1,0},{2,1},{3,2},{4,3},{5,4},{6,5},{7,6},{9,8},{10,9},{11,10},{12... | collective-permute-start | bytes 73736 | tf_op jit(solution)/shard_map/ppermute | solution.py:18
  251.9 11.9 %collective-permute-start.18 = (f32[64,24,4]{0,1,2:T(8,128)S(1)}, f32[64,24,4]{0,1,2:T(8,128)S(1)}, u32[]{:S(2)}, u32[]{:S(2)}) collective-permute-start(f32[64,24,4]{0,1,2:T(8,128)S(1)} %copy.18), channel_id=1, source_target_pairs={{0,1},{1,2},{2,3},{3,4},{4,5},{5,6},{6,7},{8,9},{9,10},{10,11},{11... | collective-permute-start | bytes 73736 | tf_op jit(solution)/shard_map/ppermute | solution.py:15
  294.1 9.6 %collective-permute-start.21 = (f32[64,4,136]{2,1,0:T(4,128)S(1)}, f32[64,4,136]{2,1,0:T(4,128)S(1)}, u32[]{:S(2)}, u32[]{:S(2)}) collective-permute-start(f32[64,4,136]{2,1,0:T(4,128)S(1)} %get-tuple-element.146), channel_id=1, source_target_pairs={{8,0},{16,8},{24,16},{9,1},{17,9},{25,17},{10,2},{18,10},{26,18},{... | collective-permute-start | bytes 417800 | tf_op jit(solution)/shard_map/ppermute | solution.py:26
  304.8 9.8 %collective-permute-start.22 = (f32[64,16,4]{2,1,0:T(8,128)S(1)}, f32[64,16,4]{2,1,0:T(8,128)S(1)}, u32[]{:S(2)}, u32[]{:S(2)}) collective-permute-start(f32[64,16,4]{2,1,0:T(8,128)S(1)} %get-tuple-element.162), channel_id=1, source_target_pairs={{0,1},{1,2},{2,3},{3,4},{4,5},{5,6},{6,7},{8,9},{9,10},{10,11},{11... | collective-permute-start | bytes 49160 | tf_op jit(solution)/shard_map/ppermute | solution.py:26
  312.7 10.8 %collective-permute-start.23 = (f32[64,16,4]{2,1,0:T(8,128)}, f32[64,16,4]{2,1,0:T(8,128)}, u32[]{:S(2)}, u32[]{:S(2)}) collective-permute-start(f32[64,16,4]{2,1,0:T(8,128)} %get-tuple-element.161), channel_id=1, source_target_pairs={{1,0},{2,1},{3,2},{4,3},{5,4},{6,5},{7,6},{9,8},{10,9},{11,10},{12... | collective-permute-start | bytes 49160 | tf_op jit(solution)/shard_map/ppermute | solution.py:26
  (9 other events, 46.8 us)
Sparse Core Ops, SparseCore 0:
  83.4 30.9 reduce-scatter.3
  198.5 29.9 reduce-scatter.5
  312.6 29.9 reduce-scatter.7
where the time goes:
time: 384 us; the launch traced here: 380 us
  matrix products  86.2 us (22%)
  blocking collectives  78.4 us (20%)
  starting transfers between devices  66.2 us (17%)
  local copies, waits for them, and re-layouts  58.7 us (15%)
  waiting for transfers between devices  57.8 us (15%)
  other arithmetic  16.6 us (4%)
  between operations  15.7 us (4%)
    psum x3, blocking collectives, on_device(): share = lax.psum(share, 'rows')  46.8 us
    ppermute x12, waiting for transfers between devices, shifted(): return lax.ppermute(block, axis, route)  42.7 us
    scatter-add x3, local copies, waits for them, and re-layouts, on_device(): grad_abund = grad_abund.at[:, :, width - radius:].add(from_right)  31.9 us
    all_gather x3, blocking collectives, on_device(): new_spectra = lax.all_gather(updated, 'cols', axis=1, tiled=True)  31.7 us
    dot_general x27, matrix products, on_device(): lax.dot_general(grad_blur, forward_bands[row_shift], (((2,), (1,)), ((),...  27.3 us
    dot_general x27, matrix products, on_device(): jnp.dot(padded[:, row_shift:row_shift + height, :], forward_bands[row_shi...  26.8 us
    ppermute x12, starting transfers between devices, shifted(): return lax.ppermute(block, axis, route)  26 us
    ppermute x6, starting transfers between devices, padded_2(): lax.ppermute(lax.slice_in_dim(block, 0, width, axis=dim), axis, backward)  21.5 us
  transfers between devices with their start and end apart: 27, of which 13 were waited for; matrix products, arithmetic and copies ran while one was open for 18% of the time, Pallas kernels for 0%

commit v1 on v0

v1 whole, which is shorter than its diff:
```python
import functools

import jax
import jax.numpy as jnp
import numpy as np
from jax import lax
from jax.experimental import pallas as pl
from jax.experimental.pallas import tpu as pltpu
from jax.sharding import PartitionSpec as P

KS = 9
RADIUS = KS // 2
EDGE = 2 * RADIUS
ITERS = 3
F32 = jnp.float32
BF16 = jnp.bfloat16
VMEM = pl.BlockSpec(memory_space=pltpu.VMEM)
SMEM = pl.BlockSpec(memory_space=pltpu.SMEM)
PARAMS = pltpu.CompilerParams(vmem_limit_bytes=52 * 1024 * 1024)
ROW_ODD, COL_ODD, UP, DOWN, LEFT, RIGHT, HALF = range(7)


def split(x):
    high = x.astype(BF16)
    return high, (x - high.astype(F32)).astype(BF16)


def mm(a, b):
    return jnp.dot(a, b, preferred_element_type=F32)


def mm_nt(a, b):
    return lax.dot_general(a, b, (((1,), (1,)), ((), ())), preferred_element_type=F32)


def lanes(shape):
    return lax.broadcasted_iota(jnp.int32, shape, len(shape) - 1)


def edges(rows, swapped):
    count = len(rows)
    lane = lanes(rows[0].shape)
    width = rows[0].shape[1]
    out = jnp.zeros_like(rows[0])
    for i, row in enumerate(rows):
        place = (i + count // 2) % count if swapped else i
        first = 0 if swapped else width - EDGE
        moved = pltpu.roll(row, (place * EDGE - first) % width, 1)
        out = jnp.where(lane // EDGE == place, moved, out)
    return out


def wide(x, total, shift):
    padded = jnp.concatenate([x, jnp.zeros((x.shape[0], total - x.shape[1]), x.dtype)], axis=1)
    return pltpu.roll(padded, shift % total, 1)


def assemble_side(left, right, above, below, height):
    total = 2 * left.shape[1]
    lane = lanes((left.shape[0], total))
    row, col = lane // EDGE, lane % EDGE
    on_left = col < RADIUS
    own = (row >= RADIUS) & (row < RADIUS + height)
    top = row < RADIUS
    bottom = (row >= RADIUS + height) & (row < 2 * RADIUS + height)
    half = EDGE * height // 2
    lo = RADIUS * EDGE - RADIUS
    hi = RADIUS * EDGE + RADIUS
    base = (RADIUS + height) * EDGE
    out = jnp.zeros((left.shape[0], total), F32)
    out = jnp.where(own & on_left, wide(left, total, lo), out)
    first = (row - RADIUS) < height // 2
    out = jnp.where(own & ~on_left & first, wide(right, total, hi - half), out)
    out = jnp.where(own & ~on_left & ~first, wide(right, total, hi + half), out)
    out = jnp.where(top & ~on_left, wide(above, total, RADIUS - RADIUS * EDGE), out)
    out = jnp.where(top & on_left, wide(above, total, -half - RADIUS * EDGE - RADIUS), out)
    out = jnp.where(bottom & on_left, wide(below, total, base - RADIUS), out)
    out = jnp.where(bottom & ~on_left, wide(below, total, base + RADIUS - half), out)
    return out


def add_rim(row, contrib, index):
    width = row.shape[1]
    start = index * EDGE
    part = contrib[:, start // width * width : start // width * width + width]
    moved = pltpu.roll(part, (-(start % width) - RADIUS) % width, 1)
    lane = lanes(row.shape)
    near = (lane < RADIUS) | (lane >= width - RADIUS)
    return row + jnp.where(near, moved, 0.0)


def first_kernel(family, a_ref, place, rows_ref, e_core, e_cross):
    channels, height, width = a_ref.shape
    rows = []
    for i in range(height):
        row = a_ref[:, i, :]
        rows_ref[i] = row
        rows.append(row)
    low, high = edges(rows, True), edges(rows, False)
    odd = place[COL_ODD] == 1
    e_core[:channels] = jnp.where(odd, low, high)
    e_cross[:channels] = jnp.where(odd, high, low)
    mark = jnp.full((8, width), family[0, 0].astype(F32), F32)
    e_core[channels:] = mark
    e_cross[channels:] = mark


def band_sum(taps, delta):
    total = jnp.zeros(delta.shape, F32)
    for v in range(KS):
        total = jnp.where(delta == v, taps[v], total)
    return total


def build_main(taps, w_high, w_low, index, width):
    shape = (width, width)
    delta = lax.broadcasted_iota(jnp.int32, shape, 0) - lax.broadcasted_iota(jnp.int32, shape, 1) + RADIUS
    blank = jnp.zeros(shape, BF16)
    for u in range(-1, KS + 1):
        if 0 <= u < KS:
            high, low = split(band_sum([taps(u, v) for v in range(KS)], delta))
        else:
            high, low = blank, blank
        for r in range(2):
            for ro in range(2):
                if (u + ro - r) % 2 == 0:
                    d = (u + ro - r) // 2
                    if 0 <= d <= RADIUS:
                        at = index + (d, slice(r * width, r * width + width), slice(ro * width, ro * width + width))
                        w_high[at] = high
                        w_low[at] = low


def rim_column(lane, width):
    c = lane % EDGE
    return jnp.where(c < RADIUS, width - RADIUS + c, c - RADIUS)


def side_column(lane, width):
    c = lane % EDGE
    return jnp.where(c < RADIUS, c - RADIUS, width + c - RADIUS)


def forward_weights(k9, w_high, w_low, s_high, s_low, height, width):
    own = lambda u, v: k9[4, u * KS + v]
    build_main(own, w_high, w_low, (), width)
    n = height * EDGE
    shape = (EDGE, n)
    lane = lanes(shape)
    c = lax.broadcasted_iota(jnp.int32, shape, 0)
    delta = side_column(c, width) - rim_column(lane, width) + RADIUS
    out_row = lane // EDGE
    bands = [band_sum([own(u, v) for v in range(KS)], delta) for u in range(KS)]
    rows = s_high.shape[0] // EDGE
    for a in range(0, rows, 2):
        blocks = []
        for b in (a, a + 1):
            total = jnp.zeros(shape, F32)
            for u in range(KS):
                total = jnp.where(out_row == b - u, bands[u], total)
            blocks.append(total)
        high, low = split(jnp.concatenate(blocks, axis=0))
        s_high[a * EDGE : a * EDGE + 2 * EDGE] = high
        s_low[a * EDGE : a * EDGE + 2 * EDGE] = low


def adjoint_weights_kernel(k9, w_high, w_low, s_high, s_low, scratch, *, height, width):
    for b in range(3):
        build_main(lambda u, v, b=b: k9[3 * b + 1, (KS - 1 - u) * KS + KS - 1 - v], w_high, w_low, (b,), width)
    n = s_high.shape[1]
    half = n // 2
    shape = (EDGE, n)
    lane = lanes(shape)
    c = lax.broadcasted_iota(jnp.int32, shape, 0)
    to_side = lane < half
    column = jnp.where(to_side, side_column(lane, width), rim_column(lane, width))
    out_row = jnp.where(to_side, lane, lane - half) // EDGE
    out_row = jnp.where(out_row < height + EDGE, out_row, -KS - 1)
    sources = (c - EDGE, width + c, rim_column(c, width))
    chunk = height * EDGE
    mid = chunk // 2

    def place_of(kind, q):
        i = q - EDGE
        if kind == 2:
            return 4 * chunk + q * EDGE
        if 0 <= i < height:
            return i * EDGE if kind == 0 else chunk + (i + height // 2) % height * EDGE
        if i < 0:
            return 2 * chunk + (mid if kind == 0 else 0) + q * EDGE
        return 3 * chunk + (0 if kind == 0 else mid) + (i - height) * EDGE

    for kind in range(3):
        delta = sources[kind] - column + RADIUS
        if kind == 2:
            delta = jnp.where(to_side, delta, -1)
        for b in range(3):
            tile = 3 * b + (0, 2, 1)[kind]
            bands = [
                band_sum([k9[tile, (KS - 1 - u) * KS + KS - 1 - v] for v in range(KS)], delta) for u in range(KS)
            ]
            q_range = (range(0, EDGE), range(EDGE, EDGE + height), range(EDGE + height, 2 * EDGE + height))[b]
            for q in q_range:
                total = jnp.zeros(shape, F32)
                for u in range(KS):
                    if 0 <= q - u < height + EDGE:
                        total = jnp.where(out_row == q - u, bands[u], total)
                at = place_of(kind, q)
                scratch[at : at + EDGE] = total
    for start in range(0, scratch.shape[0], 64):
        high, low = split(scratch[start : start + 64])
        s_high[start : start + 64] = high
        s_low[start : start + 64] = low


def blur_into(b_ref, a2_high, a2_low, side, w_high, w_low, s_high, s_low, acc):
    pairs, channels, double = acc.shape
    width = double // 2
    for d in range(RADIUS + 1):
        high = a2_high[d : d + pairs].reshape(pairs * channels, double)
        low = a2_low[d : d + pairs].reshape(pairs * channels, double)
        part = mm(high, w_high[d]) + mm(low, w_high[d]) + mm(high, w_low[d])
        part = part.reshape(pairs, channels, double)
        if d == 0:
            acc[...] = part
        else:
            acc[...] += part
    side_high, side_low = split(side)
    rim = mm(side_high, s_high[...]) + mm(side_low, s_high[...]) + mm(side_high, s_low[...])
    for i in range(2 * pairs):
        row = acc[i // 2, :, i % 2 * width : i % 2 * width + width]
        b_ref[i] = add_rim(row, rim, i)


def start_kernel(
    rows_ref, p1, p2, left, right, above, below, k9, place,
    ext_ref, side_ref, b_ref, w_high, w_low, s_high, s_low,
    a2_high, a2_low, acc,
):
    height, channels, width = rows_ref.shape
    forward_weights(k9, w_high, w_low, s_high, s_low, height, width)
    odd = place[ROW_ODD] == 1
    for a in range(height + EDGE):
        if a < RADIUS:
            row = jnp.where(odd, p1[a * channels : a * channels + channels], p2[a * channels : a * channels + channels])
        elif a < RADIUS + height:
            row = rows_ref[a - RADIUS]
        else:
            k = (a - RADIUS - height) * channels
            row = jnp.where(odd, p2[k : k + channels], p1[k : k + channels])
        ext_ref[a] = row
        high, low = split(row)
        a2_high[a // 2, :, a % 2 * width : a % 2 * width + width] = high
        a2_low[a // 2, :, a % 2 * width : a % 2 * width + width] = low
    side = assemble_side(left[...], right[...], above[...], below[...], height)
    side_ref[...] = side
    blur_into(b_ref, a2_high, a2_low, side, w_high, w_low, s_high, s_low, acc)


def spectral_kernel(
    obs_ref, bend_ref, b_ref, mine, other, place,
    g_mine, core_ref, main1, main2, cross_ref, rows_ref,
    total, *, scale,
):
    height, channels, width = b_ref.shape
    bands = obs_ref.shape[1]
    quarter = bands // 4
    second = place[HALF] == 1
    m0 = jnp.where(second, other[...], mine[...])
    m1 = jnp.where(second, mine[...], other[...])
    spectra = jnp.concatenate([m0[:, :channels], m0[:, channels:], m1[:, :channels], m1[:, channels:]], axis=0)
    m_high, m_low = split(spectra)
    m_cat = jnp.concatenate([m_high, m_low, m_high], axis=1)
    t_high, t_low = split(spectra.T)
    t_cat = jnp.concatenate([t_high, t_low], axis=0)
    rows = []
    for pair in range(height // 2):
        b_pair = jnp.concatenate([b_ref[2 * pair], b_ref[2 * pair + 1]], axis=1)
        b_high, b_low = split(b_pair)
        b_cat = jnp.concatenate([b_high, b_high, b_low], axis=0)
        linear = mm(m_cat, b_cat) * scale
        seen = jnp.concatenate([obs_ref[2 * pair], obs_ref[2 * pair + 1]], axis=1)
        bend = jnp.concatenate([bend_ref[2 * pair : 2 * pair + 1], bend_ref[2 * pair + 1 : 2 * pair + 2]], axis=1)
        bent = bend * linear
        resid = linear + bent * linear - seen
        weighted = resid * (1.0 + 2.0 * bent)
        w_high, w_low = split(weighted)
        part = mm_nt(w_high, jnp.concatenate([b_high, b_low], axis=0))
        part = part[:, :channels] + part[:, channels:] + mm_nt(w_low, b_high)
        if pair == 0:
            total[...] = part
        else:
            total[...] += part
        both = mm(t_cat, w_high)
        grad = (both[:channels] + both[channels:] + mm(t_high, w_low)) * scale
        for k in range(2):
            row = grad[:, k * width : k * width + width]
            rows_ref[2 * pair + k] = row
            rows.append(row)
    low, high = edges(rows, True), edges(rows, False)
    col_odd = place[COL_ODD] == 1
    core_ref[2 * quarter // 2 :] = jnp.where(col_odd, low, high)
    cross_ref[...] = jnp.where(col_odd, high, low)
    row_odd = place[ROW_ODD] == 1
    half = height // 2
    for i in range(half):
        main1[i] = jnp.where(row_odd, rows[i], rows[half + i])
        main2[i] = jnp.where(row_odd, rows[half + i], rows[i])
    g = total[...] * scale
    g0 = jnp.concatenate([g[:quarter], g[quarter : 2 * quarter]], axis=1)
    g1 = jnp.concatenate([g[2 * quarter : 3 * quarter], g[3 * quarter :]], axis=1)
    g_mine[...] = jnp.where(second, g1, g0)
    core_ref[:quarter] = jnp.where(second, g0, g1)


def maps_kernel(
    ext_ref, side_ref, rows_ref, p1, p2, left, right, above, below, place,
    wa_high, wa_low, sa_high, sa_low, *rest, last,
):
    if last:
        out_ref, g2_high, g2_low, acc = rest
    else:
        (wf_high, wf_low, sf_high, sf_low, ext_out, side_out, b_ref, g2_high, g2_low, a2_high, a2_low, acc, acc_b) = rest
    height, channels, width = rows_ref.shape
    ext_rows = height + EDGE
    odd = place[ROW_ODD] == 1
    lane = lanes((channels, width))
    near = []
    for q in range(height + 2 * EDGE):
        if q < EDGE:
            row = jnp.where(odd, p1[q], p2[q])
        elif q < EDGE + height:
            row = rows_ref[q - EDGE]
        else:
            row = jnp.where(odd, p2[q - EDGE - height], p1[q - EDGE - height])
        high, low = split(row)
        g2_high[q // 2, :, q % 2 * width : q % 2 * width + width] = high
        g2_low[q // 2, :, q % 2 * width : q % 2 * width + width] = low
        if q % height == 0:
            near.append(jnp.zeros((channels, width), F32))
        moved = pltpu.roll(row, (RADIUS + q * EDGE) % width, 1)
        near[-1] = jnp.where(lane // EDGE == q % height, moved, near[-1])
    side_in = jnp.concatenate([left[...], right[...], above[...], below[...]] + near, axis=1)
    side_high, side_low = split(side_in)
    side_mm = mm(side_high, sa_high[...]) + mm(side_low, sa_high[...]) + mm(side_high, sa_low[...])
    half = side_mm.shape[1] // 2
    rim = side_mm[:, half:]
    n = EDGE // 2
    own = height // 2
    out_pairs = ext_rows // 2
    acc[...] = jnp.zeros_like(acc)
    for d in range(RADIUS + 1):
        for b in range(3):
            first, end = ((0, n), (n, n + own), (n + own, 2 * n + own))[b]
            first, end = max(first, d), min(end, out_pairs + d)
            if first >= end:
                continue
            high = g2_high[first:end].reshape((end - first) * channels, 2 * width)
            low = g2_low[first:end].reshape((end - first) * channels, 2 * width)
            part = mm(high, wa_high[b, d]) + mm(low, wa_high[b, d]) + mm(high, wa_low[b, d])
            acc[first - d : end - d] += part.reshape(end - first, channels, 2 * width)
    for a in range(ext_rows):
        if last and not RADIUS <= a < RADIUS + height:
            continue
        grad = add_rim(acc[a // 2, :, a % 2 * width : a % 2 * width + width], rim, a)
        row = jnp.maximum(ext_ref[a] - 0.5 * grad, 0.0)
        if last:
            out_ref[a - RADIUS] = row
            continue
        if a < RADIUS:
            row = jnp.where(place[UP] == 1, row, 0.0)
        elif a >= RADIUS + height:
            row = jnp.where(place[DOWN] == 1, row, 0.0)
        ext_out[a] = row
        high, low = split(row)
        a2_high[a // 2, :, a % 2 * width : a % 2 * width + width] = high
        a2_low[a // 2, :, a % 2 * width : a % 2 * width + width] = low
    if last:
        return
    side = jnp.maximum(side_ref[...] - 0.5 * side_mm[:, :half], 0.0)
    where = lanes(side.shape)
    a, c = where // EDGE, where % EDGE
    outside = (
        ((a < RADIUS) & (place[UP] == 0))
        | ((a >= RADIUS + height) & (place[DOWN] == 0))
        | ((c < RADIUS) & (place[LEFT] == 0))
        | ((c >= RADIUS) & (place[RIGHT] == 0))
        | (a >= ext_rows)
    )
    side = jnp.where(outside, 0.0, side)
    side_out[...] = side
    blur_into(b_ref, a2_high, a2_low, side, wf_high, wf_low, sf_high, sf_low, acc_b)


def call(kernel, outs, scratch, specs, *args):
    return pl.pallas_call(
        kernel,
        out_shape=[jax.ShapeDtypeStruct(s, d) for s, d in outs],
        in_specs=specs,
        out_specs=[VMEM] * len(outs),
        scratch_shapes=[pltpu.VMEM(s, d) for s, d in scratch],
        compiler_params=PARAMS,
    )(*args)


def core_swap(x):
    count = lax.axis_size("cols")
    return lax.ppermute(x, "cols", [(i, i ^ 1) for i in range(count)])


def cross_swap(x):
    count = lax.axis_size("cols")
    return lax.ppermute(x, "cols", [(i, (i + 1 if i % 2 else i - 1) % count) for i in range(count)])


def pair_one(x):
    count = lax.axis_size("rows")
    return lax.ppermute(x, "rows", [(i, i ^ 1) for i in range(count)])


def pair_two(x):
    count = lax.axis_size("rows")
    pairs = [(i, i + 1) for i in range(1, count - 1, 2)]
    return lax.ppermute(x, "rows", pairs + [(b, a) for a, b in pairs])


def chips_sum(x):
    count = lax.axis_size("cols")
    step = 4
    while step < count:
        route = [(i, (((i + 1) % count) ^ step) - 1) for i in range(count)]
        x = x + lax.ppermute(x, "cols", [(i, j % count) for i, j in route])
        step *= 2
    return x


def rows_sum(x):
    count = lax.axis_size("rows")
    step = 2
    while step < count:
        x = x + lax.ppermute(x, "rows", [(i, i ^ step) for i in range(count)])
        step *= 2
    return x


def on_device(observed, nonlin, abundance, spectra, kernels, tile_family):
    bands, height, width = observed.shape
    channels = abundance.shape[0]
    n_rows, n_cols = lax.axis_size("rows"), lax.axis_size("cols")
    row_at, col_at = lax.axis_index("rows"), lax.axis_index("cols")
    pixel_count = height * width * n_rows * n_cols
    quarter = -(-bands // 32) * 8
    full = 4 * quarter
    half_of = ((col_at + 1) // 2) % 2
    col_odd, row_odd = col_at % 2 == 1, row_at % 2 == 1
    place = jnp.stack(
        [row_at % 2, col_at % 2, row_at > 0, row_at < n_rows - 1, col_at > 0, col_at < n_cols - 1, half_of]
    ).astype(jnp.int32)
    has_left = (col_at > 0).astype(F32)
    has_right = (col_at < n_cols - 1).astype(F32)
    tile = (channels, width)

    def sides(core, cross):
        left = jnp.where(col_odd, core, cross) * has_left
        right = jnp.where(col_odd, cross, core) * has_right
        lane = lanes(tile) < width // 2
        up_msg = jnp.where(lane, left, right)
        down_msg = jnp.where(lane, right, left)
        return left, right, jnp.where(row_odd, up_msg, down_msg), jnp.where(row_odd, down_msg, up_msg)

    a_rows, e_core, e_cross = call(
        first_kernel,
        [((height,) + tile, F32), ((channels + 8, width), F32), ((channels + 8, width), F32)],
        [],
        [SMEM, VMEM, SMEM],
        tile_family, abundance, place,
    )
    got_core = core_swap(e_core)
    got_cross = cross_swap(e_cross)
    left, right, side1, side2 = sides(got_core[:channels], got_cross[:channels])
    fam_left = jnp.where(col_odd, got_core[channels, 0], got_cross[channels, 0])
    fam_right = jnp.where(col_odd, got_cross[channels, 0], got_core[channels, 0])
    fam_row = jnp.stack([fam_left, tile_family[0, 0].astype(F32), fam_right])
    marks = jnp.broadcast_to(jnp.concatenate([fam_row, jnp.zeros(5, F32)])[:, None], (8, width))
    top = a_rows[:RADIUS].reshape(RADIUS * channels, width)
    bottom = a_rows[height - RADIUS :].reshape(RADIUS * channels, width)
    got1 = pair_one(jnp.concatenate([jnp.where(row_odd, top, bottom), side1, marks]))
    got2 = pair_two(jnp.concatenate([jnp.where(row_odd, bottom, top), side2, marks]))
    body = RADIUS * channels

    def above_below(x1, x2):
        return jnp.where(row_odd, x1, x2), jnp.where(row_odd, x2, x1)

    above, below = above_below(got1[body : body + channels], got2[body : body + channels])
    fam_up, fam_down = above_below(got1[body + channels :, 0][:3], got2[body + channels :, 0][:3])
    families = jnp.concatenate([fam_up, fam_row, fam_down])
    choice = jnp.arange(kernels.shape[0], dtype=F32)[None, :, None] == families[:, None, None]
    k9 = jnp.sum(jnp.where(choice, kernels.reshape(1, kernels.shape[0], KS * KS), 0.0), axis=1)

    pairs = height // 2
    ext_rows = height + EDGE
    main_w = ((RADIUS + 1, 2 * width, 2 * width), BF16)
    side_f = ((2 * width, height * EDGE), BF16)
    ext, side, blurred, wf_high, wf_low, sf_high, sf_low = call(
        start_kernel,
        [((ext_rows,) + tile, F32), ((channels, 2 * width), F32), ((height,) + tile, F32), main_w, main_w, side_f, side_f],
        [((ext_rows // 2, channels, 2 * width), BF16)] * 2 + [((pairs, channels, 2 * width), F32)],
        [VMEM] * 7 + [SMEM, SMEM],
        a_rows, got1, got2, left, right, above, below, k9, place,
    )
    main_a = ((3, RADIUS + 1, 2 * width, 2 * width), BF16)
    side_a = ((6 * width, 4 * width), BF16)
    wa = call(
        functools.partial(adjoint_weights_kernel, height=height, width=width),
        [main_a, main_a, side_a, side_a],
        [((6 * width, 4 * width), F32)],
        [SMEM],
        k9,
    )

    seen = jnp.pad(jnp.transpose(observed, (1, 0, 2)), ((0, 0), (0, full - bands), (0, 0)))
    padded = jnp.pad(spectra, ((0, full - bands), (0, 0))).reshape(2, 2, quarter, channels)
    halves = jnp.transpose(padded, (0, 2, 1, 3)).reshape(2, quarter, 2 * channels)
    mine = lax.dynamic_index_in_dim(halves, half_of, 0, False)
    other = lax.dynamic_index_in_dim(halves, 1 - half_of, 0, False)
    rate = 40.0 / pixel_count
    for step in range(ITERS):
        last = step == ITERS - 1
        g_mine, to_core, main1, main2, e_cross, g_rows = call(
            functools.partial(spectral_kernel, scale=1.0 / channels),
            [
                ((quarter, 2 * channels), F32),
                ((quarter + channels, width), F32),
                ((height // 2,) + tile, F32),
                ((height // 2,) + tile, F32),
                (tile, F32),
                ((height,) + tile, F32),
            ],
            [((full, channels), F32)],
            [VMEM] * 5 + [SMEM],
            seen, nonlin, blurred, mine, other, place,
        )
        got_core = core_swap(to_core)
        p1 = pair_one(main1)
        p2 = pair_two(main2)
        share = g_mine + got_core[:quarter]
        got_cross = cross_swap(jnp.concatenate([share, e_cross]))
        share = share + got_cross[:quarter]
        left, right, side1, side2 = sides(got_core[quarter:], got_cross[quarter:])
        share = chips_sum(share)
        got1 = pair_one(jnp.concatenate([share, side1]))
        got2 = pair_two(side2)
        share = rows_sum(share + got1[:quarter])
        above, below = above_below(got1[quarter:], got2)
        mine = jnp.maximum(mine - rate * share, 0.0)
        other = core_swap(mine)
        gathered = (ext, side, g_rows, p1, p2, left, right, above, below, place) + tuple(wa)
        g2 = [((ext_rows // 2 + RADIUS, channels, 2 * width), BF16)] * 2
        acc = [((ext_rows // 2, channels, 2 * width), F32)]
        if last:
            (out,) = call(
                functools.partial(maps_kernel, last=True),
                [((height,) + tile, F32)],
                g2 + acc,
                [VMEM] * 9 + [SMEM] + [VMEM] * 4,
                *gathered,
            )
        else:
            ext, side, blurred = call(
                functools.partial(maps_kernel, last=False),
                [((ext_rows,) + tile, F32), ((channels, 2 * width), F32), ((height,) + tile, F32)],
                g2 + [((ext_rows // 2, channels, 2 * width), BF16)] * 2 + acc + [((pairs, channels, 2 * width), F32)],
                [VMEM] * 9 + [SMEM] + [VMEM] * 8,
                *gathered, wf_high, wf_low, sf_high, sf_low,
            )
    first = jnp.where(half_of == 0, mine, other)
    second = jnp.where(half_of == 0, other, mine)
    parts = [first[:, :channels], first[:, channels:], second[:, :channels], second[:, channels:]]
    return jnp.transpose(out, (1, 0, 2)), jnp.concatenate(parts)[:bands]


def solution(mesh):
    placed = (
        P(None, "rows", "cols"),
        P("rows", "cols"),
        P(None, "rows", "cols"),
        P(),
        P(),
        P("rows", "cols"),
    )
    return jax.shard_map(
        on_device,
        mesh=mesh,
        in_specs=placed,
        out_specs=(P(None, "rows", "cols"), P()),
        check_vma=False,
    )
```

time: 384 us -> 152 us (0.40)
  matrix products: 86.2 us -> 0 us
  blocking collectives: 78.4 us -> 0 us
  Pallas kernels: 0 us -> 48.7 us
  local copies, waits for them, and re-layouts: 58.7 us -> 13.5 us
  waiting for transfers between devices: 57.8 us -> 37.3 us
  starting transfers between devices: 66.2 us -> 46.1 us
  other arithmetic: 16.6 us -> 0.9 us
  between operations: 15.7 us -> 4.35 us
    dot_general x65 -> x0, matrix products: 86.2 us -> none  [the longest x27 27.3 us: on_device(): lax.dot_general(grad_blur, forward_bands[row_shift], (((2,), (1,)), ((),...]
    pallas_call x0 -> x9, Pallas kernels: none -> 48.7 us  [call(): pl.pallas_call(kernel, out_shape=[jax.ShapeDtypeStruct(s, d) for s, d in...]
    psum x3 -> x0, blocking collectives: 46.8 us -> none  [on_device(): share = lax.psum(share, 'rows')]
    scatter-add x6 -> x0, local copies, waits for them, and re-layouts: 38.1 us -> none  [the longest x3 31.9 us: on_device(): grad_abund = grad_abund.at[:, :, width - radius:].add(from_right)]
    all_gather x3 -> x0, blocking collectives: 31.7 us -> none  [on_device(): new_spectra = lax.all_gather(updated, 'cols', axis=1, tiled=True)]
    ppermute x24 -> x31, starting transfers between devices: 66.1 us -> 46.1 us  [the longest x7 13.9 us: core_swap(): return lax.ppermute(x, 'cols', [(i, i ^ 1) for i in range(count)])]
    reduce_scatter x3 -> x0, waiting for transfers between devices: 13.4 us -> none  [on_device(): lax.psum_scatter(grad_local, 'cols', scatter_dimension=1, tiled=True)]
    add x9 -> x12, other arithmetic: 11.4 us -> 0.11 us  [the longest x3 0.03 us: on_device(): share = rows_sum(share + got1[:quarter])]
  transfers between devices with their start and end apart: 27 -> 31, of which waited for: 13 -> 15; matrix products, arithmetic and copies ran while one was open for 18% -> 6% of each run, Pallas kernels for 0% -> 19%
where the time goes in v1:
time: 152 us; the launch traced here: 151 us
  Pallas kernels  48.7 us (32%)
  starting transfers between devices  46.1 us (30%)
  waiting for transfers between devices  37.3 us (25%)
  local copies, waits for them, and re-layouts  13.5 us (9%)
  between operations  4.35 us (3%)
    pallas_call x9, Pallas kernels, call(): pl.pallas_call(kernel, out_shape=[jax.ShapeDtypeStruct(s, d) for s, d in...  48.7 us
    ppermute x3, waiting for transfers between devices, rows_sum(): x = x + lax.ppermute(x, 'rows', [(i, i ^ step) for i in range(count)])  15.3 us
    ppermute x7, starting transfers between devices, core_swap(): return lax.ppermute(x, 'cols', [(i, i ^ 1) for i in range(count)])  13.9 us
    ppermute x4, waiting for transfers between devices, cross_swap(): lax.ppermute(x, 'cols', [(i, (i + 1 if i % 2 else i - 1) % count) for i i...  10.8 us
    ppermute x7, starting transfers between devices, pair_one(): return lax.ppermute(x, 'rows', [(i, i ^ 1) for i in range(count)])  9.39 us
    unnamed x12, local copies, waits for them, and re-layouts  8.66 us
    ppermute x4, starting transfers between devices, cross_swap(): lax.ppermute(x, 'cols', [(i, (i + 1 if i % 2 else i - 1) % count) for i i...  8.3 us
    ppermute x3, starting transfers between devices, rows_sum(): x = x + lax.ppermute(x, 'rows', [(i, i ^ step) for i in range(count)])  5.41 us
  transfers between devices with their start and end apart: 31, of which 15 were waited for; matrix products, arithmetic and copies ran while one was open for 6% of the time, Pallas kernels for 19%

profile of v1, /device:TPU:1, one launch (start us, length us, event | category | flops | bytes accessed | tf_op | source)
XLA Modules:
  0.0 151.0 jit_solution(975401561356254987)
XLA Ops:
  3.6 2.6 %collective-permute-start.1 = (f32[72,128]{1,0:T(8,128)S(1)}, f32[72,128]{1,0:T(8,128)S(1)}, u32[]{:S(2)}, u32[]{:S(2)}) collective-permute-start(f32[72,128]{1,0:T(8,128)S(1)} %get-tuple-element.42), channel_id=1, source_target_pairs={{0,7},{1,2},{2,1},{3,4},{4,3},{5,6},{6,5},{7,0},{8,15},{9,10},{10,... | collective-permute-start | bytes 110600 | tf_op jit(solution)/shard_map/ppermute | solution.py:413
  11.9 4.8 %collective-permute-start.2 = (f32[328,128]{1,0:T(8,128)S(1)}, f32[328,128]{1,0:T(8,128)S(1)}, u32[]{:S(2)}, u32[]{:S(2)}) collective-permute-start(f32[328,128]{1,0:T(8,128)S(1)} %get-tuple-element.117), channel_id=1, source_target_pairs={{0,8},{8,0},{16,24},{24,16},{1,9},{9,1},{17,25},{25,17},{2,10},{10... | collective-permute-start | bytes 503816 | tf_op jit(solution)/shard_map/ppermute | solution.py:418
  18.9 3.1 %copy.27 = f32[426,16,128]{2,0,1:T(8,128)S(1)} copy(f32[426,16,128]{2,1,0:T(8,128)} %param.6) | data formatting | bytes 6979584 | tf_op args[0]
  22.0 2.2 %pad.8.obs_ref = f32[16,448,128]{2,1,0:T(8,128)} pad(f32[16,426,128]{2,1,0:T(8,128)S(1)} %bitcast.29, f32[]{:T(128)} %constant.64.clone.1), padding=0_0x0_22x0_0 | pad | bytes 7159812 | tf_op jit(solution)/shard_map/jit(_pad)/pad | solution.py:521
  24.7 3.7 %shard_map.78 = (f32[24,64,128]{2,1,0:T(8,128)}, f32[64,256]{1,0:T(8,128)S(1)}, f32[16,64,128]{2,1,0:T(8,128)S(1)}, bf16[5,256,256]{2,1,0:T(8,128)(2,1)}, bf16[5...) custom-call(f32[16,64,128]{2,1,0:T(8,128)S(1)} %get-tuple-element.40.rows_ref, ...), custom_call_target="tpu_custom_call" | custom-call | tf_op jit(solution)/shard_map/pallas_call | solution.py:396
  28.3 5.0 %shard_map.79 = (f32[112,128]{1,0:T(8,128)S(1)}, f32[176,128]{1,0:T(8,128)S(1)}, f32[8,64,128]{2,1,0:T(8,128)S(1)}, f32[8,64,128]{2,1,0:T(8,128)S(1)}, f32[64,12...) custom-call(f32[16,448,128]{2,1,0:T(8,128)} %pad.8.obs_ref, f32[16,128]{1,0:T(8,128)S(1)} %copy-done.3, ...), custom_call_target="tpu_custom_call" | custom-call | tf_op jit(solution)/shard_map/pallas_call | solution.py:396
  36.6 3.6 %collective-permute-done.7 = f32[176,128]{1,0:T(8,128)S(1)} collective-permute-done((f32[176,128]{1,0:T(8,128)S(1)}, f32[176,128]{1,0:T(8,128)S(1)}, u32[]{:S(2)}, u32[]{:S(2)}) %collective-permute-start.7) | collective-permute-done | bytes 90144 | tf_op jit(solution)/shard_map/ppermute | solution.py:413
  43.4 5.0 %shard_map.80 = (bf16[3,5,256,256]{3,2,1,0:T(8,128)(2,1)}, bf16[3,5,256,256]{3,2,1,0:T(8,128)(2,1)}, bf16[768,512]{1,0:T(8,128)(2,1)S(1)}, bf16[768,512]{1,0:T(8,128)(2,1)S(1)}) custom-call(f32[9,81]{1,0:T(8,128)S(1)} %select_reduce_fusion.k9), custom_call_target="tpu_custom_call" | custom-call | tf_op jit(solution)/shard_map/pallas_call | solution.py:396
  52.4 2.5 %collective-permute-start.11 = (f32[112,128]{1,0:T(8,128)S(1)}, f32[112,128]{1,0:T(8,128)S(1)}, u32[]{:S(2)}, u32[]{:S(2)}) collective-permute-start(f32[112,128]{1,0:T(8,128)S(1)} %slice_add_fusion.6), channel_id=1, source_target_pairs={{0,16},{8,24},{16,0},{24,8},{1,17},{9,25},{17,1},{25,9},{2,18},{10... | collective-permute-start | bytes 172040 | tf_op jit(solution)/shard_map/ppermute | solution.py:441
  55.8 5.5 %collective-permute-done.11 = f32[112,128]{1,0:T(8,128)S(1)} collective-permute-done((f32[112,128]{1,0:T(8,128)S(1)}, f32[112,128]{1,0:T(8,128)S(1)}, u32[]{:S(2)}, u32[]{:S(2)}) %collective-permute-start.11) | collective-permute-done | bytes 57376 | tf_op jit(solution)/shard_map/ppermute | solution.py:441
  61.3 3.7 %collective-permute-start.12 = (f32[112,128]{1,0:T(8,128)S(1)}, f32[112,128]{1,0:T(8,128)S(1)}, u32[]{:S(2)}, u32[]{:S(2)}) collective-permute-start(f32[112,128]{1,0:T(8,128)S(1)} %subtract_maximum_fusion.2.mine), channel_id=1, source_target_pairs={{0,1},{1,0},{2,3},{3,2},{4,5},{5,4},{6,7},{7,6},{8,9},{9,8},{10,11... | collective-permute-start | bytes 172040 | tf_op jit(solution)/shard_map/ppermute | solution.py:408
  65.0 9.5 %shard_map.81 = (f32[24,64,128]{2,1,0:T(8,128)}, f32[64,256]{1,0:T(8,128)S(1)}, f32[16,64,128]{2,1,0:T(8,128)S(1)}) custom-call(f32[24,64,128]{2,1,0:T(8,128)} %get-tuple-element.43.ext_ref, f32[64,256]{1,0:T(8,128)S(1)} %get-tuple-element.44.side_ref, f32[16,64,128]{2,1,0:T(8,128)S(1)} %get-tuple-element.46.rows_ref, ...), custom_call_target="tpu_custom_call" | custom-call | tf_op jit(solution)/shard_map/pallas_call | solution.py:396
  74.5 5.0 %shard_map.82 = (f32[112,128]{1,0:T(8,128)S(1)}, f32[176,128]{1,0:T(8,128)S(1)}, f32[8,64,128]{2,1,0:T(8,128)S(1)}, f32[8,64,128]{2,1,0:T(8,128)S(1)}, f32[64,12...) custom-call(f32[16,448,128]{2,1,0:T(8,128)} %pad.8.obs_ref, f32[16,128]{1,0:T(8,128)S(1)} %copy-done.3, ...), custom_call_target="tpu_custom_call" | custom-call | tf_op jit(solution)/shard_map/pallas_call | solution.py:396
  82.7 2.9 %collective-permute-done.16 = f32[176,128]{1,0:T(8,128)S(1)} collective-permute-done((f32[176,128]{1,0:T(8,128)S(1)}, f32[176,128]{1,0:T(8,128)S(1)}, u32[]{:S(2)}, u32[]{:S(2)}) %collective-permute-start.16) | collective-permute-done | bytes 90144 | tf_op jit(solution)/shard_map/ppermute | solution.py:413
  94.7 4.7 %collective-permute-done.20 = f32[112,128]{1,0:T(8,128)S(1)} collective-permute-done((f32[112,128]{1,0:T(8,128)S(1)}, f32[112,128]{1,0:T(8,128)S(1)}, u32[]{:S(2)}, u32[]{:S(2)}) %collective-permute-start.20) | collective-permute-done | bytes 57376 | tf_op jit(solution)/shard_map/ppermute | solution.py:441
  99.4 4.4 %collective-permute-start.21 = (f32[112,128]{1,0:T(8,128)S(1)}, f32[112,128]{1,0:T(8,128)S(1)}, u32[]{:S(2)}, u32[]{:S(2)}) collective-permute-start(f32[112,128]{1,0:T(8,128)S(1)} %subtract_maximum_fusion.1.mine), channel_id=1, source_target_pairs={{0,1},{1,0},{2,3},{3,2},{4,5},{5,4},{6,7},{7,6},{8,9},{9,8},{10,11... | collective-permute-start | bytes 172040 | tf_op jit(solution)/shard_map/ppermute | solution.py:408
  103.8 9.5 %shard_map.83 = (f32[24,64,128]{2,1,0:T(8,128)}, f32[64,256]{1,0:T(8,128)S(1)}, f32[16,64,128]{2,1,0:T(8,128)S(1)}) custom-call(f32[24,64,128]{2,1,0:T(8,128)} %get-tuple-element.60.ext_ref, f32[64,256]{1,0:T(8,128)S(1)} %get-tuple-element.61.side_ref, f32[16,64,128]{2,1,0:T(8,128)S(1)} %get-tuple-element.63.rows_ref, ...), custom_call_target="tpu_custom_call" | custom-call | tf_op jit(solution)/shard_map/pallas_call | solution.py:396
  113.4 5.0 %shard_map.84 = (f32[112,128]{1,0:T(8,128)S(1)}, f32[176,128]{1,0:T(8,128)S(1)}, f32[8,64,128]{2,1,0:T(8,128)S(1)}, f32[8,64,128]{2,1,0:T(8,128)S(1)}, f32[64,12...) custom-call(f32[16,448,128]{2,1,0:T(8,128)} %pad.8.obs_ref, f32[16,128]{1,0:T(8,128)S(1)} %copy-done.3, ...), custom_call_target="tpu_custom_call" | custom-call | tf_op jit(solution)/shard_map/pallas_call | solution.py:396
  119.8 2.9 %collective-permute-start.25 = (f32[176,128]{1,0:T(8,128)S(1)}, f32[176,128]{1,0:T(8,128)S(1)}, u32[]{:S(2)}, u32[]{:S(2)}) collective-permute-start(f32[176,128]{1,0:T(8,128)S(1)} %pad_maximum_fusion.7), channel_id=1, source_target_pairs={{0,7},{1,2},{2,1},{3,4},{4,3},{5,6},{6,5},{7,0},{8,15},{9,10},{10,... | collective-permute-start | bytes 270344 | tf_op jit(solution)/shard_map/ppermute | solution.py:413
  122.6 3.1 %collective-permute-done.25 = f32[176,128]{1,0:T(8,128)S(1)} collective-permute-done((f32[176,128]{1,0:T(8,128)S(1)}, f32[176,128]{1,0:T(8,128)S(1)}, u32[]{:S(2)}, u32[]{:S(2)}) %collective-permute-start.25) | collective-permute-done | bytes 90144 | tf_op jit(solution)/shard_map/ppermute | solution.py:413
  126.7 2.2 %collective-permute-done.26 = f32[112,128]{1,0:T(8,128)S(1)} collective-permute-done((f32[112,128]{1,0:T(8,128)S(1)}, f32[112,128]{1,0:T(8,128)S(1)}, u32[]{:S(2)}, u32[]{:S(2)}) %collective-permute-start.26) | collective-permute-done | bytes 57376 | tf_op jit(solution)/shard_map/ppermute | solution.py:432
  134.5 5.1 %collective-permute-done.29 = f32[112,128]{1,0:T(8,128)S(1)} collective-permute-done((f32[112,128]{1,0:T(8,128)S(1)}, f32[112,128]{1,0:T(8,128)S(1)}, u32[]{:S(2)}, u32[]{:S(2)}) %collective-permute-start.29) | collective-permute-done | bytes 57376 | tf_op jit(solution)/shard_map/ppermute | solution.py:441
  139.6 4.3 %collective-permute-start.30 = (f32[112,128]{1,0:T(8,128)S(1)}, f32[112,128]{1,0:T(8,128)S(1)}, u32[]{:S(2)}, u32[]{:S(2)}) collective-permute-start(f32[112,128]{1,0:T(8,128)S(1)} %subtract_maximum_fusion), channel_id=1, source_target_pairs={{0,1},{1,0},{2,3},{3,2},{4,5},{5,4},{6,7},{7,6},{8,9},{9,8},{10,11... | collective-permute-start | bytes 172040 | tf_op jit(solution)/shard_map/ppermute | solution.py:408
  143.9 5.0 %shard_map.85 = f32[16,64,128]{2,1,0:T(8,128)S(1)} custom-call(f32[24,64,128]{2,1,0:T(8,128)} %get-tuple-element.69.ext_ref, f32[64,256]{1,0:T(8,128)S(1)} %get-tuple-element.70.side_ref, f32[16,64,128]{2,1,0:T(8,128)S(1)} %get-tuple-element.72.rows_ref, f32[8,64,128]{2,1,0:T(8,128)S(1)} %collective-permute-done.22.p1, ...), custom_call_target="tpu_custom_call" | custom-call | tf_op jit(solution)/shard_map/pallas_call | solution.py:396
  (115 shorter events, 41.2 us)
Async XLA Ops:
  3.6 4.3 %collective-permute-start.1 = (f32[72,128]{1,0:T(8,128)S(1)}, f32[72,128]{1,0:T(8,128)S(1)}, u32[]{:S(2)}, u32[]{:S(2)}) collective-permute-start(f32[72,128]{1,0:T(8,128)S(1)} %get-tuple-element.42), channel_id=1, source_target_pairs={{0,7},{1,2},{2,1},{3,4},{4,3},{5,6},{6,5},{7,0},{8,15},{9,10},{10,... | collective-permute-start | bytes 110600 | tf_op jit(solution)/shard_map/ppermute | solution.py:413
  11.2 13.0 %collective-permute-start.3 = (f32[328,128]{1,0:T(8,128)S(1)}, f32[328,128]{1,0:T(8,128)S(1)}, u32[]{:S(2)}, u32[]{:S(2)}) collective-permute-start(f32[328,128]{1,0:T(8,128)S(1)} %get-tuple-element.116), channel_id=1, source_target_pairs={{8,16},{16,8},{9,17},{17,9},{10,18},{18,10},{11,19},{19,11},{12,20... | collective-permute-start | bytes 503816 | tf_op jit(solution)/shard_map/ppermute | solution.py:424
  11.9 12.4 %collective-permute-start.2 = (f32[328,128]{1,0:T(8,128)S(1)}, f32[328,128]{1,0:T(8,128)S(1)}, u32[]{:S(2)}, u32[]{:S(2)}) collective-permute-start(f32[328,128]{1,0:T(8,128)S(1)} %get-tuple-element.117), channel_id=1, source_target_pairs={{0,8},{8,0},{16,24},{24,16},{1,9},{9,1},{17,25},{25,17},{2,10},{10... | collective-permute-start | bytes 503816 | tf_op jit(solution)/shard_map/ppermute | solution.py:418
  35.6 4.6 %collective-permute-start.7 = (f32[176,128]{1,0:T(8,128)S(1)}, f32[176,128]{1,0:T(8,128)S(1)}, u32[]{:S(2)}, u32[]{:S(2)}) collective-permute-start(f32[176,128]{1,0:T(8,128)S(1)} %pad_maximum_fusion.3), channel_id=1, source_target_pairs={{0,7},{1,2},{2,1},{3,4},{4,3},{5,6},{6,5},{7,0},{8,15},{9,10},{10,... | collective-permute-start | bytes 270344 | tf_op jit(solution)/shard_map/ppermute | solution.py:413
  43.4 9.0 %collective-permute-start.9 = (f32[176,128]{1,0:T(8,128)S(1)}, f32[176,128]{1,0:T(8,128)S(1)}, u32[]{:S(2)}, u32[]{:S(2)}) collective-permute-start(f32[176,128]{1,0:T(8,128)S(1)} %pad_maximum_fusion.4), channel_id=1, source_target_pairs={{0,8},{8,0},{16,24},{24,16},{1,9},{9,1},{17,25},{25,17},{2,10},{10... | collective-permute-start | bytes 270344 | tf_op jit(solution)/shard_map/ppermute | solution.py:418
  50.3 14.7 %collective-permute-start.4 = (f32[8,64,128]{2,1,0:T(8,128)S(1)}, f32[8,64,128]{2,1,0:T(8,128)S(1)}, u32[]{:S(2)}, u32[]{:S(2)}) collective-permute-start(f32[8,64,128]{2,1,0:T(8,128)S(1)} %get-tuple-element.47), channel_id=1, source_target_pairs={{0,8},{8,0},{16,24},{24,16},{1,9},{9,1},{17,25},{25,17},{2,10},{10... | collective-permute-start | bytes 786440 | tf_op jit(solution)/shard_map/ppermute | solution.py:418
  51.7 13.3 %collective-permute-start.5 = (f32[8,64,128]{2,1,0:T(8,128)S(1)}, f32[8,64,128]{2,1,0:T(8,128)S(1)}, u32[]{:S(2)}, u32[]{:S(2)}) collective-permute-start(f32[8,64,128]{2,1,0:T(8,128)S(1)} %get-tuple-element.48), channel_id=1, source_target_pairs={{8,16},{16,8},{9,17},{17,9},{10,18},{18,10},{11,19},{19,11},{12,20... | collective-permute-start | bytes 786440 | tf_op jit(solution)/shard_map/ppermute | solution.py:424
  52.4 8.8 %collective-permute-start.11 = (f32[112,128]{1,0:T(8,128)S(1)}, f32[112,128]{1,0:T(8,128)S(1)}, u32[]{:S(2)}, u32[]{:S(2)}) collective-permute-start(f32[112,128]{1,0:T(8,128)S(1)} %slice_add_fusion.6), channel_id=1, source_target_pairs={{0,16},{8,24},{16,0},{24,8},{1,17},{9,25},{17,1},{25,9},{2,18},{10... | collective-permute-start | bytes 172040 | tf_op jit(solution)/shard_map/ppermute | solution.py:441
  54.9 10.0 %collective-permute-start.10 = (f32[64,128]{1,0:T(8,128)S(1)}, f32[64,128]{1,0:T(8,128)S(1)}, u32[]{:S(2)}, u32[]{:S(2)}) collective-permute-start(f32[64,128]{1,0:T(8,128)S(1)} %broadcast_select_fusion.14), channel_id=1, source_target_pairs={{8,16},{16,8},{9,17},{17,9},{10,18},{18,10},{11,19},{19,11},{12,20... | collective-permute-start | bytes 98312 | tf_op jit(solution)/shard_map/ppermute | solution.py:424
  61.3 13.2 %collective-permute-start.12 = (f32[112,128]{1,0:T(8,128)S(1)}, f32[112,128]{1,0:T(8,128)S(1)}, u32[]{:S(2)}, u32[]{:S(2)}) collective-permute-start(f32[112,128]{1,0:T(8,128)S(1)} %subtract_maximum_fusion.2.mine), channel_id=1, source_target_pairs={{0,1},{1,0},{2,3},{3,2},{4,5},{5,4},{6,7},{7,6},{8,9},{9,8},{10,11... | collective-permute-start | bytes 172040 | tf_op jit(solution)/shard_map/ppermute | solution.py:408
  80.9 4.7 %collective-permute-start.16 = (f32[176,128]{1,0:T(8,128)S(1)}, f32[176,128]{1,0:T(8,128)S(1)}, u32[]{:S(2)}, u32[]{:S(2)}) collective-permute-start(f32[176,128]{1,0:T(8,128)S(1)} %pad_maximum_fusion.5), channel_id=1, source_target_pairs={{0,7},{1,2},{2,1},{3,4},{4,3},{5,6},{6,5},{7,0},{8,15},{9,10},{10,... | collective-permute-start | bytes 270344 | tf_op jit(solution)/shard_map/ppermute | solution.py:413
  88.9 3.4 %collective-permute-start.18 = (f32[176,128]{1,0:T(8,128)S(1)}, f32[176,128]{1,0:T(8,128)S(1)}, u32[]{:S(2)}, u32[]{:S(2)}) collective-permute-start(f32[176,128]{1,0:T(8,128)S(1)} %pad_maximum_fusion.6), channel_id=1, source_target_pairs={{0,8},{8,0},{16,24},{24,16},{1,9},{9,1},{17,25},{25,17},{2,10},{10... | collective-permute-start | bytes 270344 | tf_op jit(solution)/shard_map/ppermute | solution.py:418
  89.1 14.7 %collective-permute-start.13 = (f32[8,64,128]{2,1,0:T(8,128)S(1)}, f32[8,64,128]{2,1,0:T(8,128)S(1)}, u32[]{:S(2)}, u32[]{:S(2)}) collective-permute-start(f32[8,64,128]{2,1,0:T(8,128)S(1)} %get-tuple-element.64), channel_id=1, source_target_pairs={{0,8},{8,0},{16,24},{24,16},{1,9},{9,1},{17,25},{25,17},{2,10},{10... | collective-permute-start | bytes 786440 | tf_op jit(solution)/shard_map/ppermute | solution.py:418
  90.4 13.4 %collective-permute-start.14 = (f32[8,64,128]{2,1,0:T(8,128)S(1)}, f32[8,64,128]{2,1,0:T(8,128)S(1)}, u32[]{:S(2)}, u32[]{:S(2)}) collective-permute-start(f32[8,64,128]{2,1,0:T(8,128)S(1)} %get-tuple-element.65), channel_id=1, source_target_pairs={{8,16},{16,8},{9,17},{17,9},{10,18},{18,10},{11,19},{19,11},{12,20... | collective-permute-start | bytes 786440 | tf_op jit(solution)/shard_map/ppermute | solution.py:424
  92.3 7.0 %collective-permute-start.20 = (f32[112,128]{1,0:T(8,128)S(1)}, f32[112,128]{1,0:T(8,128)S(1)}, u32[]{:S(2)}, u32[]{:S(2)}) collective-permute-start(f32[112,128]{1,0:T(8,128)S(1)} %slice_add_fusion.3), channel_id=1, source_target_pairs={{0,16},{8,24},{16,0},{24,8},{1,17},{9,25},{17,1},{25,9},{2,18},{10... | collective-permute-start | bytes 172040 | tf_op jit(solution)/shard_map/ppermute | solution.py:441
  93.8 10.0 %collective-permute-start.19 = (f32[64,128]{1,0:T(8,128)S(1)}, f32[64,128]{1,0:T(8,128)S(1)}, u32[]{:S(2)}, u32[]{:S(2)}) collective-permute-start(f32[64,128]{1,0:T(8,128)S(1)} %broadcast_select_fusion.12), channel_id=1, source_target_pairs={{8,16},{16,8},{9,17},{17,9},{10,18},{18,10},{11,19},{19,11},{12,20... | collective-permute-start | bytes 98312 | tf_op jit(solution)/shard_map/ppermute | solution.py:424
  99.4 14.0 %collective-permute-start.21 = (f32[112,128]{1,0:T(8,128)S(1)}, f32[112,128]{1,0:T(8,128)S(1)}, u32[]{:S(2)}, u32[]{:S(2)}) collective-permute-start(f32[112,128]{1,0:T(8,128)S(1)} %subtract_maximum_fusion.1.mine), channel_id=1, source_target_pairs={{0,1},{1,0},{2,3},{3,2},{4,5},{5,4},{6,7},{7,6},{8,9},{9,8},{10,11... | collective-permute-start | bytes 172040 | tf_op jit(solution)/shard_map/ppermute | solution.py:408
  119.8 6.0 %collective-permute-start.25 = (f32[176,128]{1,0:T(8,128)S(1)}, f32[176,128]{1,0:T(8,128)S(1)}, u32[]{:S(2)}, u32[]{:S(2)}) collective-permute-start(f32[176,128]{1,0:T(8,128)S(1)} %pad_maximum_fusion.7), channel_id=1, source_target_pairs={{0,7},{1,2},{2,1},{3,4},{4,3},{5,6},{6,5},{7,0},{8,15},{9,10},{10,... | collective-permute-start | bytes 270344 | tf_op jit(solution)/shard_map/ppermute | solution.py:413
  128.9 3.4 %collective-permute-start.27 = (f32[176,128]{1,0:T(8,128)S(1)}, f32[176,128]{1,0:T(8,128)S(1)}, u32[]{:S(2)}, u32[]{:S(2)}) collective-permute-start(f32[176,128]{1,0:T(8,128)S(1)} %pad_maximum_fusion.8), channel_id=1, source_target_pairs={{0,8},{8,0},{16,24},{24,16},{1,9},{9,1},{17,25},{25,17},{2,10},{10... | collective-permute-start | bytes 270344 | tf_op jit(solution)/shard_map/ppermute | solution.py:418
  129.2 14.7 %collective-permute-start.22 = (f32[8,64,128]{2,1,0:T(8,128)S(1)}, f32[8,64,128]{2,1,0:T(8,128)S(1)}, u32[]{:S(2)}, u32[]{:S(2)}) collective-permute-start(f32[8,64,128]{2,1,0:T(8,128)S(1)} %get-tuple-element.73), channel_id=1, source_target_pairs={{0,8},{8,0},{16,24},{24,16},{1,9},{9,1},{17,25},{25,17},{2,10},{10... | collective-permute-start | bytes 786440 | tf_op jit(solution)/shard_map/ppermute | solution.py:418
  130.5 13.5 %collective-permute-start.23 = (f32[8,64,128]{2,1,0:T(8,128)S(1)}, f32[8,64,128]{2,1,0:T(8,128)S(1)}, u32[]{:S(2)}, u32[]{:S(2)}) collective-permute-start(f32[8,64,128]{2,1,0:T(8,128)S(1)} %get-tuple-element.74), channel_id=1, source_target_pairs={{8,16},{16,8},{9,17},{17,9},{10,18},{18,10},{11,19},{19,11},{12,20... | collective-permute-start | bytes 786440 | tf_op jit(solution)/shard_map/ppermute | solution.py:424
  132.4 7.2 %collective-permute-start.29 = (f32[112,128]{1,0:T(8,128)S(1)}, f32[112,128]{1,0:T(8,128)S(1)}, u32[]{:S(2)}, u32[]{:S(2)}) collective-permute-start(f32[112,128]{1,0:T(8,128)S(1)} %slice_add_fusion), channel_id=1, source_target_pairs={{0,16},{8,24},{16,0},{24,8},{1,17},{9,25},{17,1},{25,9},{2,18},{10... | collective-permute-start | bytes 172040 | tf_op jit(solution)/shard_map/ppermute | solution.py:441
  133.9 10.0 %collective-permute-start.28 = (f32[64,128]{1,0:T(8,128)S(1)}, f32[64,128]{1,0:T(8,128)S(1)}, u32[]{:S(2)}, u32[]{:S(2)}) collective-permute-start(f32[64,128]{1,0:T(8,128)S(1)} %broadcast_select_fusion.10), channel_id=1, source_target_pairs={{8,16},{16,8},{9,17},{17,9},{10,18},{18,10},{11,19},{19,11},{12,20... | collective-permute-start | bytes 98312 | tf_op jit(solution)/shard_map/ppermute | solution.py:424
  139.6 10.5 %collective-permute-start.30 = (f32[112,128]{1,0:T(8,128)S(1)}, f32[112,128]{1,0:T(8,128)S(1)}, u32[]{:S(2)}, u32[]{:S(2)}) collective-permute-start(f32[112,128]{1,0:T(8,128)S(1)} %subtract_maximum_fusion), channel_id=1, source_target_pairs={{0,1},{1,0},{2,3},{3,2},{4,5},{5,4},{6,7},{7,6},{8,9},{9,8},{10,11... | collective-permute-start | bytes 172040 | tf_op jit(solution)/shard_map/ppermute | solution.py:408
  (11 other events, 26.4 us)

commit v2 on v1

--- a/solution.py
+++ b/solution.py
@@ -16,7 +16,7 @@
 BF16 = jnp.bfloat16
 VMEM = pl.BlockSpec(memory_space=pltpu.VMEM)
 SMEM = pl.BlockSpec(memory_space=pltpu.SMEM)
-PARAMS = pltpu.CompilerParams(vmem_limit_bytes=52 * 1024 * 1024)
+PARAMS = pltpu.CompilerParams(vmem_limit_bytes=18 * 1024 * 1024)
 ROW_ODD, COL_ODD, UP, DOWN, LEFT, RIGHT, HALF = range(7)
 
 
@@ -89,7 +89,7 @@
     return row + jnp.where(near, moved, 0.0)
 
 
-def first_kernel(family, a_ref, place, rows_ref, e_core, e_cross):
+def first_kernel(family, a_ref, place, rows_ref, e_core, e_cross, mark_ref):
     channels, height, width = a_ref.shape
     rows = []
     for i in range(height):
@@ -103,6 +103,7 @@
     mark = jnp.full((8, width), family[0, 0].astype(F32), F32)
     e_core[channels:] = mark
     e_cross[channels:] = mark
+    mark_ref[...] = mark
 
 
 def band_sum(taps, delta):
@@ -141,8 +142,14 @@
     return jnp.where(c < RADIUS, c - RADIUS, width + c - RADIUS)
 
 
-def forward_weights(k9, w_high, w_low, s_high, s_low, height, width):
-    own = lambda u, v: k9[4, u * KS + v]
+def forward_weights_kernel(family, table, obs_ref, seen_ref, w_high, w_low, s_high, s_low, sems):
+    depth, height, width = obs_ref.shape
+    copies = []
+    for i in range(height):
+        copies.append(pltpu.make_async_copy(obs_ref.at[:, i, :], seen_ref.at[i, pl.ds(0, depth), :], sems.at[i]))
+        copies[-1].start()
+    start = depth // 8 * 8
+    own = lambda u, v: table[family[0, 0], u * KS + v]
     build_main(own, w_high, w_low, (), width)
     n = height * EDGE
     shape = (EDGE, n)
@@ -162,11 +169,16 @@
         high, low = split(jnp.concatenate(blocks, axis=0))
         s_high[a * EDGE : a * EDGE + 2 * EDGE] = high
         s_low[a * EDGE : a * EDGE + 2 * EDGE] = low
-
-
-def adjoint_weights_kernel(k9, w_high, w_low, s_high, s_low, scratch, *, height, width):
+    for i in range(height):
+        copies[i].wait()
+    sub = lax.broadcasted_iota(jnp.int32, (seen_ref.shape[1] - start, width), 0)
+    for i in range(height):
+        seen_ref[i, start:] = jnp.where(sub < depth - start, seen_ref[i, start:], 0.0)
+
+
+def adjoint_weights_kernel(families, table, w_high, w_low, s_high, s_low, scratch, *, height, width):
     for b in range(3):
-        build_main(lambda u, v, b=b: k9[3 * b + 1, (KS - 1 - u) * KS + KS - 1 - v], w_high, w_low, (b,), width)
+        build_main(lambda u, v, b=b: table[families[3 * b + 1], (KS - 1 - u) * KS + KS - 1 - v], w_high, w_low, (b,), width)
     n = s_high.shape[1]
     half = n // 2
     shape = (EDGE, n)
@@ -197,7 +209,7 @@
         for b in range(3):
             tile = 3 * b + (0, 2, 1)[kind]
             bands = [
-                band_sum([k9[tile, (KS - 1 - u) * KS + KS - 1 - v] for v in range(KS)], delta) for u in range(KS)
+                band_sum([table[families[tile], (KS - 1 - u) * KS + KS - 1 - v] for v in range(KS)], delta) for u in range(KS)
             ]
             q_range = (range(0, EDGE), range(EDGE, EDGE + height), range(EDGE + height, 2 * EDGE + height))[b]
             for q in q_range:
@@ -233,12 +245,10 @@
 
 
 def start_kernel(
-    rows_ref, p1, p2, left, right, above, below, k9, place,
-    ext_ref, side_ref, b_ref, w_high, w_low, s_high, s_low,
-    a2_high, a2_low, acc,
+    rows_ref, p1, p2, left, right, above, below, place, w_high, w_low, s_high, s_low,
+    ext_ref, side_ref, b_ref, a2_high, a2_low, acc,
 ):
     height, channels, width = rows_ref.shape
-    forward_weights(k9, w_high, w_low, s_high, s_low, height, width)
     odd = place[ROW_ODD] == 1
     for a in range(height + EDGE):
         if a < RADIUS:
@@ -313,68 +323,83 @@
     core_ref[:quarter] = jnp.where(second, g0, g1)
 
 
+def put_pair(high_ref, low_ref, index, row):
+    width = row.shape[1]
+    at = (index // 2, slice(None), slice(index % 2 * width, index % 2 * width + width))
+    high_ref[at], low_ref[at] = split(row)
+
+
+def adjoint_into(acc, g_high, g_low, first, w_high, w_low, band):
+    pairs, channels, double = g_high.shape
+    for d in range(RADIUS + 1):
+        begin, end = max(first, d), min(first + pairs, acc.shape[0] + d)
+        if begin >= end:
+            continue
+        high = g_high[begin - first : end - first].reshape((end - begin) * channels, double)
+        low = g_low[begin - first : end - first].reshape((end - begin) * channels, double)
+        part = mm(high, w_high[band, d]) + mm(low, w_high[band, d]) + mm(high, w_low[band, d])
+        acc[begin - d : end - d] += part.reshape(end - begin, channels, double)
+
+
+def own_maps_kernel(rows_ref, wa_high, wa_low, acc, near_ref, g_high, g_low):
+    height, channels, width = rows_ref.shape
+    lane = lanes((channels, width))
+    near = [jnp.zeros((channels, width), F32) for _ in range(2)]
+    for i in range(height):
+        row = rows_ref[i]
+        put_pair(g_high, g_low, i, row)
+        q = i + EDGE
+        moved = pltpu.roll(row, (RADIUS + q * EDGE) % width, 1)
+        near[q // height] = jnp.where(lane // EDGE == q % height, moved, near[q // height])
+    near_ref[...] = jnp.concatenate(near, axis=1)
+    acc[...] = jnp.zeros_like(acc)
+    adjoint_into(acc, g_high, g_low, EDGE // 2, wa_high, wa_low, 1)
+
+
 def maps_kernel(
-    ext_ref, side_ref, rows_ref, p1, p2, left, right, above, below, place,
+    ext_ref, side_ref, acc_in, near_ref, p1, p2, left, right, above, below, place,
     wa_high, wa_low, sa_high, sa_low, *rest, last,
 ):
     if last:
-        out_ref, g2_high, g2_low, acc = rest
+        out_ref, g_high, g_low, acc = rest
+        height = out_ref.shape[1]
     else:
-        (wf_high, wf_low, sf_high, sf_low, ext_out, side_out, b_ref, g2_high, g2_low, a2_high, a2_low, acc, acc_b) = rest
-    height, channels, width = rows_ref.shape
+        (wf_high, wf_low, sf_high, sf_low, ext_out, side_out, b_ref, g_high, g_low, acc, a2_high, a2_low, acc_b) = rest
+        height = b_ref.shape[0]
+    channels, width = left.shape
     ext_rows = height + EDGE
     odd = place[ROW_ODD] == 1
     lane = lanes((channels, width))
-    near = []
-    for q in range(height + 2 * EDGE):
-        if q < EDGE:
-            row = jnp.where(odd, p1[q], p2[q])
-        elif q < EDGE + height:
-            row = rows_ref[q - EDGE]
-        else:
-            row = jnp.where(odd, p2[q - EDGE - height], p1[q - EDGE - height])
-        high, low = split(row)
-        g2_high[q // 2, :, q % 2 * width : q % 2 * width + width] = high
-        g2_low[q // 2, :, q % 2 * width : q % 2 * width + width] = low
-        if q % height == 0:
-            near.append(jnp.zeros((channels, width), F32))
+    near = [near_ref[:, :width], near_ref[:, width:]]
+    for k in range(2 * EDGE):
+        q = k if k < EDGE else k + height
+        row = jnp.where(odd, p1[k], p2[k]) if k < EDGE else jnp.where(odd, p2[k - EDGE], p1[k - EDGE])
+        put_pair(g_high, g_low, k, row)
         moved = pltpu.roll(row, (RADIUS + q * EDGE) % width, 1)
-        near[-1] = jnp.where(lane // EDGE == q % height, moved, near[-1])
+        near[q // height] = jnp.where(lane // EDGE == q % height, moved, near[q // height])
     side_in = jnp.concatenate([left[...], right[...], above[...], below[...]] + near, axis=1)
     side_high, side_low = split(side_in)
     side_mm = mm(side_high, sa_high[...]) + mm(side_low, sa_high[...]) + mm(side_high, sa_low[...])
     half = side_mm.shape[1] // 2
     rim = side_mm[:, half:]
+    acc[...] = acc_in[...]
     n = EDGE // 2
-    own = height // 2
-    out_pairs = ext_rows // 2
-    acc[...] = jnp.zeros_like(acc)
-    for d in range(RADIUS + 1):
-        for b in range(3):
-            first, end = ((0, n), (n, n + own), (n + own, 2 * n + own))[b]
-            first, end = max(first, d), min(end, out_pairs + d)
-            if first >= end:
-                continue
-            high = g2_high[first:end].reshape((end - first) * channels, 2 * width)
-            low = g2_low[first:end].reshape((end - first) * channels, 2 * width)
-            part = mm(high, wa_high[b, d]) + mm(low, wa_high[b, d]) + mm(high, wa_low[b, d])
-            acc[first - d : end - d] += part.reshape(end - first, channels, 2 * width)
+    adjoint_into(acc, g_high.at[:n], g_low.at[:n], 0, wa_high, wa_low, 0)
+    adjoint_into(acc, g_high.at[n:], g_low.at[n:], n + height // 2, wa_high, wa_low, 2)
     for a in range(ext_rows):
         if last and not RADIUS <= a < RADIUS + height:
             continue
         grad = add_rim(acc[a // 2, :, a % 2 * width : a % 2 * width + width], rim, a)
         row = jnp.maximum(ext_ref[a] - 0.5 * grad, 0.0)
         if last:
-            out_ref[a - RADIUS] = row
+            out_ref[:, a - RADIUS, :] = row
             continue
         if a < RADIUS:
             row = jnp.where(place[UP] == 1, row, 0.0)
         elif a >= RADIUS + height:
             row = jnp.where(place[DOWN] == 1, row, 0.0)
         ext_out[a] = row
-        high, low = split(row)
-        a2_high[a // 2, :, a % 2 * width : a % 2 * width + width] = high
-        a2_low[a // 2, :, a % 2 * width : a % 2 * width + width] = low
+        put_pair(a2_high, a2_low, a, row)
     if last:
         return
     side = jnp.maximum(side_ref[...] - 0.5 * side_mm[:, :half], 0.0)
@@ -392,14 +417,17 @@
     blur_into(b_ref, a2_high, a2_low, side, wf_high, wf_low, sf_high, sf_low, acc_b)
 
 
-def call(kernel, outs, scratch, specs, *args):
+def call(kernel, micros, outs, scratch, specs, *args):
     return pl.pallas_call(
         kernel,
         out_shape=[jax.ShapeDtypeStruct(s, d) for s, d in outs],
         in_specs=specs,
         out_specs=[VMEM] * len(outs),
-        scratch_shapes=[pltpu.VMEM(s, d) for s, d in scratch],
+        scratch_shapes=[pltpu.VMEM(*s) if isinstance(s, tuple) else s for s in scratch],
         compiler_params=PARAMS,
+        cost_estimate=pl.CostEstimate(
+            flops=int(micros * 1.15e9), bytes_accessed=int(micros * 3.7e6), transcendentals=0
+        ),
     )(*args)
 
 
@@ -468,9 +496,10 @@
         down_msg = jnp.where(lane, right, left)
         return left, right, jnp.where(row_odd, up_msg, down_msg), jnp.where(row_odd, down_msg, up_msg)
 
-    a_rows, e_core, e_cross = call(
+    a_rows, e_core, e_cross, mark = call(
         first_kernel,
-        [((height,) + tile, F32), ((channels + 8, width), F32), ((channels + 8, width), F32)],
+        1,
+        [((height,) + tile, F32), ((channels + 8, width), F32), ((channels + 8, width), F32), ((8, width), F32)],
         [],
         [SMEM, VMEM, SMEM],
         tile_family, abundance, place,
@@ -478,10 +507,9 @@
     got_core = core_swap(e_core)
     got_cross = cross_swap(e_cross)
     left, right, side1, side2 = sides(got_core[:channels], got_cross[:channels])
-    fam_left = jnp.where(col_odd, got_core[channels, 0], got_cross[channels, 0])
-    fam_right = jnp.where(col_odd, got_cross[channels, 0], got_core[channels, 0])
-    fam_row = jnp.stack([fam_left, tile_family[0, 0].astype(F32), fam_right])
-    marks = jnp.broadcast_to(jnp.concatenate([fam_row, jnp.zeros(5, F32)])[:, None], (8, width))
+    mark_left = jnp.where(col_odd, got_core[channels:], got_cross[channels:])
+    mark_right = jnp.where(col_odd, got_cross[channels:], got_core[channels:])
+    marks = jnp.concatenate([mark_left, mark, mark_right])
     top = a_rows[:RADIUS].reshape(RADIUS * channels, width)
     bottom = a_rows[height - RADIUS :].reshape(RADIUS * channels, width)
     got1 = pair_one(jnp.concatenate([jnp.where(row_odd, top, bottom), side1, marks]))
@@ -492,33 +520,44 @@
         return jnp.where(row_odd, x1, x2), jnp.where(row_odd, x2, x1)
 
     above, below = above_below(got1[body : body + channels], got2[body : body + channels])
-    fam_up, fam_down = above_below(got1[body + channels :, 0][:3], got2[body + channels :, 0][:3])
-    families = jnp.concatenate([fam_up, fam_row, fam_down])
-    choice = jnp.arange(kernels.shape[0], dtype=F32)[None, :, None] == families[:, None, None]
-    k9 = jnp.sum(jnp.where(choice, kernels.reshape(1, kernels.shape[0], KS * KS), 0.0), axis=1)
-
+    table = kernels.reshape(kernels.shape[0], KS * KS)
     pairs = height // 2
     ext_rows = height + EDGE
     main_w = ((RADIUS + 1, 2 * width, 2 * width), BF16)
     side_f = ((2 * width, height * EDGE), BF16)
-    ext, side, blurred, wf_high, wf_low, sf_high, sf_low = call(
+    any_space = pl.BlockSpec(memory_space=pl.ANY)
+    seen, *wf = call(
+        forward_weights_kernel,
+        3,
+        [((height, full, width), F32), main_w, main_w, side_f, side_f],
+        [pltpu.SemaphoreType.DMA((height,))],
+        [SMEM, SMEM, any_space],
+        tile_family, table, observed,
+    )
+    got1, got2, seen, *wf = lax.optimization_barrier((got1, got2, seen, *wf))
+    ext, side, blurred = call(
         start_kernel,
-        [((ext_rows,) + tile, F32), ((channels, 2 * width), F32), ((height,) + tile, F32), main_w, main_w, side_f, side_f],
+        2,
+        [((ext_rows,) + tile, F32), ((channels, 2 * width), F32), ((height,) + tile, F32)],
         [((ext_rows // 2, channels, 2 * width), BF16)] * 2 + [((pairs, channels, 2 * width), F32)],
-        [VMEM] * 7 + [SMEM, SMEM],
-        a_rows, got1, got2, left, right, above, below, k9, place,
+        [VMEM] * 7 + [SMEM] + [VMEM] * 4,
+        a_rows, got1, got2, left, right, above, below, place, *wf,
     )
+    marks_up, marks_down = above_below(got1[body + channels :], got2[body + channels :])
+    families = jnp.concatenate([marks_up, marks, marks_down])[::8, 0].astype(jnp.int32)
     main_a = ((3, RADIUS + 1, 2 * width, 2 * width), BF16)
     side_a = ((6 * width, 4 * width), BF16)
-    wa = call(
-        functools.partial(adjoint_weights_kernel, height=height, width=width),
-        [main_a, main_a, side_a, side_a],
-        [((6 * width, 4 * width), F32)],
-        [SMEM],
-        k9,
-    )
-
-    seen = jnp.pad(jnp.transpose(observed, (1, 0, 2)), ((0, 0), (0, full - bands), (0, 0)))
+
+    def adjoint_weights():
+        return call(
+            functools.partial(adjoint_weights_kernel, height=height, width=width),
+            3,
+            [main_a, main_a, side_a, side_a],
+            [((6 * width, 4 * width), F32)],
+            [SMEM, SMEM],
+            families, table,
+        )
+
     padded = jnp.pad(spectra, ((0, full - bands), (0, 0))).reshape(2, 2, quarter, channels)
     halves = jnp.transpose(padded, (0, 2, 1, 3)).reshape(2, quarter, 2 * channels)
     mine = lax.dynamic_index_in_dim(halves, half_of, 0, False)
@@ -528,6 +567,7 @@
         last = step == ITERS - 1
         g_mine, to_core, main1, main2, e_cross, g_rows = call(
             functools.partial(spectral_kernel, scale=1.0 / channels),
+            5,
             [
                 ((quarter, 2 * channels), F32),
                 ((quarter + channels, width), F32),
@@ -545,38 +585,57 @@
         p2 = pair_two(main2)
         share = g_mine + got_core[:quarter]
         got_cross = cross_swap(jnp.concatenate([share, e_cross]))
+        if step == 0:
+            wa = adjoint_weights()
+            got_cross, *wa = lax.optimization_barrier((got_cross, *wa))
         share = share + got_cross[:quarter]
         left, right, side1, side2 = sides(got_core[quarter:], got_cross[quarter:])
+        own, near = call(
+            own_maps_kernel,
+            2,
+            [((ext_rows // 2, channels, 2 * width), F32), ((channels, 2 * width), F32)],
+            [((pairs, channels, 2 * width), BF16)] * 2,
+            [VMEM] * 3,
+            g_rows, wa[0], wa[1],
+        )
         share = chips_sum(share)
+        share, own, near, p1, p2 = lax.optimization_barrier((share, own, near, p1, p2))
         got1 = pair_one(jnp.concatenate([share, side1]))
         got2 = pair_two(side2)
-        share = rows_sum(share + got1[:quarter])
+        share = share + got1[:quarter]
         above, below = above_below(got1[quarter:], got2)
-        mine = jnp.maximum(mine - rate * share, 0.0)
-        other = core_swap(mine)
-        gathered = (ext, side, g_rows, p1, p2, left, right, above, below, place) + tuple(wa)
-        g2 = [((ext_rows // 2 + RADIUS, channels, 2 * width), BF16)] * 2
+        gathered = (ext, side, own, near, p1, p2, left, right, above, below, place) + tuple(wa)
+        g2 = [((EDGE, channels, 2 * width), BF16)] * 2
         acc = [((ext_rows // 2, channels, 2 * width), F32)]
         if last:
-            (out,) = call(
+            made = call(
                 functools.partial(maps_kernel, last=True),
-                [((height,) + tile, F32)],
+                3,
+                [((channels, height, width), F32)],
                 g2 + acc,
-                [VMEM] * 9 + [SMEM] + [VMEM] * 4,
+                [VMEM] * 10 + [SMEM] + [VMEM] * 4,
                 *gathered,
             )
         else:
-            ext, side, blurred = call(
+            made = call(
                 functools.partial(maps_kernel, last=False),
+                4,
                 [((ext_rows,) + tile, F32), ((channels, 2 * width), F32), ((height,) + tile, F32)],
-                g2 + [((ext_rows // 2, channels, 2 * width), BF16)] * 2 + acc + [((pairs, channels, 2 * width), F32)],
-                [VMEM] * 9 + [SMEM] + [VMEM] * 8,
-                *gathered, wf_high, wf_low, sf_high, sf_low,
+                g2 + acc + [((ext_rows // 2, channels, 2 * width), BF16)] * 2 + [((pairs, channels, 2 * width), F32)],
+                [VMEM] * 10 + [SMEM] + [VMEM] * 8,
+                *gathered, *wf,
             )
+        share, *made = lax.optimization_barrier((rows_sum(share), *made))
+        mine = jnp.maximum(mine - rate * share, 0.0)
+        other = core_swap(mine)
+        if last:
+            (out,) = made
+        else:
+            ext, side, blurred = made
     first = jnp.where(half_of == 0, mine, other)
     second = jnp.where(half_of == 0, other, mine)
     parts = [first[:, :channels], first[:, channels:], second[:, :channels], second[:, channels:]]
-    return jnp.transpose(out, (1, 0, 2)), jnp.concatenate(parts)[:bands]
+    return out, jnp.concatenate(parts)[:bands]
 
 
 def solution(mesh):

time: 152 us -> 110 us (0.72)
  waiting for transfers between devices: 37.3 us -> 18.8 us
  Pallas kernels: 48.7 us -> 33.1 us
  local copies, waits for them, and re-layouts: 13.5 us -> 6.35 us
  starting transfers between devices: 46.1 us -> 49 us
  between operations: 4.35 us -> 2.04 us
    pallas_call x9 -> x13, Pallas kernels: 48.7 us -> 33.1 us  [call(): pl.pallas_call(kernel, out_shape=[jax.ShapeDtypeStruct(s, d) for s, d in...]
    ppermute x3, waiting for transfers between devices: 15.3 us -> 0.01 us  [rows_sum(): x = x + lax.ppermute(x, 'rows', [(i, i ^ step) for i in range(count)])]
    ppermute x7, starting transfers between devices: 9.39 us -> 14 us  [pair_one(): return lax.ppermute(x, 'rows', [(i, i ^ 1) for i in range(count)])]
    ppermute x4, starting transfers between devices: 8.3 us -> 4.43 us  [cross_swap(): lax.ppermute(x, 'cols', [(i, (i + 1 if i % 2 else i - 1) % count) for i i...]
    unnamed x12 -> x23, local copies, waits for them, and re-layouts: 8.66 us -> 5.67 us
    ppermute x4, waiting for transfers between devices: 10.8 us -> 8.13 us  [cross_swap(): lax.ppermute(x, 'cols', [(i, (i + 1 if i % 2 else i - 1) % count) for i i...]
    pad x1 -> x0, local copies, waits for them, and re-layouts: 2.2 us -> none  [on_device(): jnp.pad(jnp.transpose(observed, (1, 0, 2)), ((0, 0), (0, full - bands), (...]
  transfers between devices with their start and end apart: 31 -> 31, of which waited for: 15 -> 14; matrix products, arithmetic and copies ran while one was open for 6% -> 1% of each run, Pallas kernels for 19% -> 18%
where the time goes in v2:
time: 110 us
  starting transfers between devices  49 us (45%)
  Pallas kernels  33.1 us (30%)
  waiting for transfers between devices  18.8 us (17%)
  local copies, waits for them, and re-layouts  6.35 us (6%)
  between operations  2.04 us (2%)
    pallas_call x13, Pallas kernels, call(): pl.pallas_call(kernel, out_shape=[jax.ShapeDtypeStruct(s, d) for s, d in...  33.1 us
    ppermute x7, starting transfers between devices, core_swap(): return lax.ppermute(x, 'cols', [(i, i ^ 1) for i in range(count)])  14.9 us
    ppermute x7, starting transfers between devices, pair_one(): return lax.ppermute(x, 'rows', [(i, i ^ 1) for i in range(count)])  14 us
    ppermute x4, waiting for transfers between devices, cross_swap(): lax.ppermute(x, 'cols', [(i, (i + 1 if i % 2 else i - 1) % count) for i i...  8.13 us
    ppermute x3, starting transfers between devices, rows_sum(): x = x + lax.ppermute(x, 'rows', [(i, i ^ step) for i in range(count)])  6.9 us
    unnamed x23, local copies, waits for them, and re-layouts  5.67 us
    ppermute x7, starting transfers between devices, pair_two(): return lax.ppermute(x, 'rows', pairs + [(b, a) for a, b in pairs])  5.01 us
    ppermute x4, starting transfers between devices, cross_swap(): lax.ppermute(x, 'cols', [(i, (i + 1 if i % 2 else i - 1) % count) for i i...  4.43 us
  transfers between devices with their start and end apart: 31, of which 14 were waited for; matrix products, arithmetic and copies ran while one was open for 1% of the time, Pallas kernels for 18%

profile of v2, /device:TPU:1, one launch (start us, length us, event | category | flops | bytes accessed | tf_op | source)
XLA Modules:
  0.0 109.8 jit_solution(4256348823992186383)
XLA Ops:
  3.6 2.6 %collective-permute-start.1 = (f32[72,128]{1,0:T(8,128)S(1)}, f32[72,128]{1,0:T(8,128)S(1)}, u32[]{:S(2)}, u32[]{:S(2)}) collective-permute-start(f32[72,128]{1,0:T(8,128)S(1)} %get-tuple-element.87), channel_id=1, source_target_pairs={{0,7},{1,2},{2,1},{3,4},{4,3},{5,6},{6,5},{7,0},{8,15},{9,10},{10,... | collective-permute-start | bytes 110600 | tf_op jit(solution)/shard_map/ppermute | solution.py:441
  8.0 2.3 %collective-permute-start.2 = (f32[344,128]{1,0:T(8,128)S(1)}, f32[344,128]{1,0:T(8,128)S(1)}, u32[]{:S(2)}, u32[]{:S(2)}) collective-permute-start(f32[344,128]{1,0:T(8,128)S(1)} %constant_dynamic-update-slice_fusion), channel_id=1, source_target_pairs={{0,8},{8,0},{16,24},{24,16},{1,9},{9,1},{17,25},{25,17},{2,10},{10... | collective-permute-start | bytes 528392 | tf_op jit(solution)/shard_map/ppermute | solution.py:446
  10.9 2.0 %copy-done = f32[426,16,128]{2,1,0:T(8,128)S(1)} copy-done((f32[426,16,128]{2,1,0:T(8,128)S(1)}, f32[426,16,128]{2,1,0:T(8,128)}, u32[]{:S(2)}) %copy-start) | copy-done | bytes 3489816
  12.9 3.8 %shard_map.78 = (f32[16,448,128]{2,1,0:T(8,128)S(1)}, bf16[5,256,256]{2,1,0:T(8,128)(2,1)S(1)}, bf16[5,256,256]{2,1,0:T(8,128)(2,1)S(1)}, bf16[256,128]{1,0:T(8,128)(2,1)S(1)}, bf16[256,128]{1,0:T(8,128)(2,1)S(1)}) custom-call(s32[1,1]{1,0:T(1,128)S(6)} %copy.28.family, f32[8,81]{1,0:T(8,128)S(1)} %reshape.20.table, f32[426,16,128]{2,1,0:T(8,128)S(1)} %copy-done), custom_call_target="tpu_custom_call" | custom-call | flops 3449999872 | bytes 11100000 | tf_op jit(solution)/shard_map/pallas_call | solution.py:421
  18.6 2.0 %shard_map.79 = (f32[24,64,128]{2,1,0:T(8,128)S(1)}, f32[64,256]{1,0:T(8,128)S(1)}, f32[16,64,128]{2,1,0:T(8,128)S(1)}) custom-call(f32[16,64,128]{2,1,0:T(8,128)S(1)} %get-tuple-element.85.rows_ref, f32[344,128]{1,0:T(8,128)S(1)} %collective-permute-done.2.p1, f32[344,128]{1,0:T(8,128)S(1)} %collective-permute-done.3.p2, ...), custom_call_target="tpu_custom_call" | custom-call | flops 2300000000 | bytes 7400000 | tf_op jit(solution)/shard_map/pallas_call | solution.py:421
  20.6 3.5 %shard_map.80 = (f32[112,128]{1,0:T(8,128)S(1)}, f32[176,128]{1,0:T(8,128)S(1)}, f32[8,64,128]{2,1,0:T(8,128)S(1)}, f32[8,64,128]{2,1,0:T(8,128)S(1)}, f32[64,12...) custom-call(f32[16,448,128]{2,1,0:T(8,128)S(1)} %copy-done.4, f32[16,128]{1,0:T(8,128)S(1)} %copy-done.2, ...), custom_call_target="tpu_custom_call" | custom-call | flops 5750000128 | bytes 18500000 | tf_op jit(solution)/shard_map/pallas_call | solution.py:421
  25.1 4.1 %collective-permute-start.7 = (f32[8,64,128]{2,1,0:T(8,128)S(1)}, f32[8,64,128]{2,1,0:T(8,128)S(1)}, u32[]{:S(2)}, u32[]{:S(2)}) collective-permute-start(f32[8,64,128]{2,1,0:T(8,128)S(1)} %get-tuple-element.115), channel_id=1, source_target_pairs={{0,8},{8,0},{16,24},{24,16},{1,9},{9,1},{17,25},{25,17},{2,10},{10... | collective-permute-start | bytes 786440 | tf_op jit(solution)/shard_map/ppermute | solution.py:446
  31.5 3.2 %shard_map.81 = (bf16[3,5,256,256]{3,2,1,0:T(8,128)(2,1)S(1)}, bf16[3,5,256,256]{3,2,1,0:T(8,128)(2,1)S(1)}, bf16[768,512]{1,0:T(8,128)(2,1)S(1)}, bf16[768,512]{1,0:T(8,128)(2,1)S(1)}) custom-call(s32[9]{0:T(128)S(1)} %convert_reduce_fusion.families, f32[8,81]{1,0:T(8,128)S(1)} %reshape.20.table), custom_call_target="tpu_custom_call" | custom-call | flops 3449999872 | bytes 11100000 | tf_op jit(solution)/shard_map/pallas_call | solution.py:421
  41.6 2.4 %collective-permute-start.10 = (f32[112,128]{1,0:T(8,128)S(1)}, f32[112,128]{1,0:T(8,128)S(1)}, u32[]{:S(2)}, u32[]{:S(2)}) collective-permute-start(f32[112,128]{1,0:T(8,128)S(1)} %slice_add_fusion.6), channel_id=1, source_target_pairs={{0,16},{8,24},{16,0},{24,8},{1,17},{9,25},{17,1},{25,9},{2,18},{10... | collective-permute-start | bytes 172040 | tf_op jit(solution)/shard_map/ppermute | solution.py:469
  44.0 3.2 %shard_map.83 = (f32[24,64,128]{2,1,0:T(8,128)S(1)}, f32[64,256]{1,0:T(8,128)S(1)}, f32[16,64,128]{2,1,0:T(8,128)S(1)}) custom-call(f32[24,64,128]{2,1,0:T(8,128)S(1)} %get-tuple-element.118.ext_ref, f32[64,256]{1,0:T(8,128)S(1)} %get-tuple-element.119.side_ref, f32[12,64,256]{2,1,0:T(8,128)S(1)} %get-tuple-element.120.acc_in, ...), custom_call_target="tpu_custom_call" | custom-call | flops 4600000000 | bytes 14800000 | tf_op jit(solution)/shard_map/pallas_call | solution.py:421
  47.3 4.3 %collective-permute-start.12 = (f32[112,128]{1,0:T(8,128)S(1)}, f32[112,128]{1,0:T(8,128)S(1)}, u32[]{:S(2)}, u32[]{:S(2)}) collective-permute-start(f32[112,128]{1,0:T(8,128)S(1)} %subtract_maximum_fusion.2.mine), channel_id=1, source_target_pairs={{0,1},{1,0},{2,3},{3,2},{4,5},{5,4},{6,7},{7,6},{8,9},{9,8},{10,11... | collective-permute-start | bytes 172040 | tf_op jit(solution)/shard_map/ppermute | solution.py:436
  52.5 3.5 %shard_map.84 = (f32[112,128]{1,0:T(8,128)S(1)}, f32[176,128]{1,0:T(8,128)S(1)}, f32[8,64,128]{2,1,0:T(8,128)S(1)}, f32[8,64,128]{2,1,0:T(8,128)S(1)}, f32[64,12...) custom-call(f32[16,448,128]{2,1,0:T(8,128)S(1)} %copy-done.4, f32[16,128]{1,0:T(8,128)S(1)} %copy-done.2, ...), custom_call_target="tpu_custom_call" | custom-call | flops 5750000128 | bytes 18500000 | tf_op jit(solution)/shard_map/pallas_call | solution.py:421
  59.0 3.3 %collective-permute-done.14 = f32[176,128]{1,0:T(8,128)S(1)} collective-permute-done((f32[176,128]{1,0:T(8,128)S(1)}, f32[176,128]{1,0:T(8,128)S(1)}, u32[]{:S(2)}, u32[]{:S(2)}) %collective-permute-start.14) | collective-permute-done | bytes 90144 | tf_op jit(solution)/shard_map/ppermute | solution.py:441
  65.5 3.0 %collective-permute-start.18 = (f32[176,128]{1,0:T(8,128)S(1)}, f32[176,128]{1,0:T(8,128)S(1)}, u32[]{:S(2)}, u32[]{:S(2)}) collective-permute-start(f32[176,128]{1,0:T(8,128)S(1)} %pad_maximum_fusion.6), channel_id=1, source_target_pairs={{0,8},{8,0},{16,24},{24,16},{1,9},{9,1},{17,25},{25,17},{2,10},{10... | collective-permute-start | bytes 270344 | tf_op jit(solution)/shard_map/ppermute | solution.py:446
  70.4 2.2 %collective-permute-start.19 = (f32[112,128]{1,0:T(8,128)S(1)}, f32[112,128]{1,0:T(8,128)S(1)}, u32[]{:S(2)}, u32[]{:S(2)}) collective-permute-start(f32[112,128]{1,0:T(8,128)S(1)} %slice_add_fusion.3), channel_id=1, source_target_pairs={{0,16},{8,24},{16,0},{24,8},{1,17},{9,25},{17,1},{25,9},{2,18},{10... | collective-permute-start | bytes 172040 | tf_op jit(solution)/shard_map/ppermute | solution.py:469
  72.6 3.2 %shard_map.86 = (f32[24,64,128]{2,1,0:T(8,128)S(1)}, f32[64,256]{1,0:T(8,128)S(1)}, f32[16,64,128]{2,1,0:T(8,128)S(1)}) custom-call(f32[24,64,128]{2,1,0:T(8,128)S(1)} %get-tuple-element.140.ext_ref, f32[64,256]{1,0:T(8,128)S(1)} %get-tuple-element.141.side_ref, f32[12,64,256]{2,1,0:T(8,128)S(1)} %get-tuple-element.142.acc_in, ...), custom_call_target="tpu_custom_call" | custom-call | flops 4600000000 | bytes 14800000 | tf_op jit(solution)/shard_map/pallas_call | solution.py:421
  75.9 3.8 %collective-permute-start.21 = (f32[112,128]{1,0:T(8,128)S(1)}, f32[112,128]{1,0:T(8,128)S(1)}, u32[]{:S(2)}, u32[]{:S(2)}) collective-permute-start(f32[112,128]{1,0:T(8,128)S(1)} %subtract_maximum_fusion.1.mine), channel_id=1, source_target_pairs={{0,1},{1,0},{2,3},{3,2},{4,5},{5,4},{6,7},{7,6},{8,9},{9,8},{10,11... | collective-permute-start | bytes 172040 | tf_op jit(solution)/shard_map/ppermute | solution.py:436
  80.6 3.5 %shard_map.87 = (f32[112,128]{1,0:T(8,128)S(1)}, f32[176,128]{1,0:T(8,128)S(1)}, f32[8,64,128]{2,1,0:T(8,128)S(1)}, f32[8,64,128]{2,1,0:T(8,128)S(1)}, f32[64,12...) custom-call(f32[16,448,128]{2,1,0:T(8,128)S(1)} %copy-done.4, f32[16,128]{1,0:T(8,128)S(1)} %copy-done.2, ...), custom_call_target="tpu_custom_call" | custom-call | flops 5750000128 | bytes 18500000 | tf_op jit(solution)/shard_map/pallas_call | solution.py:421
  87.2 3.7 %collective-permute-done.23 = f32[176,128]{1,0:T(8,128)S(1)} collective-permute-done((f32[176,128]{1,0:T(8,128)S(1)}, f32[176,128]{1,0:T(8,128)S(1)}, u32[]{:S(2)}, u32[]{:S(2)}) %collective-permute-start.23) | collective-permute-done | bytes 90144 | tf_op jit(solution)/shard_map/ppermute | solution.py:441
  91.9 2.1 %collective-permute-done.24 = f32[112,128]{1,0:T(8,128)S(1)} collective-permute-done((f32[112,128]{1,0:T(8,128)S(1)}, f32[112,128]{1,0:T(8,128)S(1)}, u32[]{:S(2)}, u32[]{:S(2)}) %collective-permute-start.24) | collective-permute-done | bytes 57376 | tf_op jit(solution)/shard_map/ppermute | solution.py:460
  94.0 2.2 %collective-permute-start.27 = (f32[176,128]{1,0:T(8,128)S(1)}, f32[176,128]{1,0:T(8,128)S(1)}, u32[]{:S(2)}, u32[]{:S(2)}) collective-permute-start(f32[176,128]{1,0:T(8,128)S(1)} %pad_maximum_fusion.8), channel_id=1, source_target_pairs={{0,8},{8,0},{16,24},{24,16},{1,9},{9,1},{17,25},{25,17},{2,10},{10... | collective-permute-start | bytes 270344 | tf_op jit(solution)/shard_map/ppermute | solution.py:446
  98.2 2.3 %collective-permute-start.28 = (f32[112,128]{1,0:T(8,128)S(1)}, f32[112,128]{1,0:T(8,128)S(1)}, u32[]{:S(2)}, u32[]{:S(2)}) collective-permute-start(f32[112,128]{1,0:T(8,128)S(1)} %slice_add_fusion), channel_id=1, source_target_pairs={{0,16},{8,24},{16,0},{24,8},{1,17},{9,25},{17,1},{25,9},{2,18},{10... | collective-permute-start | bytes 172040 | tf_op jit(solution)/shard_map/ppermute | solution.py:469
  100.5 2.5 %shard_map.89 = f32[64,16,128]{2,1,0:T(8,128)} custom-call(f32[24,64,128]{2,1,0:T(8,128)S(1)} %get-tuple-element.160.ext_ref, f32[64,256]{1,0:T(8,128)S(1)} %get-tuple-element.161.side_ref, f32[12,64,256]{2,1,0:T(8,128)S(1)} %get-tuple-element.162.acc_in, f32[64,256]{1,0:T(8,128)S(1)} %get-tuple-element.163.near_ref, ...), custom_call_target="tpu_custom_call" | custom-call | flops 3449999872 | bytes 11100000 | tf_op jit(solution)/shard_map/pallas_call | solution.py:421
  103.0 5.0 %collective-permute-start.30 = (f32[112,128]{1,0:T(8,128)S(1)}, f32[112,128]{1,0:T(8,128)S(1)}, u32[]{:S(2)}, u32[]{:S(2)}) collective-permute-start(f32[112,128]{1,0:T(8,128)S(1)} %subtract_maximum_fusion), channel_id=1, source_target_pairs={{0,1},{1,0},{2,3},{3,2},{4,5},{5,4},{6,7},{7,6},{8,9},{9,8},{10,11... | collective-permute-start | bytes 172040 | tf_op jit(solution)/shard_map/ppermute | solution.py:436
  (130 shorter events, 34.1 us)
Async XLA Ops:
  3.6 4.3 %collective-permute-start.1 = (f32[72,128]{1,0:T(8,128)S(1)}, f32[72,128]{1,0:T(8,128)S(1)}, u32[]{:S(2)}, u32[]{:S(2)}) collective-permute-start(f32[72,128]{1,0:T(8,128)S(1)} %get-tuple-element.87), channel_id=1, source_target_pairs={{0,7},{1,2},{2,1},{3,4},{4,3},{5,6},{6,5},{7,0},{8,15},{9,10},{10,... | collective-permute-start | bytes 110600 | tf_op jit(solution)/shard_map/ppermute | solution.py:441
  8.0 10.5 %collective-permute-start.2 = (f32[344,128]{1,0:T(8,128)S(1)}, f32[344,128]{1,0:T(8,128)S(1)}, u32[]{:S(2)}, u32[]{:S(2)}) collective-permute-start(f32[344,128]{1,0:T(8,128)S(1)} %constant_dynamic-update-slice_fusion), channel_id=1, source_target_pairs={{0,8},{8,0},{16,24},{24,16},{1,9},{9,1},{17,25},{25,17},{2,10},{10... | collective-permute-start | bytes 528392 | tf_op jit(solution)/shard_map/ppermute | solution.py:446
  10.3 8.2 %collective-permute-start.3 = (f32[344,128]{1,0:T(8,128)S(1)}, f32[344,128]{1,0:T(8,128)S(1)}, u32[]{:S(2)}, u32[]{:S(2)}) collective-permute-start(f32[344,128]{1,0:T(8,128)S(1)} %get-tuple-element.181), channel_id=1, source_target_pairs={{8,16},{16,8},{9,17},{17,9},{10,18},{18,10},{11,19},{19,11},{12,20... | collective-permute-start | bytes 528392 | tf_op jit(solution)/shard_map/ppermute | solution.py:452
  24.1 6.1 %collective-permute-start.4 = (f32[176,128]{1,0:T(8,128)S(1)}, f32[176,128]{1,0:T(8,128)S(1)}, u32[]{:S(2)}, u32[]{:S(2)}) collective-permute-start(f32[176,128]{1,0:T(8,128)S(1)} %get-tuple-element.103), channel_id=1, source_target_pairs={{0,1},{1,0},{2,3},{3,2},{4,5},{5,4},{6,7},{7,6},{8,9},{9,8},{10,11... | collective-permute-start | bytes 270344 | tf_op jit(solution)/shard_map/ppermute | solution.py:436
  25.1 12.9 %collective-permute-start.7 = (f32[8,64,128]{2,1,0:T(8,128)S(1)}, f32[8,64,128]{2,1,0:T(8,128)S(1)}, u32[]{:S(2)}, u32[]{:S(2)}) collective-permute-start(f32[8,64,128]{2,1,0:T(8,128)S(1)} %get-tuple-element.115), channel_id=1, source_target_pairs={{0,8},{8,0},{16,24},{24,16},{1,9},{9,1},{17,25},{25,17},{2,10},{10... | collective-permute-start | bytes 786440 | tf_op jit(solution)/shard_map/ppermute | solution.py:446
  29.2 8.8 %collective-permute-start.8 = (f32[8,64,128]{2,1,0:T(8,128)S(1)}, f32[8,64,128]{2,1,0:T(8,128)S(1)}, u32[]{:S(2)}, u32[]{:S(2)}) collective-permute-start(f32[8,64,128]{2,1,0:T(8,128)S(1)} %get-tuple-element.116), channel_id=1, source_target_pairs={{8,16},{16,8},{9,17},{17,9},{10,18},{18,10},{11,19},{19,11},{12,20... | collective-permute-start | bytes 786440 | tf_op jit(solution)/shard_map/ppermute | solution.py:452
  30.2 4.7 %collective-permute-start.5 = (f32[176,128]{1,0:T(8,128)S(1)}, f32[176,128]{1,0:T(8,128)S(1)}, u32[]{:S(2)}, u32[]{:S(2)}) collective-permute-start(f32[176,128]{1,0:T(8,128)S(1)} %pad_maximum_fusion.3), channel_id=1, source_target_pairs={{0,7},{1,2},{2,1},{3,4},{4,3},{5,6},{6,5},{7,0},{8,15},{9,10},{10,... | collective-permute-start | bytes 270344 | tf_op jit(solution)/shard_map/ppermute | solution.py:441
  39.6 4.4 %collective-permute-start.11 = (f32[64,128]{1,0:T(8,128)S(1)}, f32[64,128]{1,0:T(8,128)S(1)}, u32[]{:S(2)}, u32[]{:S(2)}) collective-permute-start(f32[64,128]{1,0:T(8,128)S(1)} %get-tuple-element.178), channel_id=1, source_target_pairs={{8,16},{16,8},{9,17},{17,9},{10,18},{18,10},{11,19},{19,11},{12,20... | collective-permute-start | bytes 98312 | tf_op jit(solution)/shard_map/ppermute | solution.py:452
  41.6 5.7 %collective-permute-start.10 = (f32[112,128]{1,0:T(8,128)S(1)}, f32[112,128]{1,0:T(8,128)S(1)}, u32[]{:S(2)}, u32[]{:S(2)}) collective-permute-start(f32[112,128]{1,0:T(8,128)S(1)} %slice_add_fusion.6), channel_id=1, source_target_pairs={{0,16},{8,24},{16,0},{24,8},{1,17},{9,25},{17,1},{25,9},{2,18},{10... | collective-permute-start | bytes 172040 | tf_op jit(solution)/shard_map/ppermute | solution.py:469
  47.3 5.2 %collective-permute-start.12 = (f32[112,128]{1,0:T(8,128)S(1)}, f32[112,128]{1,0:T(8,128)S(1)}, u32[]{:S(2)}, u32[]{:S(2)}) collective-permute-start(f32[112,128]{1,0:T(8,128)S(1)} %subtract_maximum_fusion.2.mine), channel_id=1, source_target_pairs={{0,1},{1,0},{2,3},{3,2},{4,5},{5,4},{6,7},{7,6},{8,9},{9,8},{10,11... | collective-permute-start | bytes 172040 | tf_op jit(solution)/shard_map/ppermute | solution.py:436
  56.4 9.1 %collective-permute-start.16 = (f32[8,64,128]{2,1,0:T(8,128)S(1)}, f32[8,64,128]{2,1,0:T(8,128)S(1)}, u32[]{:S(2)}, u32[]{:S(2)}) collective-permute-start(f32[8,64,128]{2,1,0:T(8,128)S(1)} %get-tuple-element.137), channel_id=1, source_target_pairs={{0,8},{8,0},{16,24},{24,16},{1,9},{9,1},{17,25},{25,17},{2,10},{10... | collective-permute-start | bytes 786440 | tf_op jit(solution)/shard_map/ppermute | solution.py:446
  56.5 9.0 %collective-permute-start.17 = (f32[8,64,128]{2,1,0:T(8,128)S(1)}, f32[8,64,128]{2,1,0:T(8,128)S(1)}, u32[]{:S(2)}, u32[]{:S(2)}) collective-permute-start(f32[8,64,128]{2,1,0:T(8,128)S(1)} %get-tuple-element.138), channel_id=1, source_target_pairs={{8,16},{16,8},{9,17},{17,9},{10,18},{18,10},{11,19},{19,11},{12,20... | collective-permute-start | bytes 786440 | tf_op jit(solution)/shard_map/ppermute | solution.py:452
  57.3 5.0 %collective-permute-start.14 = (f32[176,128]{1,0:T(8,128)S(1)}, f32[176,128]{1,0:T(8,128)S(1)}, u32[]{:S(2)}, u32[]{:S(2)}) collective-permute-start(f32[176,128]{1,0:T(8,128)S(1)} %pad_maximum_fusion.5), channel_id=1, source_target_pairs={{0,7},{1,2},{2,1},{3,4},{4,3},{5,6},{6,5},{7,0},{8,15},{9,10},{10,... | collective-permute-start | bytes 270344 | tf_op jit(solution)/shard_map/ppermute | solution.py:441
  65.5 4.9 %collective-permute-start.18 = (f32[176,128]{1,0:T(8,128)S(1)}, f32[176,128]{1,0:T(8,128)S(1)}, u32[]{:S(2)}, u32[]{:S(2)}) collective-permute-start(f32[176,128]{1,0:T(8,128)S(1)} %pad_maximum_fusion.6), channel_id=1, source_target_pairs={{0,8},{8,0},{16,24},{24,16},{1,9},{9,1},{17,25},{25,17},{2,10},{10... | collective-permute-start | bytes 270344 | tf_op jit(solution)/shard_map/ppermute | solution.py:446
  68.5 4.1 %collective-permute-start.20 = (f32[64,128]{1,0:T(8,128)S(1)}, f32[64,128]{1,0:T(8,128)S(1)}, u32[]{:S(2)}, u32[]{:S(2)}) collective-permute-start(f32[64,128]{1,0:T(8,128)S(1)} %get-tuple-element.175), channel_id=1, source_target_pairs={{8,16},{16,8},{9,17},{17,9},{10,18},{18,10},{11,19},{19,11},{12,20... | collective-permute-start | bytes 98312 | tf_op jit(solution)/shard_map/ppermute | solution.py:452
  70.4 5.4 %collective-permute-start.19 = (f32[112,128]{1,0:T(8,128)S(1)}, f32[112,128]{1,0:T(8,128)S(1)}, u32[]{:S(2)}, u32[]{:S(2)}) collective-permute-start(f32[112,128]{1,0:T(8,128)S(1)} %slice_add_fusion.3), channel_id=1, source_target_pairs={{0,16},{8,24},{16,0},{24,8},{1,17},{9,25},{17,1},{25,9},{2,18},{10... | collective-permute-start | bytes 172040 | tf_op jit(solution)/shard_map/ppermute | solution.py:469
  75.9 4.7 %collective-permute-start.21 = (f32[112,128]{1,0:T(8,128)S(1)}, f32[112,128]{1,0:T(8,128)S(1)}, u32[]{:S(2)}, u32[]{:S(2)}) collective-permute-start(f32[112,128]{1,0:T(8,128)S(1)} %subtract_maximum_fusion.1.mine), channel_id=1, source_target_pairs={{0,1},{1,0},{2,3},{3,2},{4,5},{5,4},{6,7},{7,6},{8,9},{9,8},{10,11... | collective-permute-start | bytes 172040 | tf_op jit(solution)/shard_map/ppermute | solution.py:436
  84.5 9.5 %collective-permute-start.25 = (f32[8,64,128]{2,1,0:T(8,128)S(1)}, f32[8,64,128]{2,1,0:T(8,128)S(1)}, u32[]{:S(2)}, u32[]{:S(2)}) collective-permute-start(f32[8,64,128]{2,1,0:T(8,128)S(1)} %get-tuple-element.157), channel_id=1, source_target_pairs={{0,8},{8,0},{16,24},{24,16},{1,9},{9,1},{17,25},{25,17},{2,10},{10... | collective-permute-start | bytes 786440 | tf_op jit(solution)/shard_map/ppermute | solution.py:446
  85.2 8.9 %collective-permute-start.26 = (f32[8,64,128]{2,1,0:T(8,128)S(1)}, f32[8,64,128]{2,1,0:T(8,128)S(1)}, u32[]{:S(2)}, u32[]{:S(2)}) collective-permute-start(f32[8,64,128]{2,1,0:T(8,128)S(1)} %get-tuple-element.158), channel_id=1, source_target_pairs={{8,16},{16,8},{9,17},{17,9},{10,18},{18,10},{11,19},{19,11},{12,20... | collective-permute-start | bytes 786440 | tf_op jit(solution)/shard_map/ppermute | solution.py:452
  85.9 5.0 %collective-permute-start.23 = (f32[176,128]{1,0:T(8,128)S(1)}, f32[176,128]{1,0:T(8,128)S(1)}, u32[]{:S(2)}, u32[]{:S(2)}) collective-permute-start(f32[176,128]{1,0:T(8,128)S(1)} %pad_maximum_fusion.7), channel_id=1, source_target_pairs={{0,7},{1,2},{2,1},{3,4},{4,3},{5,6},{6,5},{7,0},{8,15},{9,10},{10,... | collective-permute-start | bytes 270344 | tf_op jit(solution)/shard_map/ppermute | solution.py:441
  94.0 4.2 %collective-permute-start.27 = (f32[176,128]{1,0:T(8,128)S(1)}, f32[176,128]{1,0:T(8,128)S(1)}, u32[]{:S(2)}, u32[]{:S(2)}) collective-permute-start(f32[176,128]{1,0:T(8,128)S(1)} %pad_maximum_fusion.8), channel_id=1, source_target_pairs={{0,8},{8,0},{16,24},{24,16},{1,9},{9,1},{17,25},{25,17},{2,10},{10... | collective-permute-start | bytes 270344 | tf_op jit(solution)/shard_map/ppermute | solution.py:446
  96.3 4.2 %collective-permute-start.29 = (f32[64,128]{1,0:T(8,128)S(1)}, f32[64,128]{1,0:T(8,128)S(1)}, u32[]{:S(2)}, u32[]{:S(2)}) collective-permute-start(f32[64,128]{1,0:T(8,128)S(1)} %get-tuple-element.172), channel_id=1, source_target_pairs={{8,16},{16,8},{9,17},{17,9},{10,18},{18,10},{11,19},{19,11},{12,20... | collective-permute-start | bytes 98312 | tf_op jit(solution)/shard_map/ppermute | solution.py:452
  98.2 4.8 %collective-permute-start.28 = (f32[112,128]{1,0:T(8,128)S(1)}, f32[112,128]{1,0:T(8,128)S(1)}, u32[]{:S(2)}, u32[]{:S(2)}) collective-permute-start(f32[112,128]{1,0:T(8,128)S(1)} %slice_add_fusion), channel_id=1, source_target_pairs={{0,16},{8,24},{16,0},{24,8},{1,17},{9,25},{17,1},{25,9},{2,18},{10... | collective-permute-start | bytes 172040 | tf_op jit(solution)/shard_map/ppermute | solution.py:469
  103.0 5.9 %collective-permute-start.30 = (f32[112,128]{1,0:T(8,128)S(1)}, f32[112,128]{1,0:T(8,128)S(1)}, u32[]{:S(2)}, u32[]{:S(2)}) collective-permute-start(f32[112,128]{1,0:T(8,128)S(1)} %subtract_maximum_fusion), channel_id=1, source_target_pairs={{0,1},{1,0},{2,3},{3,2},{4,5},{5,4},{6,7},{7,6},{8,9},{9,8},{10,11... | collective-permute-start | bytes 172040 | tf_op jit(solution)/shard_map/ppermute | solution.py:436
  (14 other events, 37.9 us)

commit v3 on v2

--- a/solution.py
+++ b/solution.py
@@ -142,14 +142,25 @@
     return jnp.where(c < RADIUS, c - RADIUS, width + c - RADIUS)
 
 
-def forward_weights_kernel(family, table, obs_ref, seen_ref, w_high, w_low, s_high, s_low, sems):
+def forward_weights_kernel(family, table, place, obs_ref, spectra_ref, seen_ref, mine, other, w_high, w_low, s_high, s_low, sems):
     depth, height, width = obs_ref.shape
     copies = []
     for i in range(height):
         copies.append(pltpu.make_async_copy(obs_ref.at[:, i, :], seen_ref.at[i, pl.ds(0, depth), :], sems.at[i]))
         copies[-1].start()
     start = depth // 8 * 8
-    own = lambda u, v: table[family[0, 0], u * KS + v]
+    channels = spectra_ref.shape[0]
+    quarter = seen_ref.shape[1] // 4
+    total = -(-seen_ref.shape[1] // 128) * 128
+    spectra = jnp.concatenate([spectra_ref[...], jnp.zeros((channels, total - depth), F32)], axis=1).T
+    halves = [
+        jnp.concatenate([spectra[q * quarter : (q + 1) * quarter], spectra[(q + 1) * quarter : (q + 2) * quarter]], axis=1)
+        for q in (0, 2)
+    ]
+    second = place[HALF] == 1
+    mine[...] = jnp.where(second, halves[1], halves[0])
+    other[...] = jnp.where(second, halves[0], halves[1])
+    own = lambda u, v: table[u, family[0, 0], v]
     build_main(own, w_high, w_low, (), width)
     n = height * EDGE
     shape = (EDGE, n)
@@ -176,9 +187,13 @@
         seen_ref[i, start:] = jnp.where(sub < depth - start, seen_ref[i, start:], 0.0)
 
 
-def adjoint_weights_kernel(families, table, w_high, w_low, s_high, s_low, scratch, *, height, width):
+def adjoint_weights_kernel(marks_up, marks, marks_down, table, w_high, w_low, s_high, s_low, scratch, *, height, width):
+    families = []
+    for ref in (marks_up, marks, marks_down):
+        for k in range(3):
+            families.append(jnp.max(ref[8 * k : 8 * k + 8]).astype(jnp.int32))
     for b in range(3):
-        build_main(lambda u, v, b=b: table[families[3 * b + 1], (KS - 1 - u) * KS + KS - 1 - v], w_high, w_low, (b,), width)
+        build_main(lambda u, v, b=b: table[KS - 1 - u, families[3 * b + 1], KS - 1 - v], w_high, w_low, (b,), width)
     n = s_high.shape[1]
     half = n // 2
     shape = (EDGE, n)
@@ -209,7 +224,7 @@
         for b in range(3):
             tile = 3 * b + (0, 2, 1)[kind]
             bands = [
-                band_sum([table[families[tile], (KS - 1 - u) * KS + KS - 1 - v] for v in range(KS)], delta) for u in range(KS)
+                band_sum([table[KS - 1 - u, families[tile], KS - 1 - v] for v in range(KS)], delta) for u in range(KS)
             ]
             q_range = (range(0, EDGE), range(EDGE, EDGE + height), range(EDGE + height, 2 * EDGE + height))[b]
             for q in q_range:
@@ -253,11 +268,13 @@
     for a in range(height + EDGE):
         if a < RADIUS:
             row = jnp.where(odd, p1[a * channels : a * channels + channels], p2[a * channels : a * channels + channels])
+            row = jnp.where(place[UP] == 1, row, 0.0)
         elif a < RADIUS + height:
             row = rows_ref[a - RADIUS]
         else:
             k = (a - RADIUS - height) * channels
             row = jnp.where(odd, p2[k : k + channels], p1[k : k + channels])
+            row = jnp.where(place[DOWN] == 1, row, 0.0)
         ext_ref[a] = row
         high, low = split(row)
         a2_high[a // 2, :, a % 2 * width : a % 2 * width + width] = high
@@ -356,36 +373,44 @@
     adjoint_into(acc, g_high, g_low, EDGE // 2, wa_high, wa_low, 1)
 
 
-def maps_kernel(
-    ext_ref, side_ref, acc_in, near_ref, p1, p2, left, right, above, below, place,
-    wa_high, wa_low, sa_high, sa_low, *rest, last,
-):
-    if last:
-        out_ref, g_high, g_low, acc = rest
-        height = out_ref.shape[1]
-    else:
-        (wf_high, wf_low, sf_high, sf_low, ext_out, side_out, b_ref, g_high, g_low, acc, a2_high, a2_low, acc_b) = rest
-        height = b_ref.shape[0]
-    channels, width = left.shape
-    ext_rows = height + EDGE
+def halo_maps_kernel(acc_in, near_in, p1, p2, place, wa_high, wa_low, acc, near_ref, g_high, g_low):
+    channels = near_in.shape[0]
+    width = near_in.shape[1] // 2
+    height = 2 * acc.shape[0] - EDGE
     odd = place[ROW_ODD] == 1
     lane = lanes((channels, width))
-    near = [near_ref[:, :width], near_ref[:, width:]]
+    near = [near_in[:, :width], near_in[:, width:]]
     for k in range(2 * EDGE):
         q = k if k < EDGE else k + height
-        row = jnp.where(odd, p1[k], p2[k]) if k < EDGE else jnp.where(odd, p2[k - EDGE], p1[k - EDGE])
+        if k < EDGE:
+            row = jnp.where(place[UP] == 1, jnp.where(odd, p1[k], p2[k]), 0.0)
+        else:
+            row = jnp.where(place[DOWN] == 1, jnp.where(odd, p2[k - EDGE], p1[k - EDGE]), 0.0)
         put_pair(g_high, g_low, k, row)
         moved = pltpu.roll(row, (RADIUS + q * EDGE) % width, 1)
         near[q // height] = jnp.where(lane // EDGE == q % height, moved, near[q // height])
-    side_in = jnp.concatenate([left[...], right[...], above[...], below[...]] + near, axis=1)
+    near_ref[...] = jnp.concatenate(near, axis=1)
+    n = EDGE // 2
+    adjoint_into(acc, g_high.at[:n], g_low.at[:n], 0, wa_high, wa_low, 0)
+    adjoint_into(acc, g_high.at[n:], g_low.at[n:], n + height // 2, wa_high, wa_low, 2)
+
+
+def maps_kernel(
+    ext_ref, side_ref, acc, near_ref, left, right, above, below, place, sa_high, sa_low, *rest, last,
+):
+    if last:
+        (out_ref,) = rest
+        height = out_ref.shape[1]
+    else:
+        (wf_high, wf_low, sf_high, sf_low, ext_out, side_out, b_ref, a2_high, a2_low, acc_b) = rest
+        height = b_ref.shape[0]
+    width = left.shape[1]
+    ext_rows = height + EDGE
+    side_in = jnp.concatenate([left[...], right[...], above[...], below[...], near_ref[...]], axis=1)
     side_high, side_low = split(side_in)
     side_mm = mm(side_high, sa_high[...]) + mm(side_low, sa_high[...]) + mm(side_high, sa_low[...])
     half = side_mm.shape[1] // 2
     rim = side_mm[:, half:]
-    acc[...] = acc_in[...]
-    n = EDGE // 2
-    adjoint_into(acc, g_high.at[:n], g_low.at[:n], 0, wa_high, wa_low, 0)
-    adjoint_into(acc, g_high.at[n:], g_low.at[n:], n + height // 2, wa_high, wa_low, 2)
     for a in range(ext_rows):
         if last and not RADIUS <= a < RADIUS + height:
             continue
@@ -417,13 +442,23 @@
     blur_into(b_ref, a2_high, a2_low, side, wf_high, wf_low, sf_high, sf_low, acc_b)
 
 
-def call(kernel, micros, outs, scratch, specs, *args):
+def spectra_kernel(mine, other, place, out_ref):
+    channels, depth = out_ref.shape
+    second = place[HALF] == 1
+    first = jnp.where(second, other[...], mine[...])
+    last = jnp.where(second, mine[...], other[...])
+    parts = [first[:, :channels], first[:, channels:], last[:, :channels], last[:, channels:]]
+    out_ref[...] = jnp.concatenate(parts, axis=0).T[:, :depth]
+
+
+def call(kernel, micros, outs, scratch, specs, *args, aliases=None):
     return pl.pallas_call(
         kernel,
         out_shape=[jax.ShapeDtypeStruct(s, d) for s, d in outs],
         in_specs=specs,
         out_specs=[VMEM] * len(outs),
         scratch_shapes=[pltpu.VMEM(*s) if isinstance(s, tuple) else s for s in scratch],
+        input_output_aliases=aliases or {},
         compiler_params=PARAMS,
         cost_estimate=pl.CostEstimate(
             flops=int(micros * 1.15e9), bytes_accessed=int(micros * 3.7e6), transcendentals=0
@@ -448,27 +483,17 @@
 
 def pair_two(x):
     count = lax.axis_size("rows")
-    pairs = [(i, i + 1) for i in range(1, count - 1, 2)]
-    return lax.ppermute(x, "rows", pairs + [(b, a) for a, b in pairs])
-
-
-def chips_sum(x):
+    return lax.ppermute(x, "rows", [(i, min(max(i + 1 if i % 2 else i - 1, 0), count - 1)) for i in range(count)])
+
+
+def col_swap(x, mask):
     count = lax.axis_size("cols")
-    step = 4
-    while step < count:
-        route = [(i, (((i + 1) % count) ^ step) - 1) for i in range(count)]
-        x = x + lax.ppermute(x, "cols", [(i, j % count) for i, j in route])
-        step *= 2
-    return x
-
-
-def rows_sum(x):
+    return lax.ppermute(x, "cols", [(i, (((i + 1) % count ^ mask) - 1) % count) for i in range(count)])
+
+
+def row_swap(x, mask):
     count = lax.axis_size("rows")
-    step = 2
-    while step < count:
-        x = x + lax.ppermute(x, "rows", [(i, i ^ step) for i in range(count)])
-        step *= 2
-    return x
+    return lax.ppermute(x, "rows", [(i, i ^ mask) for i in range(count)])
 
 
 def on_device(observed, nonlin, abundance, spectra, kernels, tile_family):
@@ -486,6 +511,12 @@
     ).astype(jnp.int32)
     has_left = (col_at > 0).astype(F32)
     has_right = (col_at < n_cols - 1).astype(F32)
+    has_up = (row_at > 0).astype(F32)
+    has_down = (row_at < n_rows - 1).astype(F32)
+    table = jnp.transpose(kernels, (1, 0, 2))
+    place, abundance, row_odd, col_odd, has_left, has_right, has_up, has_down = lax.optimization_barrier(
+        (place, abundance, row_odd, col_odd, has_left, has_right, has_up, has_down)
+    )
     tile = (channels, width)
 
     def sides(core, cross):
@@ -520,21 +551,22 @@
         return jnp.where(row_odd, x1, x2), jnp.where(row_odd, x2, x1)
 
     above, below = above_below(got1[body : body + channels], got2[body : body + channels])
-    table = kernels.reshape(kernels.shape[0], KS * KS)
+    above, below = above * has_up, below * has_down
     pairs = height // 2
     ext_rows = height + EDGE
     main_w = ((RADIUS + 1, 2 * width, 2 * width), BF16)
     side_f = ((2 * width, height * EDGE), BF16)
-    any_space = pl.BlockSpec(memory_space=pl.ANY)
-    seen, *wf = call(
+    hbm = pl.BlockSpec(memory_space=pltpu.HBM)
+    half_shape = ((quarter, 2 * channels), F32)
+    seen, mine, other, *wf = call(
         forward_weights_kernel,
         3,
-        [((height, full, width), F32), main_w, main_w, side_f, side_f],
+        [((height, full, width), F32), half_shape, half_shape, main_w, main_w, side_f, side_f],
         [pltpu.SemaphoreType.DMA((height,))],
-        [SMEM, SMEM, any_space],
-        tile_family, table, observed,
+        [SMEM, SMEM, SMEM, hbm, VMEM],
+        tile_family, table, place, observed, spectra.T,
     )
-    got1, got2, seen, *wf = lax.optimization_barrier((got1, got2, seen, *wf))
+    got1, got2, seen, mine, other, *wf = lax.optimization_barrier((got1, got2, seen, mine, other, *wf))
     ext, side, blurred = call(
         start_kernel,
         2,
@@ -544,7 +576,6 @@
         a_rows, got1, got2, left, right, above, below, place, *wf,
     )
     marks_up, marks_down = above_below(got1[body + channels :], got2[body + channels :])
-    families = jnp.concatenate([marks_up, marks, marks_down])[::8, 0].astype(jnp.int32)
     main_a = ((3, RADIUS + 1, 2 * width, 2 * width), BF16)
     side_a = ((6 * width, 4 * width), BF16)
 
@@ -554,15 +585,24 @@
             3,
             [main_a, main_a, side_a, side_a],
             [((6 * width, 4 * width), F32)],
-            [SMEM, SMEM],
-            families, table,
+            [VMEM, VMEM, VMEM, SMEM],
+            marks_up, marks, marks_down, table,
         )
 
-    padded = jnp.pad(spectra, ((0, full - bands), (0, 0))).reshape(2, 2, quarter, channels)
-    halves = jnp.transpose(padded, (0, 2, 1, 3)).reshape(2, quarter, 2 * channels)
-    mine = lax.dynamic_index_in_dim(halves, half_of, 0, False)
-    other = lax.dynamic_index_in_dim(halves, 1 - half_of, 0, False)
     rate = 40.0 / pixel_count
+    acc_shape = ((ext_rows // 2, channels, 2 * width), F32)
+    near_shape = ((channels, 2 * width), F32)
+
+    def own_part(g_rows, wa):
+        return call(
+            own_maps_kernel,
+            2,
+            [acc_shape, near_shape],
+            [((pairs, channels, 2 * width), BF16)] * 2,
+            [VMEM] * 3,
+            g_rows, wa[0], wa[1],
+        )
+
     for step in range(ITERS):
         last = step == ITERS - 1
         g_mine, to_core, main1, main2, e_cross, g_rows = call(
@@ -582,60 +622,77 @@
         )
         got_core = core_swap(to_core)
         p1 = pair_one(main1)
+        share = g_mine + got_core[:quarter]
+        if step > 0:
+            own, near = own_part(g_rows, wa)
+            main2, own, near = lax.optimization_barrier((main2, own, near))
         p2 = pair_two(main2)
-        share = g_mine + got_core[:quarter]
         got_cross = cross_swap(jnp.concatenate([share, e_cross]))
         if step == 0:
             wa = adjoint_weights()
             got_cross, *wa = lax.optimization_barrier((got_cross, *wa))
+            own, near = own_part(g_rows, wa)
         share = share + got_cross[:quarter]
         left, right, side1, side2 = sides(got_core[quarter:], got_cross[quarter:])
+        step_size = 4
+        while step_size < n_cols:
+            share = share + col_swap(share, step_size)
+            step_size *= 2
+        share, own, near = lax.optimization_barrier((share, own, near))
         own, near = call(
-            own_maps_kernel,
-            2,
-            [((ext_rows // 2, channels, 2 * width), F32), ((channels, 2 * width), F32)],
-            [((pairs, channels, 2 * width), BF16)] * 2,
-            [VMEM] * 3,
-            g_rows, wa[0], wa[1],
+            halo_maps_kernel,
+            1.5,
+            [acc_shape, near_shape],
+            [((EDGE, channels, 2 * width), BF16)] * 2,
+            [VMEM] * 4 + [SMEM] + [VMEM] * 2,
+            own, near, p1, p2, place, wa[0], wa[1],
+            aliases={0: 0, 1: 1},
         )
-        share = chips_sum(share)
-        share, own, near, p1, p2 = lax.optimization_barrier((share, own, near, p1, p2))
         got1 = pair_one(jnp.concatenate([share, side1]))
-        got2 = pair_two(side2)
-        share = share + got1[:quarter]
+        if n_rows == 4:
+            got2 = row_swap(jnp.concatenate([share, side2]), 3)
+            got3 = row_swap(share, 2)
+            got1, got2, own, near = lax.optimization_barrier((got1, got2, own, near))
+            share = (share + got1[:quarter]) + (got3 + got2[:quarter])
+            got2 = got2[quarter:]
+        else:
+            got2 = pair_two(side2)
+            got1, got2, own, near = lax.optimization_barrier((got1, got2, own, near))
+            share = share + got1[:quarter]
+            step_size = 2
+            while step_size < n_rows:
+                share = share + row_swap(share, step_size)
+                step_size *= 2
         above, below = above_below(got1[quarter:], got2)
-        gathered = (ext, side, own, near, p1, p2, left, right, above, below, place) + tuple(wa)
-        g2 = [((EDGE, channels, 2 * width), BF16)] * 2
-        acc = [((ext_rows // 2, channels, 2 * width), F32)]
+        above, below = above * has_up, below * has_down
+        gathered = (ext, side, own, near, left, right, above, below, place) + tuple(wa[2:])
         if last:
             made = call(
                 functools.partial(maps_kernel, last=True),
-                3,
+                1.5,
                 [((channels, height, width), F32)],
-                g2 + acc,
-                [VMEM] * 10 + [SMEM] + [VMEM] * 4,
+                [],
+                [VMEM] * 8 + [SMEM] + [VMEM] * 2,
                 *gathered,
             )
         else:
             made = call(
                 functools.partial(maps_kernel, last=False),
-                4,
+                2.5,
                 [((ext_rows,) + tile, F32), ((channels, 2 * width), F32), ((height,) + tile, F32)],
-                g2 + acc + [((ext_rows // 2, channels, 2 * width), BF16)] * 2 + [((pairs, channels, 2 * width), F32)],
-                [VMEM] * 10 + [SMEM] + [VMEM] * 8,
+                [((ext_rows // 2, channels, 2 * width), BF16)] * 2 + [((pairs, channels, 2 * width), F32)],
+                [VMEM] * 8 + [SMEM] + [VMEM] * 6,
                 *gathered, *wf,
             )
-        share, *made = lax.optimization_barrier((rows_sum(share), *made))
+        share, *made = lax.optimization_barrier((share, *made))
         mine = jnp.maximum(mine - rate * share, 0.0)
         other = core_swap(mine)
         if last:
             (out,) = made
         else:
             ext, side, blurred = made
-    first = jnp.where(half_of == 0, mine, other)
-    second = jnp.where(half_of == 0, other, mine)
-    parts = [first[:, :channels], first[:, channels:], second[:, :channels], second[:, channels:]]
-    return out, jnp.concatenate(parts)[:bands]
+    (result,) = call(spectra_kernel, 1, [((channels, bands), F32)], [], [VMEM, VMEM, SMEM], mine, other, place)
+    return out, result.T
 
 
 def solution(mesh):

time: 110 us -> 109 us (level)
  starting transfers between devices: 49 us -> 43.4 us
  Pallas kernels: 33.1 us -> 38.4 us
  local copies, waits for them, and re-layouts: 6.35 us -> 1.3 us
  waiting for transfers between devices: 18.8 us -> 23.4 us
    ppermute x13, waiting for transfers between devices: 4.27 us -> 12.5 us  [the longest x6 7.42 us: row_swap(): return lax.ppermute(x, 'rows', [(i, i ^ mask) for i in range(count)])]
    ppermute x7, starting transfers between devices: 14 us -> 7.31 us  [pair_one(): return lax.ppermute(x, 'rows', [(i, i ^ 1) for i in range(count)])]
    pallas_call x13 -> x17, Pallas kernels: 33.1 us -> 38.4 us  [call(): pl.pallas_call(kernel, out_shape=[jax.ShapeDtypeStruct(s, d) for s, d in...]
    unnamed x23 -> x14, local copies, waits for them, and re-layouts: 5.67 us -> 1.21 us
    ppermute x4, waiting for transfers between devices: 8.13 us -> 5.74 us  [cross_swap(): lax.ppermute(x, 'cols', [(i, (i + 1 if i % 2 else i - 1) % count) for i i...]
    ppermute x7, waiting for transfers between devices: 3.57 us -> 1.52 us  [pair_one(): return lax.ppermute(x, 'rows', [(i, i ^ 1) for i in range(count)])]
    ppermute x7, starting transfers between devices: 14.9 us -> 13 us  [core_swap(): return lax.ppermute(x, 'cols', [(i, i ^ 1) for i in range(count)])]
    ppermute x4, starting transfers between devices: 4.43 us -> 6.04 us  [cross_swap(): lax.ppermute(x, 'cols', [(i, (i + 1 if i % 2 else i - 1) % count) for i i...]
  transfers between devices with their start and end apart: 31 -> 31, of which waited for: 14 -> 15; matrix products, arithmetic and copies ran while one was open for 1% -> 0% of each run, Pallas kernels for 18% -> 22%
where the time goes in v3:
time: 109 us
  starting transfers between devices  43.4 us (40%)
  Pallas kernels  38.4 us (35%)
  waiting for transfers between devices  23.4 us (21%)
  between operations  1.99 us (2%)
  local copies, waits for them, and re-layouts  1.3 us (1%)
    pallas_call x17, Pallas kernels, call(): pl.pallas_call(kernel, out_shape=[jax.ShapeDtypeStruct(s, d) for s, d in...  38.4 us
    ppermute x7, starting transfers between devices, core_swap(): return lax.ppermute(x, 'cols', [(i, i ^ 1) for i in range(count)])  13 us
    ppermute x6, starting transfers between devices, row_swap(): return lax.ppermute(x, 'rows', [(i, i ^ mask) for i in range(count)])  11.2 us
    ppermute x6, waiting for transfers between devices, row_swap(): return lax.ppermute(x, 'rows', [(i, i ^ mask) for i in range(count)])  7.42 us
    ppermute x7, starting transfers between devices, pair_one(): return lax.ppermute(x, 'rows', [(i, i ^ 1) for i in range(count)])  7.31 us
    ppermute x4, starting transfers between devices, cross_swap(): lax.ppermute(x, 'cols', [(i, (i + 1 if i % 2 else i - 1) % count) for i i...  6.04 us
    ppermute x4, waiting for transfers between devices, cross_swap(): lax.ppermute(x, 'cols', [(i, (i + 1 if i % 2 else i - 1) % count) for i i...  5.74 us
    ppermute x3, waiting for transfers between devices, col_swap(): lax.ppermute(x, 'cols', [(i, (((i + 1) % count ^ mask) - 1) % count) for...  5.09 us
  transfers between devices with their start and end apart: 31, of which 15 were waited for; matrix products, arithmetic and copies ran while one was open for 0% of the time, Pallas kernels for 22%

profile of v3, /device:TPU:1, one launch (start us, length us, event | category | flops | bytes accessed | tf_op | source)
XLA Modules:
  0.0 108.9 jit_solution(5874222581759201372)
XLA Ops:
  3.9 2.6 %collective-permute-start.1 = (f32[72,128]{1,0:T(8,128)S(1)}, f32[72,128]{1,0:T(8,128)S(1)}, u32[]{:S(2)}, u32[]{:S(2)}) collective-permute-start(f32[72,128]{1,0:T(8,128)S(1)} %get-tuple-element.121), channel_id=1, source_target_pairs={{0,7},{1,2},{2,1},{3,4},{4,3},{5,6},{6,5},{7,0},{8,15},{9,10},{10,... | collective-permute-start | bytes 110600 | tf_op jit(solution)/shard_map/ppermute | solution.py:476
  6.6 1.6 %collective-permute-done.1 = f32[72,128]{1,0:T(8,128)S(1)} collective-permute-done((f32[72,128]{1,0:T(8,128)S(1)}, f32[72,128]{1,0:T(8,128)S(1)}, u32[]{:S(2)}, u32[]{:S(2)}) %collective-permute-start.1) | collective-permute-done | bytes 36896 | tf_op jit(solution)/shard_map/ppermute | solution.py:476
  8.2 2.3 %collective-permute-start.2 = (f32[344,128]{1,0:T(8,128)S(1)}, f32[344,128]{1,0:T(8,128)S(1)}, u32[]{:S(2)}, u32[]{:S(2)}) collective-permute-start(f32[344,128]{1,0:T(8,128)S(1)} %constant_dynamic-update-slice_fusion), channel_id=1, source_target_pairs={{0,8},{8,0},{16,24},{24,16},{1,9},{9,1},{17,25},{25,17},{2,10},{10... | collective-permute-start | bytes 528392 | tf_op jit(solution)/shard_map/ppermute | solution.py:481
  11.2 4.5 %shard_map.78 = (f32[16,448,128]{2,1,0:T(8,128)S(1)}, f32[112,128]{1,0:T(8,128)S(1)}, f32[112,128]{1,0:T(8,128)S(1)}, bf16[5,256,256]{2,1,0:T(8,128)(2,1)S(1)}, ...) custom-call(s32[1,1]{1,0:T(1,128)S(6)} %copy.28.family, ...), custom_call_target="tpu_custom_call" | custom-call | flops 3449999872 | bytes 11100000 | tf_op jit(solution)/shard_map/pallas_call | solution.py:455
  15.8 2.0 %shard_map.79 = (f32[24,64,128]{2,1,0:T(8,128)S(1)}, f32[64,256]{1,0:T(8,128)S(1)}, f32[16,64,128]{2,1,0:T(8,128)S(1)}) custom-call(f32[16,64,128]{2,1,0:T(8,128)S(1)} %get-tuple-element.118.rows_ref, f32[344,128]{1,0:T(8,128)S(1)} %collective-permute-done.2.p1, f32[344,128]{1,0:T(8,128)S(1)} %collective-permute-done.3.p2, ...), custom_call_target="tpu_custom_call" | custom-call | flops 2300000000 | bytes 7400000 | tf_op jit(solution)/shard_map/pallas_call | solution.py:455
  17.8 3.5 %shard_map.80 = (f32[112,128]{1,0:T(8,128)S(1)}, f32[176,128]{1,0:T(8,128)S(1)}, f32[8,64,128]{2,1,0:T(8,128)S(1)}, f32[8,64,128]{2,1,0:T(8,128)S(1)}, f32[64,12...) custom-call(f32[16,448,128]{2,1,0:T(8,128)S(1)} %get-tuple-element.132.obs_ref, f32[16,128]{1,0:T(8,128)S(1)} %copy-done.4, ...), custom_call_target="tpu_custom_call" | custom-call | flops 5750000128 | bytes 18500000 | tf_op jit(solution)/shard_map/pallas_call | solution.py:455
  22.3 4.1 %collective-permute-start.9 = (f32[8,64,128]{2,1,0:T(8,128)S(1)}, f32[8,64,128]{2,1,0:T(8,128)S(1)}, u32[]{:S(2)}, u32[]{:S(2)}) collective-permute-start(f32[8,64,128]{2,1,0:T(8,128)S(1)} %get-tuple-element.160), channel_id=1, source_target_pairs={{0,8},{8,0},{16,24},{24,16},{1,9},{9,1},{17,25},{25,17},{2,10},{10... | collective-permute-start | bytes 786440 | tf_op jit(solution)/shard_map/ppermute | solution.py:481
  28.6 4.0 %shard_map.81 = (bf16[3,5,256,256]{3,2,1,0:T(8,128)(2,1)S(1)}, bf16[3,5,256,256]{3,2,1,0:T(8,128)(2,1)S(1)}, bf16[768,512]{1,0:T(8,128)(2,1)S(1)}, bf16[768,512]{1,0:T(8,128)(2,1)S(1)}) custom-call(f32[24,128]{1,0:T(8,128)S(1)} %get-tuple-element.247.marks_up, f32[24,128]{1,0:T(8,128)S(1)} %pad_maximum_fusion.9.marks, ...), custom_call_target="tpu_custom_call" | custom-call | flops 3449999872 | bytes 11100000 | tf_op jit(solution)/shard_map/pallas_call | solution.py:455
  35.7 2.5 %collective-permute-start.11 = (f32[112,128]{1,0:T(8,128)S(1)}, f32[112,128]{1,0:T(8,128)S(1)}, u32[]{:S(2)}, u32[]{:S(2)}) collective-permute-start(f32[112,128]{1,0:T(8,128)S(1)} %add.76), channel_id=1, source_target_pairs={{0,16},{8,24},{16,0},{24,8},{1,17},{9,25},{17,1},{25,9},{2,18},{10... | collective-permute-start | bytes 172040 | tf_op jit(solution)/shard_map/ppermute | solution.py:496
  38.2 2.7 %collective-permute-start.8 = (f32[176,128]{1,0:T(8,128)S(1)}, f32[176,128]{1,0:T(8,128)S(1)}, u32[]{:S(2)}, u32[]{:S(2)}) collective-permute-start(f32[176,128]{1,0:T(8,128)S(1)} %get-tuple-element.260), channel_id=1, source_target_pairs={{0,24},{8,16},{16,8},{24,0},{1,25},{9,17},{17,9},{25,1},{2,26},{10... | collective-permute-start | bytes 270344 | tf_op jit(solution)/shard_map/ppermute | solution.py:496
  45.0 2.6 %shard_map.84 = (f32[24,64,128]{2,1,0:T(8,128)S(1)}, f32[64,256]{1,0:T(8,128)S(1)}, f32[16,64,128]{2,1,0:T(8,128)S(1)}) custom-call(f32[24,64,128]{2,1,0:T(8,128)S(1)} %get-tuple-element.166.ext_ref, f32[64,256]{1,0:T(8,128)S(1)} %get-tuple-element.167.side_ref, f32[12,64,256]{2,1,0:T(8,128)S(1)} %get-tuple-element.168.acc, ...), custom_call_target="tpu_custom_call" | custom-call | flops 2875000064 | bytes 9250000 | tf_op jit(solution)/shard_map/pallas_call | solution.py:455
  47.7 3.4 %collective-permute-start.12 = (f32[112,128]{1,0:T(8,128)S(1)}, f32[112,128]{1,0:T(8,128)S(1)}, u32[]{:S(2)}, u32[]{:S(2)}) collective-permute-start(f32[112,128]{1,0:T(8,128)S(1)} %subtract_maximum_fusion.2.mine), channel_id=1, source_target_pairs={{0,1},{1,0},{2,3},{3,2},{4,5},{5,4},{6,7},{7,6},{8,9},{9,8},{10,11... | collective-permute-start | bytes 172040 | tf_op jit(solution)/shard_map/ppermute | solution.py:471
  52.0 3.5 %shard_map.85 = (f32[112,128]{1,0:T(8,128)S(1)}, f32[176,128]{1,0:T(8,128)S(1)}, f32[8,64,128]{2,1,0:T(8,128)S(1)}, f32[8,64,128]{2,1,0:T(8,128)S(1)}, f32[64,12...) custom-call(f32[16,448,128]{2,1,0:T(8,128)S(1)} %get-tuple-element.132.obs_ref, f32[16,128]{1,0:T(8,128)S(1)} %copy-done.4, ...), custom_call_target="tpu_custom_call" | custom-call | flops 5750000128 | bytes 18500000 | tf_op jit(solution)/shard_map/pallas_call | solution.py:455
  60.0 2.0 %collective-permute-done.14 = f32[176,128]{1,0:T(8,128)S(1)} collective-permute-done((f32[176,128]{1,0:T(8,128)S(1)}, f32[176,128]{1,0:T(8,128)S(1)}, u32[]{:S(2)}, u32[]{:S(2)}) %collective-permute-start.14) | collective-permute-done | bytes 90144 | tf_op jit(solution)/shard_map/ppermute | solution.py:476
  62.9 2.2 %collective-permute-done.15 = f32[112,128]{1,0:T(8,128)S(1)} collective-permute-done((f32[112,128]{1,0:T(8,128)S(1)}, f32[112,128]{1,0:T(8,128)S(1)}, u32[]{:S(2)}, u32[]{:S(2)}) %collective-permute-start.15) | collective-permute-done | bytes 57376 | tf_op jit(solution)/shard_map/ppermute | solution.py:491
  69.5 3.1 %collective-permute-done.17 = f32[176,128]{1,0:T(8,128)S(1)} collective-permute-done((f32[176,128]{1,0:T(8,128)S(1)}, f32[176,128]{1,0:T(8,128)S(1)}, u32[]{:S(2)}, u32[]{:S(2)}) %collective-permute-start.17) | collective-permute-done | bytes 90144 | tf_op jit(solution)/shard_map/ppermute | solution.py:496
  72.6 2.6 %shard_map.88 = (f32[24,64,128]{2,1,0:T(8,128)S(1)}, f32[64,256]{1,0:T(8,128)S(1)}, f32[16,64,128]{2,1,0:T(8,128)S(1)}) custom-call(f32[24,64,128]{2,1,0:T(8,128)S(1)} %get-tuple-element.195.ext_ref, f32[64,256]{1,0:T(8,128)S(1)} %get-tuple-element.196.side_ref, f32[12,64,256]{2,1,0:T(8,128)S(1)} %get-tuple-element.197.acc, ...), custom_call_target="tpu_custom_call" | custom-call | flops 2875000064 | bytes 9250000 | tf_op jit(solution)/shard_map/pallas_call | solution.py:455
  75.3 3.7 %collective-permute-start.21 = (f32[112,128]{1,0:T(8,128)S(1)}, f32[112,128]{1,0:T(8,128)S(1)}, u32[]{:S(2)}, u32[]{:S(2)}) collective-permute-start(f32[112,128]{1,0:T(8,128)S(1)} %subtract_maximum_fusion.1.mine), channel_id=1, source_target_pairs={{0,1},{1,0},{2,3},{3,2},{4,5},{5,4},{6,7},{7,6},{8,9},{9,8},{10,11... | collective-permute-start | bytes 172040 | tf_op jit(solution)/shard_map/ppermute | solution.py:471
  79.8 3.5 %shard_map.89 = (f32[112,128]{1,0:T(8,128)S(1)}, f32[176,128]{1,0:T(8,128)S(1)}, f32[8,64,128]{2,1,0:T(8,128)S(1)}, f32[8,64,128]{2,1,0:T(8,128)S(1)}, f32[64,12...) custom-call(f32[16,448,128]{2,1,0:T(8,128)S(1)} %get-tuple-element.132.obs_ref, f32[16,128]{1,0:T(8,128)S(1)} %copy-done.4, ...), custom_call_target="tpu_custom_call" | custom-call | flops 5750000128 | bytes 18500000 | tf_op jit(solution)/shard_map/pallas_call | solution.py:455
  87.8 2.1 %collective-permute-done.23 = f32[176,128]{1,0:T(8,128)S(1)} collective-permute-done((f32[176,128]{1,0:T(8,128)S(1)}, f32[176,128]{1,0:T(8,128)S(1)}, u32[]{:S(2)}, u32[]{:S(2)}) %collective-permute-start.23) | collective-permute-done | bytes 90144 | tf_op jit(solution)/shard_map/ppermute | solution.py:476
  90.7 2.3 %collective-permute-done.24 = f32[112,128]{1,0:T(8,128)S(1)} collective-permute-done((f32[112,128]{1,0:T(8,128)S(1)}, f32[112,128]{1,0:T(8,128)S(1)}, u32[]{:S(2)}, u32[]{:S(2)}) %collective-permute-start.24) | collective-permute-done | bytes 57376 | tf_op jit(solution)/shard_map/ppermute | solution.py:491
  97.4 3.1 %collective-permute-done.26 = f32[176,128]{1,0:T(8,128)S(1)} collective-permute-done((f32[176,128]{1,0:T(8,128)S(1)}, f32[176,128]{1,0:T(8,128)S(1)}, u32[]{:S(2)}, u32[]{:S(2)}) %collective-permute-start.26) | collective-permute-done | bytes 90144 | tf_op jit(solution)/shard_map/ppermute | solution.py:496
  100.5 2.1 %shard_map.92 = f32[64,16,128]{2,1,0:T(8,128)} custom-call(f32[24,64,128]{2,1,0:T(8,128)S(1)} %get-tuple-element.222.ext_ref, f32[64,256]{1,0:T(8,128)S(1)} %get-tuple-element.223.side_ref, f32[12,64,256]{2,1,0:T(8,128)S(1)} %get-tuple-element.224.acc, f32[64,256]{1,0:T(8,128)S(1)} %get-tuple-element.225.near_ref, f32[64,128]{1,0:T(8,128)S(1)} %get-tuple-element.230.left, ...), custom_call_target="tpu_custom_call" | custom-call | flops 1724999936 | bytes 5550000 | tf_op jit(solution)/shard_map/pallas_call | solution.py:455
  102.7 3.9 %collective-permute-start.30 = (f32[112,128]{1,0:T(8,128)S(1)}, f32[112,128]{1,0:T(8,128)S(1)}, u32[]{:S(2)}, u32[]{:S(2)}) collective-permute-start(f32[112,128]{1,0:T(8,128)S(1)} %subtract_maximum_fusion.mine), channel_id=1, source_target_pairs={{0,1},{1,0},{2,3},{3,2},{4,5},{5,4},{6,7},{7,6},{8,9},{9,8},{10,11... | collective-permute-start | bytes 172040 | tf_op jit(solution)/shard_map/ppermute | solution.py:471
  (110 shorter events, 36.9 us)
Async XLA Ops:
  3.9 4.3 %collective-permute-start.1 = (f32[72,128]{1,0:T(8,128)S(1)}, f32[72,128]{1,0:T(8,128)S(1)}, u32[]{:S(2)}, u32[]{:S(2)}) collective-permute-start(f32[72,128]{1,0:T(8,128)S(1)} %get-tuple-element.121), channel_id=1, source_target_pairs={{0,7},{1,2},{2,1},{3,4},{4,3},{5,6},{6,5},{7,0},{8,15},{9,10},{10,... | collective-permute-start | bytes 110600 | tf_op jit(solution)/shard_map/ppermute | solution.py:476
  8.2 7.5 %collective-permute-start.2 = (f32[344,128]{1,0:T(8,128)S(1)}, f32[344,128]{1,0:T(8,128)S(1)}, u32[]{:S(2)}, u32[]{:S(2)}) collective-permute-start(f32[344,128]{1,0:T(8,128)S(1)} %constant_dynamic-update-slice_fusion), channel_id=1, source_target_pairs={{0,8},{8,0},{16,24},{24,16},{1,9},{9,1},{17,25},{25,17},{2,10},{10... | collective-permute-start | bytes 528392 | tf_op jit(solution)/shard_map/ppermute | solution.py:481
  10.5 5.2 %collective-permute-start.3 = (f32[344,128]{1,0:T(8,128)S(1)}, f32[344,128]{1,0:T(8,128)S(1)}, u32[]{:S(2)}, u32[]{:S(2)}) collective-permute-start(f32[344,128]{1,0:T(8,128)S(1)} %get-tuple-element.237), channel_id=1, source_target_pairs={{0,0},{8,16},{16,8},{24,24},{1,1},{9,17},{17,9},{25,25},{2,2},{10,... | collective-permute-start | bytes 528392 | tf_op jit(solution)/shard_map/ppermute | solution.py:486
  21.3 6.0 %collective-permute-start.4 = (f32[176,128]{1,0:T(8,128)S(1)}, f32[176,128]{1,0:T(8,128)S(1)}, u32[]{:S(2)}, u32[]{:S(2)}) collective-permute-start(f32[176,128]{1,0:T(8,128)S(1)} %get-tuple-element.145), channel_id=1, source_target_pairs={{0,1},{1,0},{2,3},{3,2},{4,5},{5,4},{6,7},{7,6},{8,9},{9,8},{10,11... | collective-permute-start | bytes 270344 | tf_op jit(solution)/shard_map/ppermute | solution.py:471
  22.3 18.7 %collective-permute-start.9 = (f32[8,64,128]{2,1,0:T(8,128)S(1)}, f32[8,64,128]{2,1,0:T(8,128)S(1)}, u32[]{:S(2)}, u32[]{:S(2)}) collective-permute-start(f32[8,64,128]{2,1,0:T(8,128)S(1)} %get-tuple-element.160), channel_id=1, source_target_pairs={{0,8},{8,0},{16,24},{24,16},{1,9},{9,1},{17,25},{25,17},{2,10},{10... | collective-permute-start | bytes 786440 | tf_op jit(solution)/shard_map/ppermute | solution.py:481
  26.4 14.6 %collective-permute-start.10 = (f32[8,64,128]{2,1,0:T(8,128)S(1)}, f32[8,64,128]{2,1,0:T(8,128)S(1)}, u32[]{:S(2)}, u32[]{:S(2)}) collective-permute-start(f32[8,64,128]{2,1,0:T(8,128)S(1)} %get-tuple-element.161), channel_id=1, source_target_pairs={{0,0},{8,16},{16,8},{24,24},{1,1},{9,17},{17,9},{25,25},{2,2},{10,... | collective-permute-start | bytes 786440 | tf_op jit(solution)/shard_map/ppermute | solution.py:486
  27.3 5.3 %collective-permute-start.5 = (f32[176,128]{1,0:T(8,128)S(1)}, f32[176,128]{1,0:T(8,128)S(1)}, u32[]{:S(2)}, u32[]{:S(2)}) collective-permute-start(f32[176,128]{1,0:T(8,128)S(1)} %pad_maximum_fusion.6), channel_id=1, source_target_pairs={{0,7},{1,2},{2,1},{3,4},{4,3},{5,6},{6,5},{7,0},{8,15},{9,10},{10,... | collective-permute-start | bytes 270344 | tf_op jit(solution)/shard_map/ppermute | solution.py:476
  35.7 11.9 %collective-permute-start.11 = (f32[112,128]{1,0:T(8,128)S(1)}, f32[112,128]{1,0:T(8,128)S(1)}, u32[]{:S(2)}, u32[]{:S(2)}) collective-permute-start(f32[112,128]{1,0:T(8,128)S(1)} %add.76), channel_id=1, source_target_pairs={{0,16},{8,24},{16,0},{24,8},{1,17},{9,25},{17,1},{25,9},{2,18},{10... | collective-permute-start | bytes 172040 | tf_op jit(solution)/shard_map/ppermute | solution.py:496
  38.2 5.3 %collective-permute-start.8 = (f32[176,128]{1,0:T(8,128)S(1)}, f32[176,128]{1,0:T(8,128)S(1)}, u32[]{:S(2)}, u32[]{:S(2)}) collective-permute-start(f32[176,128]{1,0:T(8,128)S(1)} %get-tuple-element.260), channel_id=1, source_target_pairs={{0,24},{8,16},{16,8},{24,0},{1,25},{9,17},{17,9},{25,1},{2,26},{10... | collective-permute-start | bytes 270344 | tf_op jit(solution)/shard_map/ppermute | solution.py:496
  47.7 4.3 %collective-permute-start.12 = (f32[112,128]{1,0:T(8,128)S(1)}, f32[112,128]{1,0:T(8,128)S(1)}, u32[]{:S(2)}, u32[]{:S(2)}) collective-permute-start(f32[112,128]{1,0:T(8,128)S(1)} %subtract_maximum_fusion.2.mine), channel_id=1, source_target_pairs={{0,1},{1,0},{2,3},{3,2},{4,5},{5,4},{6,7},{7,6},{8,9},{9,8},{10,11... | collective-permute-start | bytes 172040 | tf_op jit(solution)/shard_map/ppermute | solution.py:471
  55.9 12.2 %collective-permute-start.18 = (f32[8,64,128]{2,1,0:T(8,128)S(1)}, f32[8,64,128]{2,1,0:T(8,128)S(1)}, u32[]{:S(2)}, u32[]{:S(2)}) collective-permute-start(f32[8,64,128]{2,1,0:T(8,128)S(1)} %get-tuple-element.189), channel_id=1, source_target_pairs={{0,8},{8,0},{16,24},{24,16},{1,9},{9,1},{17,25},{25,17},{2,10},{10... | collective-permute-start | bytes 786440 | tf_op jit(solution)/shard_map/ppermute | solution.py:481
  56.9 5.2 %collective-permute-start.14 = (f32[176,128]{1,0:T(8,128)S(1)}, f32[176,128]{1,0:T(8,128)S(1)}, u32[]{:S(2)}, u32[]{:S(2)}) collective-permute-start(f32[176,128]{1,0:T(8,128)S(1)} %pad_maximum_fusion.7), channel_id=1, source_target_pairs={{0,7},{1,2},{2,1},{3,4},{4,3},{5,6},{6,5},{7,0},{8,15},{9,10},{10,... | collective-permute-start | bytes 270344 | tf_op jit(solution)/shard_map/ppermute | solution.py:476
  59.1 9.0 %collective-permute-start.19 = (f32[8,64,128]{2,1,0:T(8,128)S(1)}, f32[8,64,128]{2,1,0:T(8,128)S(1)}, u32[]{:S(2)}, u32[]{:S(2)}) collective-permute-start(f32[8,64,128]{2,1,0:T(8,128)S(1)} %get-tuple-element.190), channel_id=1, source_target_pairs={{0,0},{8,16},{16,8},{24,24},{1,1},{9,17},{17,9},{25,25},{2,2},{10,... | collective-permute-start | bytes 786440 | tf_op jit(solution)/shard_map/ppermute | solution.py:486
  65.1 10.1 %collective-permute-start.20 = (f32[112,128]{1,0:T(8,128)S(1)}, f32[112,128]{1,0:T(8,128)S(1)}, u32[]{:S(2)}, u32[]{:S(2)}) collective-permute-start(f32[112,128]{1,0:T(8,128)S(1)} %add.82), channel_id=1, source_target_pairs={{0,16},{8,24},{16,0},{24,8},{1,17},{9,25},{17,1},{25,9},{2,18},{10... | collective-permute-start | bytes 172040 | tf_op jit(solution)/shard_map/ppermute | solution.py:496
  66.7 6.0 %collective-permute-start.17 = (f32[176,128]{1,0:T(8,128)S(1)}, f32[176,128]{1,0:T(8,128)S(1)}, u32[]{:S(2)}, u32[]{:S(2)}) collective-permute-start(f32[176,128]{1,0:T(8,128)S(1)} %get-tuple-element.258), channel_id=1, source_target_pairs={{0,24},{8,16},{16,8},{24,0},{1,25},{9,17},{17,9},{25,1},{2,26},{10... | collective-permute-start | bytes 270344 | tf_op jit(solution)/shard_map/ppermute | solution.py:496
  68.1 4.5 %collective-permute-start.16 = (f32[176,128]{1,0:T(8,128)S(1)}, f32[176,128]{1,0:T(8,128)S(1)}, u32[]{:S(2)}, u32[]{:S(2)}) collective-permute-start(f32[176,128]{1,0:T(8,128)S(1)} %get-tuple-element.259), channel_id=1, source_target_pairs={{0,8},{8,0},{16,24},{24,16},{1,9},{9,1},{17,25},{25,17},{2,10},{10... | collective-permute-start | bytes 270344 | tf_op jit(solution)/shard_map/ppermute | solution.py:481
  75.3 4.6 %collective-permute-start.21 = (f32[112,128]{1,0:T(8,128)S(1)}, f32[112,128]{1,0:T(8,128)S(1)}, u32[]{:S(2)}, u32[]{:S(2)}) collective-permute-start(f32[112,128]{1,0:T(8,128)S(1)} %subtract_maximum_fusion.1.mine), channel_id=1, source_target_pairs={{0,1},{1,0},{2,3},{3,2},{4,5},{5,4},{6,7},{7,6},{8,9},{9,8},{10,11... | collective-permute-start | bytes 172040 | tf_op jit(solution)/shard_map/ppermute | solution.py:471
  83.8 12.3 %collective-permute-start.27 = (f32[8,64,128]{2,1,0:T(8,128)S(1)}, f32[8,64,128]{2,1,0:T(8,128)S(1)}, u32[]{:S(2)}, u32[]{:S(2)}) collective-permute-start(f32[8,64,128]{2,1,0:T(8,128)S(1)} %get-tuple-element.216), channel_id=1, source_target_pairs={{0,8},{8,0},{16,24},{24,16},{1,9},{9,1},{17,25},{25,17},{2,10},{10... | collective-permute-start | bytes 786440 | tf_op jit(solution)/shard_map/ppermute | solution.py:481
  84.7 5.2 %collective-permute-start.23 = (f32[176,128]{1,0:T(8,128)S(1)}, f32[176,128]{1,0:T(8,128)S(1)}, u32[]{:S(2)}, u32[]{:S(2)}) collective-permute-start(f32[176,128]{1,0:T(8,128)S(1)} %pad_maximum_fusion.8), channel_id=1, source_target_pairs={{0,7},{1,2},{2,1},{3,4},{4,3},{5,6},{6,5},{7,0},{8,15},{9,10},{10,... | collective-permute-start | bytes 270344 | tf_op jit(solution)/shard_map/ppermute | solution.py:476
  87.1 9.0 %collective-permute-start.28 = (f32[8,64,128]{2,1,0:T(8,128)S(1)}, f32[8,64,128]{2,1,0:T(8,128)S(1)}, u32[]{:S(2)}, u32[]{:S(2)}) collective-permute-start(f32[8,64,128]{2,1,0:T(8,128)S(1)} %get-tuple-element.217), channel_id=1, source_target_pairs={{0,0},{8,16},{16,8},{24,24},{1,1},{9,17},{17,9},{25,25},{2,2},{10,... | collective-permute-start | bytes 786440 | tf_op jit(solution)/shard_map/ppermute | solution.py:486
  93.1 9.6 %collective-permute-start.29 = (f32[112,128]{1,0:T(8,128)S(1)}, f32[112,128]{1,0:T(8,128)S(1)}, u32[]{:S(2)}, u32[]{:S(2)}) collective-permute-start(f32[112,128]{1,0:T(8,128)S(1)} %add.88), channel_id=1, source_target_pairs={{0,16},{8,24},{16,0},{24,8},{1,17},{9,25},{17,1},{25,9},{2,18},{10... | collective-permute-start | bytes 172040 | tf_op jit(solution)/shard_map/ppermute | solution.py:496
  94.6 6.0 %collective-permute-start.26 = (f32[176,128]{1,0:T(8,128)S(1)}, f32[176,128]{1,0:T(8,128)S(1)}, u32[]{:S(2)}, u32[]{:S(2)}) collective-permute-start(f32[176,128]{1,0:T(8,128)S(1)} %get-tuple-element.256), channel_id=1, source_target_pairs={{0,24},{8,16},{16,8},{24,0},{1,25},{9,17},{17,9},{25,1},{2,26},{10... | collective-permute-start | bytes 270344 | tf_op jit(solution)/shard_map/ppermute | solution.py:496
  96.1 4.5 %collective-permute-start.25 = (f32[176,128]{1,0:T(8,128)S(1)}, f32[176,128]{1,0:T(8,128)S(1)}, u32[]{:S(2)}, u32[]{:S(2)}) collective-permute-start(f32[176,128]{1,0:T(8,128)S(1)} %get-tuple-element.257), channel_id=1, source_target_pairs={{0,8},{8,0},{16,24},{24,16},{1,9},{9,1},{17,25},{25,17},{2,10},{10... | collective-permute-start | bytes 270344 | tf_op jit(solution)/shard_map/ppermute | solution.py:481
  102.7 4.8 %collective-permute-start.30 = (f32[112,128]{1,0:T(8,128)S(1)}, f32[112,128]{1,0:T(8,128)S(1)}, u32[]{:S(2)}, u32[]{:S(2)}) collective-permute-start(f32[112,128]{1,0:T(8,128)S(1)} %subtract_maximum_fusion.mine), channel_id=1, source_target_pairs={{0,1},{1,0},{2,3},{3,2},{4,5},{5,4},{6,7},{7,6},{8,9},{9,8},{10,11... | collective-permute-start | bytes 172040 | tf_op jit(solution)/shard_map/ppermute | solution.py:471
  (12 other events, 49.5 us)

commit v4 on v3

--- a/solution.py
+++ b/solution.py
@@ -27,6 +27,12 @@
 
 def mm(a, b):
     return jnp.dot(a, b, preferred_element_type=F32)
+
+
+def mm_split(high, low, w_high, w_low):
+    rows = high.shape[0]
+    both = mm(jnp.concatenate([high, low], axis=0), w_high)
+    return both[:rows] + both[rows:] + mm(high, w_low)
 
 
 def mm_nt(a, b):
@@ -246,14 +252,14 @@
     for d in range(RADIUS + 1):
         high = a2_high[d : d + pairs].reshape(pairs * channels, double)
         low = a2_low[d : d + pairs].reshape(pairs * channels, double)
-        part = mm(high, w_high[d]) + mm(low, w_high[d]) + mm(high, w_low[d])
+        part = mm_split(high, low, w_high[d], w_low[d])
         part = part.reshape(pairs, channels, double)
         if d == 0:
             acc[...] = part
         else:
             acc[...] += part
     side_high, side_low = split(side)
-    rim = mm(side_high, s_high[...]) + mm(side_low, s_high[...]) + mm(side_high, s_low[...])
+    rim = mm_split(side_high, side_low, s_high[...], s_low[...])
     for i in range(2 * pairs):
         row = acc[i // 2, :, i % 2 * width : i % 2 * width + width]
         b_ref[i] = add_rim(row, rim, i)
@@ -329,10 +335,10 @@
     core_ref[2 * quarter // 2 :] = jnp.where(col_odd, low, high)
     cross_ref[...] = jnp.where(col_odd, high, low)
     row_odd = place[ROW_ODD] == 1
-    half = height // 2
-    for i in range(half):
-        main1[i] = jnp.where(row_odd, rows[i], rows[half + i])
-        main2[i] = jnp.where(row_odd, rows[half + i], rows[i])
+    halo = main1.shape[0]
+    for i in range(halo):
+        main1[i] = jnp.where(row_odd, rows[i], rows[height - halo + i])
+        main2[i] = jnp.where(row_odd, rows[height - halo + i], rows[i])
     g = total[...] * scale
     g0 = jnp.concatenate([g[:quarter], g[quarter : 2 * quarter]], axis=1)
     g1 = jnp.concatenate([g[2 * quarter : 3 * quarter], g[3 * quarter :]], axis=1)
@@ -354,7 +360,7 @@
             continue
         high = g_high[begin - first : end - first].reshape((end - begin) * channels, double)
         low = g_low[begin - first : end - first].reshape((end - begin) * channels, double)
-        part = mm(high, w_high[band, d]) + mm(low, w_high[band, d]) + mm(high, w_low[band, d])
+        part = mm_split(high, low, w_high[band, d], w_low[band, d])
         acc[begin - d : end - d] += part.reshape(end - begin, channels, double)
 
 
@@ -380,19 +386,21 @@
     odd = place[ROW_ODD] == 1
     lane = lanes((channels, width))
     near = [near_in[:, :width], near_in[:, width:]]
-    for k in range(2 * EDGE):
-        q = k if k < EDGE else k + height
-        if k < EDGE:
+    halo = p1.shape[0]
+    for k in range(2 * halo):
+        if k < halo:
+            q = EDGE - halo + k
             row = jnp.where(place[UP] == 1, jnp.where(odd, p1[k], p2[k]), 0.0)
         else:
-            row = jnp.where(place[DOWN] == 1, jnp.where(odd, p2[k - EDGE], p1[k - EDGE]), 0.0)
+            q = EDGE + height + k - halo
+            row = jnp.where(place[DOWN] == 1, jnp.where(odd, p2[k - halo], p1[k - halo]), 0.0)
         put_pair(g_high, g_low, k, row)
         moved = pltpu.roll(row, (RADIUS + q * EDGE) % width, 1)
         near[q // height] = jnp.where(lane // EDGE == q % height, moved, near[q // height])
     near_ref[...] = jnp.concatenate(near, axis=1)
-    n = EDGE // 2
-    adjoint_into(acc, g_high.at[:n], g_low.at[:n], 0, wa_high, wa_low, 0)
-    adjoint_into(acc, g_high.at[n:], g_low.at[n:], n + height // 2, wa_high, wa_low, 2)
+    n = halo // 2
+    adjoint_into(acc, g_high.at[:n], g_low.at[:n], EDGE // 2 - n, wa_high, wa_low, 0)
+    adjoint_into(acc, g_high.at[n:], g_low.at[n:], (EDGE + height) // 2, wa_high, wa_low, 2)
 
 
 def maps_kernel(
@@ -408,9 +416,9 @@
     ext_rows = height + EDGE
     side_in = jnp.concatenate([left[...], right[...], above[...], below[...], near_ref[...]], axis=1)
     side_high, side_low = split(side_in)
-    side_mm = mm(side_high, sa_high[...]) + mm(side_low, sa_high[...]) + mm(side_high, sa_low[...])
-    half = side_mm.shape[1] // 2
-    rim = side_mm[:, half:]
+    half = sa_high.shape[1] // 2
+    far = sa_high.shape[0] - 2 * width
+    rim = mm_split(side_high[:, :far], side_low[:, :far], sa_high[:far, half:], sa_low[:far, half:])
     for a in range(ext_rows):
         if last and not RADIUS <= a < RADIUS + height:
             continue
@@ -427,7 +435,8 @@
         put_pair(a2_high, a2_low, a, row)
     if last:
         return
-    side = jnp.maximum(side_ref[...] - 0.5 * side_mm[:, :half], 0.0)
+    side_grad = mm_split(side_high, side_low, sa_high[:, :half], sa_low[:, :half])
+    side = jnp.maximum(side_ref[...] - 0.5 * side_grad, 0.0)
     where = lanes(side.shape)
     a, c = where // EDGE, where % EDGE
     outside = (
@@ -605,14 +614,15 @@
 
     for step in range(ITERS):
         last = step == ITERS - 1
+        halo = RADIUS if last else EDGE
         g_mine, to_core, main1, main2, e_cross, g_rows = call(
             functools.partial(spectral_kernel, scale=1.0 / channels),
             5,
             [
                 ((quarter, 2 * channels), F32),
                 ((quarter + channels, width), F32),
-                ((height // 2,) + tile, F32),
-                ((height // 2,) + tile, F32),
+                ((halo,) + tile, F32),
+                ((halo,) + tile, F32),
                 (tile, F32),
                 ((height,) + tile, F32),
             ],
@@ -643,7 +653,7 @@
             halo_maps_kernel,
             1.5,
             [acc_shape, near_shape],
-            [((EDGE, channels, 2 * width), BF16)] * 2,
+            [((halo, channels, 2 * width), BF16)] * 2,
             [VMEM] * 4 + [SMEM] + [VMEM] * 2,
             own, near, p1, p2, place, wa[0], wa[1],
             aliases={0: 0, 1: 1},
@@ -684,7 +694,6 @@
                 [VMEM] * 8 + [SMEM] + [VMEM] * 6,
                 *gathered, *wf,
             )
-        share, *made = lax.optimization_barrier((share, *made))
         mine = jnp.maximum(mine - rate * share, 0.0)
         other = core_swap(mine)
         if last:

time: 109 us -> 107 us (0.982)
  waiting for transfers between devices: 23.4 us -> 19 us
  starting transfers between devices: 43.4 us -> 46 us
    ppermute x7, starting transfers between devices: 7.31 us -> 17 us  [pair_one(): return lax.ppermute(x, 'rows', [(i, i ^ 1) for i in range(count)])]
    ppermute x6, starting transfers between devices: 11.2 us -> 7.09 us  [row_swap(): return lax.ppermute(x, 'rows', [(i, i ^ mask) for i in range(count)])]
    ppermute x4, waiting for transfers between devices: 5.74 us -> 2.02 us  [cross_swap(): lax.ppermute(x, 'cols', [(i, (i + 1 if i % 2 else i - 1) % count) for i i...]
    ppermute x7, starting transfers between devices: 13 us -> 9.65 us  [core_swap(): return lax.ppermute(x, 'cols', [(i, i ^ 1) for i in range(count)])]
    ppermute x7, waiting for transfers between devices: 1.52 us -> 0.02 us  [pair_one(): return lax.ppermute(x, 'rows', [(i, i ^ 1) for i in range(count)])]
    ppermute x6, waiting for transfers between devices: 7.42 us -> 8.54 us  [row_swap(): return lax.ppermute(x, 'rows', [(i, i ^ mask) for i in range(count)])]
    ppermute x7, waiting for transfers between devices: 3.64 us -> 2.55 us  [core_swap(): return lax.ppermute(x, 'cols', [(i, i ^ 1) for i in range(count)])]
  transfers between devices with their start and end apart: 31 -> 31, of which waited for: 15 -> 10; matrix products, arithmetic and copies ran while one was open for 0% -> 0% of each run, Pallas kernels for 22% -> 21%
where the time goes in v4:
time: 107 us; the launch traced here: 106 us
  starting transfers between devices  46 us (43%)
  Pallas kernels  37.7 us (35%)
  waiting for transfers between devices  19 us (18%)
  between operations  2.01 us (2%)
  local copies, waits for them, and re-layouts  1.28 us (1%)
    pallas_call x17, Pallas kernels, call(): pl.pallas_call(kernel, out_shape=[jax.ShapeDtypeStruct(s, d) for s, d in...  37.7 us
    ppermute x7, starting transfers between devices, pair_one(): return lax.ppermute(x, 'rows', [(i, i ^ 1) for i in range(count)])  17 us
    ppermute x7, starting transfers between devices, core_swap(): return lax.ppermute(x, 'cols', [(i, i ^ 1) for i in range(count)])  9.65 us
    ppermute x6, waiting for transfers between devices, row_swap(): return lax.ppermute(x, 'rows', [(i, i ^ mask) for i in range(count)])  8.54 us
    ppermute x6, starting transfers between devices, row_swap(): return lax.ppermute(x, 'rows', [(i, i ^ mask) for i in range(count)])  7.09 us
    ppermute x4, starting transfers between devices, cross_swap(): lax.ppermute(x, 'cols', [(i, (i + 1 if i % 2 else i - 1) % count) for i i...  6.63 us
    ppermute x3, waiting for transfers between devices, col_swap(): lax.ppermute(x, 'cols', [(i, (((i + 1) % count ^ mask) - 1) % count) for...  5.87 us
    ppermute x4, starting transfers between devices, pair_two(): lax.ppermute(x, 'rows', [(i, min(max(i + 1 if i % 2 else i - 1, 0), count...  3.07 us
  transfers between devices with their start and end apart: 31, of which 10 were waited for; matrix products, arithmetic and copies ran while one was open for 0% of the time, Pallas kernels for 21%

profile of v4, /device:TPU:1, one launch (start us, length us, event | category | flops | bytes accessed | tf_op | source)
XLA Modules:
  0.0 106.5 jit_solution(8028110571407508429)
XLA Ops:
  3.9 2.6 %collective-permute-start.1 = (f32[72,128]{1,0:T(8,128)S(1)}, f32[72,128]{1,0:T(8,128)S(1)}, u32[]{:S(2)}, u32[]{:S(2)}) collective-permute-start(f32[72,128]{1,0:T(8,128)S(1)} %get-tuple-element.111), channel_id=1, source_target_pairs={{0,7},{1,2},{2,1},{3,4},{4,3},{5,6},{6,5},{7,0},{8,15},{9,10},{10,... | collective-permute-start | bytes 110600 | tf_op jit(solution)/shard_map/ppermute | solution.py:485
  8.2 2.3 %collective-permute-start.2 = (f32[344,128]{1,0:T(8,128)S(1)}, f32[344,128]{1,0:T(8,128)S(1)}, u32[]{:S(2)}, u32[]{:S(2)}) collective-permute-start(f32[344,128]{1,0:T(8,128)S(1)} %constant_dynamic-update-slice_fusion), channel_id=1, source_target_pairs={{0,8},{8,0},{16,24},{24,16},{1,9},{9,1},{17,25},{25,17},{2,10},{10... | collective-permute-start | bytes 528392 | tf_op jit(solution)/shard_map/ppermute | solution.py:490
  11.2 4.5 %shard_map.78 = (f32[16,448,128]{2,1,0:T(8,128)S(1)}, f32[112,128]{1,0:T(8,128)S(1)}, f32[112,128]{1,0:T(8,128)S(1)}, bf16[5,256,256]{2,1,0:T(8,128)(2,1)S(1)}, ...) custom-call(s32[1,1]{1,0:T(1,128)S(6)} %copy.28.family, ...), custom_call_target="tpu_custom_call" | custom-call | flops 3449999872 | bytes 11100000 | tf_op jit(solution)/shard_map/pallas_call | solution.py:464
  15.8 2.0 %shard_map.79 = (f32[24,64,128]{2,1,0:T(8,128)S(1)}, f32[64,256]{1,0:T(8,128)S(1)}, f32[16,64,128]{2,1,0:T(8,128)S(1)}) custom-call(f32[16,64,128]{2,1,0:T(8,128)S(1)} %get-tuple-element.107.rows_ref, f32[344,128]{1,0:T(8,128)S(1)} %collective-permute-done.2.p1, f32[344,128]{1,0:T(8,128)S(1)} %collective-permute-done.3.p2, ...), custom_call_target="tpu_custom_call" | custom-call | flops 2300000000 | bytes 7400000 | tf_op jit(solution)/shard_map/pallas_call | solution.py:464
  17.8 3.5 %shard_map.80 = (f32[112,128]{1,0:T(8,128)S(1)}, f32[176,128]{1,0:T(8,128)S(1)}, f32[8,64,128]{2,1,0:T(8,128)S(1)}, f32[8,64,128]{2,1,0:T(8,128)S(1)}, f32[64,12...) custom-call(f32[16,448,128]{2,1,0:T(8,128)S(1)} %get-tuple-element.132.obs_ref, f32[16,128]{1,0:T(8,128)S(1)} %copy-done.4, ...), custom_call_target="tpu_custom_call" | custom-call | flops 5750000128 | bytes 18500000 | tf_op jit(solution)/shard_map/pallas_call | solution.py:464
  23.2 6.5 %collective-permute-start.9 = (f32[8,64,128]{2,1,0:T(8,128)S(1)}, f32[8,64,128]{2,1,0:T(8,128)S(1)}, u32[]{:S(2)}, u32[]{:S(2)}) collective-permute-start(f32[8,64,128]{2,1,0:T(8,128)S(1)} %get-tuple-element.152), channel_id=1, source_target_pairs={{0,8},{8,0},{16,24},{24,16},{1,9},{9,1},{17,25},{25,17},{2,10},{10... | collective-permute-start | bytes 786440 | tf_op jit(solution)/shard_map/ppermute | solution.py:490
  29.7 2.2 %collective-permute-start.5 = (f32[176,128]{1,0:T(8,128)S(1)}, f32[176,128]{1,0:T(8,128)S(1)}, u32[]{:S(2)}, u32[]{:S(2)}) collective-permute-start(f32[176,128]{1,0:T(8,128)S(1)} %pad_maximum_fusion.6), channel_id=1, source_target_pairs={{0,7},{1,2},{2,1},{3,4},{4,3},{5,6},{6,5},{7,0},{8,15},{9,10},{10,... | collective-permute-start | bytes 270344 | tf_op jit(solution)/shard_map/ppermute | solution.py:485
  31.9 4.0 %shard_map.81 = (bf16[3,5,256,256]{3,2,1,0:T(8,128)(2,1)S(1)}, bf16[3,5,256,256]{3,2,1,0:T(8,128)(2,1)S(1)}, bf16[768,512]{1,0:T(8,128)(2,1)S(1)}, bf16[768,512]{1,0:T(8,128)(2,1)S(1)}) custom-call(f32[24,128]{1,0:T(8,128)S(1)} %get-tuple-element.227.marks_up, f32[24,128]{1,0:T(8,128)S(1)} %pad_maximum_fusion.9.marks, ...), custom_call_target="tpu_custom_call" | custom-call | flops 3449999872 | bytes 11100000 | tf_op jit(solution)/shard_map/pallas_call | solution.py:464
  40.1 2.6 %collective-permute-start.8 = (f32[176,128]{1,0:T(8,128)S(1)}, f32[176,128]{1,0:T(8,128)S(1)}, u32[]{:S(2)}, u32[]{:S(2)}) collective-permute-start(f32[176,128]{1,0:T(8,128)S(1)} %get-tuple-element.240), channel_id=1, source_target_pairs={{0,24},{8,16},{16,8},{24,0},{1,25},{9,17},{17,9},{25,1},{2,26},{10... | collective-permute-start | bytes 270344 | tf_op jit(solution)/shard_map/ppermute | solution.py:505
  44.1 2.2 %collective-permute-done.8 = f32[176,128]{1,0:T(8,128)S(1)} collective-permute-done((f32[176,128]{1,0:T(8,128)S(1)}, f32[176,128]{1,0:T(8,128)S(1)}, u32[]{:S(2)}, u32[]{:S(2)}) %collective-permute-start.8) | collective-permute-done | bytes 90144 | tf_op jit(solution)/shard_map/ppermute | solution.py:505
  46.4 3.1 %collective-permute-start.12 = (f32[112,128]{1,0:T(8,128)S(1)}, f32[112,128]{1,0:T(8,128)S(1)}, u32[]{:S(2)}, u32[]{:S(2)}) collective-permute-start(f32[112,128]{1,0:T(8,128)S(1)} %subtract_maximum_fusion.2.mine), channel_id=1, source_target_pairs={{0,1},{1,0},{2,3},{3,2},{4,5},{5,4},{6,7},{7,6},{8,9},{9,8},{10,11... | collective-permute-start | bytes 172040 | tf_op jit(solution)/shard_map/ppermute | solution.py:480
  49.4 2.4 %shard_map.84 = (f32[24,64,128]{2,1,0:T(8,128)S(1)}, f32[64,256]{1,0:T(8,128)S(1)}, f32[16,64,128]{2,1,0:T(8,128)S(1)}) custom-call(f32[24,64,128]{2,1,0:T(8,128)S(1)} %get-tuple-element.130.ext_ref, f32[64,256]{1,0:T(8,128)S(1)} %get-tuple-element.131.side_ref, f32[12,64,256]{2,1,0:T(8,128)S(1)} %get-tuple-element.156.acc, ...), custom_call_target="tpu_custom_call" | custom-call | flops 2875000064 | bytes 9250000 | tf_op jit(solution)/shard_map/pallas_call | solution.py:464
  51.8 3.5 %shard_map.85 = (f32[112,128]{1,0:T(8,128)S(1)}, f32[176,128]{1,0:T(8,128)S(1)}, f32[8,64,128]{2,1,0:T(8,128)S(1)}, f32[8,64,128]{2,1,0:T(8,128)S(1)}, f32[64,12...) custom-call(f32[16,448,128]{2,1,0:T(8,128)S(1)} %get-tuple-element.132.obs_ref, f32[16,128]{1,0:T(8,128)S(1)} %copy-done.4, ...), custom_call_target="tpu_custom_call" | custom-call | flops 5750000128 | bytes 18500000 | tf_op jit(solution)/shard_map/pallas_call | solution.py:464
  62.8 2.6 %collective-permute-done.15 = f32[112,128]{1,0:T(8,128)S(1)} collective-permute-done((f32[112,128]{1,0:T(8,128)S(1)}, f32[112,128]{1,0:T(8,128)S(1)}, u32[]{:S(2)}, u32[]{:S(2)}) %collective-permute-start.15) | collective-permute-done | bytes 57376 | tf_op jit(solution)/shard_map/ppermute | solution.py:500
  70.4 3.7 %collective-permute-done.17 = f32[176,128]{1,0:T(8,128)S(1)} collective-permute-done((f32[176,128]{1,0:T(8,128)S(1)}, f32[176,128]{1,0:T(8,128)S(1)}, u32[]{:S(2)}, u32[]{:S(2)}) %collective-permute-start.17) | collective-permute-done | bytes 90144 | tf_op jit(solution)/shard_map/ppermute | solution.py:505
  74.1 2.8 %collective-permute-start.21 = (f32[112,128]{1,0:T(8,128)S(1)}, f32[112,128]{1,0:T(8,128)S(1)}, u32[]{:S(2)}, u32[]{:S(2)}) collective-permute-start(f32[112,128]{1,0:T(8,128)S(1)} %subtract_maximum_fusion.1.mine), channel_id=1, source_target_pairs={{0,1},{1,0},{2,3},{3,2},{4,5},{5,4},{6,7},{7,6},{8,9},{9,8},{10,11... | collective-permute-start | bytes 172040 | tf_op jit(solution)/shard_map/ppermute | solution.py:480
  77.0 2.4 %shard_map.88 = (f32[24,64,128]{2,1,0:T(8,128)S(1)}, f32[64,256]{1,0:T(8,128)S(1)}, f32[16,64,128]{2,1,0:T(8,128)S(1)}) custom-call(f32[24,64,128]{2,1,0:T(8,128)S(1)} %get-tuple-element.162.ext_ref, f32[64,256]{1,0:T(8,128)S(1)} %get-tuple-element.163.side_ref, f32[12,64,256]{2,1,0:T(8,128)S(1)} %get-tuple-element.181.acc, ...), custom_call_target="tpu_custom_call" | custom-call | flops 2875000064 | bytes 9250000 | tf_op jit(solution)/shard_map/pallas_call | solution.py:464
  79.4 3.5 %shard_map.89 = (f32[112,128]{1,0:T(8,128)S(1)}, f32[176,128]{1,0:T(8,128)S(1)}, f32[4,64,128]{2,1,0:T(8,128)S(1)}, f32[4,64,128]{2,1,0:T(8,128)S(1)}, f32[64,12...) custom-call(f32[16,448,128]{2,1,0:T(8,128)S(1)} %get-tuple-element.132.obs_ref, f32[16,128]{1,0:T(8,128)S(1)} %copy-done.4, ...), custom_call_target="tpu_custom_call" | custom-call | flops 5750000128 | bytes 18500000 | tf_op jit(solution)/shard_map/pallas_call | solution.py:464
  87.3 2.4 %collective-permute-start.27 = (f32[4,64,128]{2,1,0:T(8,128)S(1)}, f32[4,64,128]{2,1,0:T(8,128)S(1)}, u32[]{:S(2)}, u32[]{:S(2)}) collective-permute-start(f32[4,64,128]{2,1,0:T(8,128)S(1)} %get-tuple-element.200), channel_id=1, source_target_pairs={{0,8},{8,0},{16,24},{24,16},{1,9},{9,1},{17,25},{25,17},{2,10},{10... | collective-permute-start | bytes 393224 | tf_op jit(solution)/shard_map/ppermute | solution.py:490
  90.3 2.8 %collective-permute-done.24 = f32[112,128]{1,0:T(8,128)S(1)} collective-permute-done((f32[112,128]{1,0:T(8,128)S(1)}, f32[112,128]{1,0:T(8,128)S(1)}, u32[]{:S(2)}, u32[]{:S(2)}) %collective-permute-start.24) | collective-permute-done | bytes 57376 | tf_op jit(solution)/shard_map/ppermute | solution.py:500
  94.4 2.4 %collective-permute-start.26 = (f32[176,128]{1,0:T(8,128)S(1)}, f32[176,128]{1,0:T(8,128)S(1)}, u32[]{:S(2)}, u32[]{:S(2)}) collective-permute-start(f32[176,128]{1,0:T(8,128)S(1)} %get-tuple-element.236), channel_id=1, source_target_pairs={{0,24},{8,16},{16,8},{24,0},{1,25},{9,17},{17,9},{25,1},{2,26},{10... | collective-permute-start | bytes 270344 | tf_op jit(solution)/shard_map/ppermute | solution.py:505
  98.0 2.6 %collective-permute-done.26 = f32[176,128]{1,0:T(8,128)S(1)} collective-permute-done((f32[176,128]{1,0:T(8,128)S(1)}, f32[176,128]{1,0:T(8,128)S(1)}, u32[]{:S(2)}, u32[]{:S(2)}) %collective-permute-start.26) | collective-permute-done | bytes 90144 | tf_op jit(solution)/shard_map/ppermute | solution.py:505
  100.6 2.5 %collective-permute-start.30 = (f32[112,128]{1,0:T(8,128)S(1)}, f32[112,128]{1,0:T(8,128)S(1)}, u32[]{:S(2)}, u32[]{:S(2)}) collective-permute-start(f32[112,128]{1,0:T(8,128)S(1)} %subtract_maximum_fusion.mine), channel_id=1, source_target_pairs={{0,1},{1,0},{2,3},{3,2},{4,5},{5,4},{6,7},{7,6},{8,9},{9,8},{10,11... | collective-permute-start | bytes 172040 | tf_op jit(solution)/shard_map/ppermute | solution.py:480
  103.1 2.0 %shard_map.92 = f32[64,16,128]{2,1,0:T(8,128)} custom-call(f32[24,64,128]{2,1,0:T(8,128)S(1)} %get-tuple-element.185.ext_ref, f32[64,256]{1,0:T(8,128)S(1)} %get-tuple-element.186.side_ref, f32[12,64,256]{2,1,0:T(8,128)S(1)} %get-tuple-element.204.acc, f32[64,256]{1,0:T(8,128)S(1)} %get-tuple-element.205.near_ref, f32[64,128]{1,0:T(8,128)S(1)} %get-tuple-element.210.left, ...), custom_call_target="tpu_custom_call" | custom-call | flops 1724999936 | bytes 5550000 | tf_op jit(solution)/shard_map/pallas_call | solution.py:464
  (107 shorter events, 33.5 us)
Async XLA Ops:
  3.9 4.3 %collective-permute-start.1 = (f32[72,128]{1,0:T(8,128)S(1)}, f32[72,128]{1,0:T(8,128)S(1)}, u32[]{:S(2)}, u32[]{:S(2)}) collective-permute-start(f32[72,128]{1,0:T(8,128)S(1)} %get-tuple-element.111), channel_id=1, source_target_pairs={{0,7},{1,2},{2,1},{3,4},{4,3},{5,6},{6,5},{7,0},{8,15},{9,10},{10,... | collective-permute-start | bytes 110600 | tf_op jit(solution)/shard_map/ppermute | solution.py:485
  8.2 7.5 %collective-permute-start.2 = (f32[344,128]{1,0:T(8,128)S(1)}, f32[344,128]{1,0:T(8,128)S(1)}, u32[]{:S(2)}, u32[]{:S(2)}) collective-permute-start(f32[344,128]{1,0:T(8,128)S(1)} %constant_dynamic-update-slice_fusion), channel_id=1, source_target_pairs={{0,8},{8,0},{16,24},{24,16},{1,9},{9,1},{17,25},{25,17},{2,10},{10... | collective-permute-start | bytes 528392 | tf_op jit(solution)/shard_map/ppermute | solution.py:490
  10.5 5.2 %collective-permute-start.3 = (f32[344,128]{1,0:T(8,128)S(1)}, f32[344,128]{1,0:T(8,128)S(1)}, u32[]{:S(2)}, u32[]{:S(2)}) collective-permute-start(f32[344,128]{1,0:T(8,128)S(1)} %get-tuple-element.217), channel_id=1, source_target_pairs={{0,0},{8,16},{16,8},{24,24},{1,1},{9,17},{17,9},{25,25},{2,2},{10,... | collective-permute-start | bytes 528392 | tf_op jit(solution)/shard_map/ppermute | solution.py:495
  21.3 8.3 %collective-permute-start.4 = (f32[176,128]{1,0:T(8,128)S(1)}, f32[176,128]{1,0:T(8,128)S(1)}, u32[]{:S(2)}, u32[]{:S(2)}) collective-permute-start(f32[176,128]{1,0:T(8,128)S(1)} %get-tuple-element.137), channel_id=1, source_target_pairs={{0,1},{1,0},{2,3},{3,2},{4,5},{5,4},{6,7},{7,6},{8,9},{9,8},{10,11... | collective-permute-start | bytes 270344 | tf_op jit(solution)/shard_map/ppermute | solution.py:480
  22.3 20.4 %collective-permute-start.10 = (f32[8,64,128]{2,1,0:T(8,128)S(1)}, f32[8,64,128]{2,1,0:T(8,128)S(1)}, u32[]{:S(2)}, u32[]{:S(2)}) collective-permute-start(f32[8,64,128]{2,1,0:T(8,128)S(1)} %get-tuple-element.153), channel_id=1, source_target_pairs={{0,0},{8,16},{16,8},{24,24},{1,1},{9,17},{17,9},{25,25},{2,2},{10,... | collective-permute-start | bytes 786440 | tf_op jit(solution)/shard_map/ppermute | solution.py:495
  23.2 19.6 %collective-permute-start.9 = (f32[8,64,128]{2,1,0:T(8,128)S(1)}, f32[8,64,128]{2,1,0:T(8,128)S(1)}, u32[]{:S(2)}, u32[]{:S(2)}) collective-permute-start(f32[8,64,128]{2,1,0:T(8,128)S(1)} %get-tuple-element.152), channel_id=1, source_target_pairs={{0,8},{8,0},{16,24},{24,16},{1,9},{9,1},{17,25},{25,17},{2,10},{10... | collective-permute-start | bytes 786440 | tf_op jit(solution)/shard_map/ppermute | solution.py:490
  29.7 6.2 %collective-permute-start.5 = (f32[176,128]{1,0:T(8,128)S(1)}, f32[176,128]{1,0:T(8,128)S(1)}, u32[]{:S(2)}, u32[]{:S(2)}) collective-permute-start(f32[176,128]{1,0:T(8,128)S(1)} %pad_maximum_fusion.6), channel_id=1, source_target_pairs={{0,7},{1,2},{2,1},{3,4},{4,3},{5,6},{6,5},{7,0},{8,15},{9,10},{10,... | collective-permute-start | bytes 270344 | tf_op jit(solution)/shard_map/ppermute | solution.py:485
  39.1 7.3 %collective-permute-start.11 = (f32[112,128]{1,0:T(8,128)S(1)}, f32[112,128]{1,0:T(8,128)S(1)}, u32[]{:S(2)}, u32[]{:S(2)}) collective-permute-start(f32[112,128]{1,0:T(8,128)S(1)} %add.76), channel_id=1, source_target_pairs={{0,16},{8,24},{16,0},{24,8},{1,17},{9,25},{17,1},{25,9},{2,18},{10... | collective-permute-start | bytes 172040 | tf_op jit(solution)/shard_map/ppermute | solution.py:505
  39.2 4.9 %collective-permute-start.7 = (f32[176,128]{1,0:T(8,128)S(1)}, f32[176,128]{1,0:T(8,128)S(1)}, u32[]{:S(2)}, u32[]{:S(2)}) collective-permute-start(f32[176,128]{1,0:T(8,128)S(1)} %get-tuple-element.241), channel_id=1, source_target_pairs={{0,8},{8,0},{16,24},{24,16},{1,9},{9,1},{17,25},{25,17},{2,10},{10... | collective-permute-start | bytes 270344 | tf_op jit(solution)/shard_map/ppermute | solution.py:490
  40.1 6.2 %collective-permute-start.8 = (f32[176,128]{1,0:T(8,128)S(1)}, f32[176,128]{1,0:T(8,128)S(1)}, u32[]{:S(2)}, u32[]{:S(2)}) collective-permute-start(f32[176,128]{1,0:T(8,128)S(1)} %get-tuple-element.240), channel_id=1, source_target_pairs={{0,24},{8,16},{16,8},{24,0},{1,25},{9,17},{17,9},{25,1},{2,26},{10... | collective-permute-start | bytes 270344 | tf_op jit(solution)/shard_map/ppermute | solution.py:505
  46.4 5.4 %collective-permute-start.12 = (f32[112,128]{1,0:T(8,128)S(1)}, f32[112,128]{1,0:T(8,128)S(1)}, u32[]{:S(2)}, u32[]{:S(2)}) collective-permute-start(f32[112,128]{1,0:T(8,128)S(1)} %subtract_maximum_fusion.2.mine), channel_id=1, source_target_pairs={{0,1},{1,0},{2,3},{3,2},{4,5},{5,4},{6,7},{7,6},{8,9},{9,8},{10,11... | collective-permute-start | bytes 172040 | tf_op jit(solution)/shard_map/ppermute | solution.py:480
  56.7 5.2 %collective-permute-start.14 = (f32[176,128]{1,0:T(8,128)S(1)}, f32[176,128]{1,0:T(8,128)S(1)}, u32[]{:S(2)}, u32[]{:S(2)}) collective-permute-start(f32[176,128]{1,0:T(8,128)S(1)} %pad_maximum_fusion.7), channel_id=1, source_target_pairs={{0,7},{1,2},{2,1},{3,4},{4,3},{5,6},{6,5},{7,0},{8,15},{9,10},{10,... | collective-permute-start | bytes 270344 | tf_op jit(solution)/shard_map/ppermute | solution.py:485
  58.7 10.4 %collective-permute-start.19 = (f32[8,64,128]{2,1,0:T(8,128)S(1)}, f32[8,64,128]{2,1,0:T(8,128)S(1)}, u32[]{:S(2)}, u32[]{:S(2)}) collective-permute-start(f32[8,64,128]{2,1,0:T(8,128)S(1)} %get-tuple-element.178), channel_id=1, source_target_pairs={{0,0},{8,16},{16,8},{24,24},{1,1},{9,17},{17,9},{25,25},{2,2},{10,... | collective-permute-start | bytes 786440 | tf_op jit(solution)/shard_map/ppermute | solution.py:495
  59.6 9.5 %collective-permute-start.18 = (f32[8,64,128]{2,1,0:T(8,128)S(1)}, f32[8,64,128]{2,1,0:T(8,128)S(1)}, u32[]{:S(2)}, u32[]{:S(2)}) collective-permute-start(f32[8,64,128]{2,1,0:T(8,128)S(1)} %get-tuple-element.177), channel_id=1, source_target_pairs={{0,8},{8,0},{16,24},{24,16},{1,9},{9,1},{17,25},{25,17},{2,10},{10... | collective-permute-start | bytes 786440 | tf_op jit(solution)/shard_map/ppermute | solution.py:490
  65.4 8.7 %collective-permute-start.20 = (f32[112,128]{1,0:T(8,128)S(1)}, f32[112,128]{1,0:T(8,128)S(1)}, u32[]{:S(2)}, u32[]{:S(2)}) collective-permute-start(f32[112,128]{1,0:T(8,128)S(1)} %add.82), channel_id=1, source_target_pairs={{0,16},{8,24},{16,0},{24,8},{1,17},{9,25},{17,1},{25,9},{2,18},{10... | collective-permute-start | bytes 172040 | tf_op jit(solution)/shard_map/ppermute | solution.py:505
  67.9 6.2 %collective-permute-start.17 = (f32[176,128]{1,0:T(8,128)S(1)}, f32[176,128]{1,0:T(8,128)S(1)}, u32[]{:S(2)}, u32[]{:S(2)}) collective-permute-start(f32[176,128]{1,0:T(8,128)S(1)} %get-tuple-element.238), channel_id=1, source_target_pairs={{0,24},{8,16},{16,8},{24,0},{1,25},{9,17},{17,9},{25,1},{2,26},{10... | collective-permute-start | bytes 270344 | tf_op jit(solution)/shard_map/ppermute | solution.py:505
  74.1 5.2 %collective-permute-start.21 = (f32[112,128]{1,0:T(8,128)S(1)}, f32[112,128]{1,0:T(8,128)S(1)}, u32[]{:S(2)}, u32[]{:S(2)}) collective-permute-start(f32[112,128]{1,0:T(8,128)S(1)} %subtract_maximum_fusion.1.mine), channel_id=1, source_target_pairs={{0,1},{1,0},{2,3},{3,2},{4,5},{5,4},{6,7},{7,6},{8,9},{9,8},{10,11... | collective-permute-start | bytes 172040 | tf_op jit(solution)/shard_map/ppermute | solution.py:480
  84.2 5.4 %collective-permute-start.23 = (f32[176,128]{1,0:T(8,128)S(1)}, f32[176,128]{1,0:T(8,128)S(1)}, u32[]{:S(2)}, u32[]{:S(2)}) collective-permute-start(f32[176,128]{1,0:T(8,128)S(1)} %pad_maximum_fusion.8), channel_id=1, source_target_pairs={{0,7},{1,2},{2,1},{3,4},{4,3},{5,6},{6,5},{7,0},{8,15},{9,10},{10,... | collective-permute-start | bytes 270344 | tf_op jit(solution)/shard_map/ppermute | solution.py:485
  86.6 10.2 %collective-permute-start.28 = (f32[4,64,128]{2,1,0:T(8,128)S(1)}, f32[4,64,128]{2,1,0:T(8,128)S(1)}, u32[]{:S(2)}, u32[]{:S(2)}) collective-permute-start(f32[4,64,128]{2,1,0:T(8,128)S(1)} %get-tuple-element.201), channel_id=1, source_target_pairs={{0,0},{8,16},{16,8},{24,24},{1,1},{9,17},{17,9},{25,25},{2,2},{10,... | collective-permute-start | bytes 393224 | tf_op jit(solution)/shard_map/ppermute | solution.py:495
  87.3 9.5 %collective-permute-start.27 = (f32[4,64,128]{2,1,0:T(8,128)S(1)}, f32[4,64,128]{2,1,0:T(8,128)S(1)}, u32[]{:S(2)}, u32[]{:S(2)}) collective-permute-start(f32[4,64,128]{2,1,0:T(8,128)S(1)} %get-tuple-element.200), channel_id=1, source_target_pairs={{0,8},{8,0},{16,24},{24,16},{1,9},{9,1},{17,25},{25,17},{2,10},{10... | collective-permute-start | bytes 393224 | tf_op jit(solution)/shard_map/ppermute | solution.py:490
  93.1 7.5 %collective-permute-start.29 = (f32[112,128]{1,0:T(8,128)S(1)}, f32[112,128]{1,0:T(8,128)S(1)}, u32[]{:S(2)}, u32[]{:S(2)}) collective-permute-start(f32[112,128]{1,0:T(8,128)S(1)} %add.88), channel_id=1, source_target_pairs={{0,16},{8,24},{16,0},{24,8},{1,17},{9,25},{17,1},{25,9},{2,18},{10... | collective-permute-start | bytes 172040 | tf_op jit(solution)/shard_map/ppermute | solution.py:505
  93.2 4.8 %collective-permute-start.25 = (f32[176,128]{1,0:T(8,128)S(1)}, f32[176,128]{1,0:T(8,128)S(1)}, u32[]{:S(2)}, u32[]{:S(2)}) collective-permute-start(f32[176,128]{1,0:T(8,128)S(1)} %get-tuple-element.237), channel_id=1, source_target_pairs={{0,8},{8,0},{16,24},{24,16},{1,9},{9,1},{17,25},{25,17},{2,10},{10... | collective-permute-start | bytes 270344 | tf_op jit(solution)/shard_map/ppermute | solution.py:490
  94.4 6.1 %collective-permute-start.26 = (f32[176,128]{1,0:T(8,128)S(1)}, f32[176,128]{1,0:T(8,128)S(1)}, u32[]{:S(2)}, u32[]{:S(2)}) collective-permute-start(f32[176,128]{1,0:T(8,128)S(1)} %get-tuple-element.236), channel_id=1, source_target_pairs={{0,24},{8,16},{16,8},{24,0},{1,25},{9,17},{17,9},{25,1},{2,26},{10... | collective-permute-start | bytes 270344 | tf_op jit(solution)/shard_map/ppermute | solution.py:505
  100.6 4.5 %collective-permute-start.30 = (f32[112,128]{1,0:T(8,128)S(1)}, f32[112,128]{1,0:T(8,128)S(1)}, u32[]{:S(2)}, u32[]{:S(2)}) collective-permute-start(f32[112,128]{1,0:T(8,128)S(1)} %subtract_maximum_fusion.mine), channel_id=1, source_target_pairs={{0,1},{1,0},{2,3},{3,2},{4,5},{5,4},{6,7},{7,6},{8,9},{9,8},{10,11... | collective-permute-start | bytes 172040 | tf_op jit(solution)/shard_map/ppermute | solution.py:480
  (12 other events, 50.3 us)

commit v5 on v4

--- a/solution.py
+++ b/solution.py
@@ -193,13 +193,24 @@
         seen_ref[i, start:] = jnp.where(sub < depth - start, seen_ref[i, start:], 0.0)
 
 
-def adjoint_weights_kernel(marks_up, marks, marks_down, table, w_high, w_low, s_high, s_low, scratch, *, height, width):
+def flipped(table, family):
+    return lambda u, v: table[KS - 1 - u, family, KS - 1 - v]
+
+
+def own_weights_kernel(marks, table, w_high, w_low):
+    family = jnp.max(marks[8:16]).astype(jnp.int32)
+    build_main(flipped(table, family), w_high, w_low, (), w_high.shape[1] // 2)
+
+
+def halo_weights_kernel(
+    marks_up, marks, marks_down, table, w_high, w_low, s_high, s_low, scratch, *, height, width
+):
     families = []
     for ref in (marks_up, marks, marks_down):
         for k in range(3):
             families.append(jnp.max(ref[8 * k : 8 * k + 8]).astype(jnp.int32))
-    for b in range(3):
-        build_main(lambda u, v, b=b: table[KS - 1 - u, families[3 * b + 1], KS - 1 - v], w_high, w_low, (b,), width)
+    for b in range(2):
+        build_main(flipped(table, families[6 * b + 1]), w_high, w_low, (b,), width)
     n = s_high.shape[1]
     half = n // 2
     shape = (EDGE, n)
@@ -352,7 +363,7 @@
     high_ref[at], low_ref[at] = split(row)
 
 
-def adjoint_into(acc, g_high, g_low, first, w_high, w_low, band):
+def adjoint_into(acc, g_high, g_low, first, w_high, w_low):
     pairs, channels, double = g_high.shape
     for d in range(RADIUS + 1):
         begin, end = max(first, d), min(first + pairs, acc.shape[0] + d)
@@ -360,7 +371,7 @@
             continue
         high = g_high[begin - first : end - first].reshape((end - begin) * channels, double)
         low = g_low[begin - first : end - first].reshape((end - begin) * channels, double)
-        part = mm_split(high, low, w_high[band, d], w_low[band, d])
+        part = mm_split(high, low, w_high[d], w_low[d])
         acc[begin - d : end - d] += part.reshape(end - begin, channels, double)
 
 
@@ -376,7 +387,7 @@
         near[q // height] = jnp.where(lane // EDGE == q % height, moved, near[q // height])
     near_ref[...] = jnp.concatenate(near, axis=1)
     acc[...] = jnp.zeros_like(acc)
-    adjoint_into(acc, g_high, g_low, EDGE // 2, wa_high, wa_low, 1)
+    adjoint_into(acc, g_high, g_low, EDGE // 2, wa_high, wa_low)
 
 
 def halo_maps_kernel(acc_in, near_in, p1, p2, place, wa_high, wa_low, acc, near_ref, g_high, g_low):
@@ -399,8 +410,8 @@
         near[q // height] = jnp.where(lane // EDGE == q % height, moved, near[q // height])
     near_ref[...] = jnp.concatenate(near, axis=1)
     n = halo // 2
-    adjoint_into(acc, g_high.at[:n], g_low.at[:n], EDGE // 2 - n, wa_high, wa_low, 0)
-    adjoint_into(acc, g_high.at[n:], g_low.at[n:], (EDGE + height) // 2, wa_high, wa_low, 2)
+    adjoint_into(acc, g_high.at[:n], g_low.at[:n], EDGE // 2 - n, wa_high.at[0], wa_low.at[0])
+    adjoint_into(acc, g_high.at[n:], g_low.at[n:], (EDGE + height) // 2, wa_high.at[1], wa_low.at[1])
 
 
 def maps_kernel(
@@ -585,12 +596,12 @@
         a_rows, got1, got2, left, right, above, below, place, *wf,
     )
     marks_up, marks_down = above_below(got1[body + channels :], got2[body + channels :])
-    main_a = ((3, RADIUS + 1, 2 * width, 2 * width), BF16)
+    main_a = ((2, RADIUS + 1, 2 * width, 2 * width), BF16)
     side_a = ((6 * width, 4 * width), BF16)
 
-    def adjoint_weights():
+    def halo_weights(marks):
         return call(
-            functools.partial(adjoint_weights_kernel, height=height, width=width),
+            functools.partial(halo_weights_kernel, height=height, width=width),
             3,
             [main_a, main_a, side_a, side_a],
             [((6 * width, 4 * width), F32)],
@@ -602,14 +613,14 @@
     acc_shape = ((ext_rows // 2, channels, 2 * width), F32)
     near_shape = ((channels, 2 * width), F32)
 
-    def own_part(g_rows, wa):
+    def own_part(g_rows):
         return call(
             own_maps_kernel,
             2,
             [acc_shape, near_shape],
             [((pairs, channels, 2 * width), BF16)] * 2,
             [VMEM] * 3,
-            g_rows, wa[0], wa[1],
+            g_rows, *w_own,
         )
 
     for step in range(ITERS):
@@ -633,22 +644,27 @@
         got_core = core_swap(to_core)
         p1 = pair_one(main1)
         share = g_mine + got_core[:quarter]
-        if step > 0:
-            own, near = own_part(g_rows, wa)
-            main2, own, near = lax.optimization_barrier((main2, own, near))
+        main2, share = lax.optimization_barrier((main2, share))
         p2 = pair_two(main2)
         got_cross = cross_swap(jnp.concatenate([share, e_cross]))
+        share = share + got_cross[:quarter]
         if step == 0:
-            wa = adjoint_weights()
-            got_cross, *wa = lax.optimization_barrier((got_cross, *wa))
-            own, near = own_part(g_rows, wa)
-        share = share + got_cross[:quarter]
+            share, marks = lax.optimization_barrier((share, marks))
+            wa = halo_weights(marks)
+        else:
+            share, g_rows = lax.optimization_barrier((share, g_rows))
+            own, near = own_part(g_rows)
         left, right, side1, side2 = sides(got_core[quarter:], got_cross[quarter:])
         step_size = 4
         while step_size < n_cols:
             share = share + col_swap(share, step_size)
             step_size *= 2
-        share, own, near = lax.optimization_barrier((share, own, near))
+        if step == 0:
+            share, g_rows, marks, *wa = lax.optimization_barrier((share, g_rows, marks, *wa))
+            w_own = call(own_weights_kernel, 1, [main_w, main_w], [], [VMEM, SMEM], marks, table)
+            own, near = own_part(g_rows)
+        else:
+            share, own, near = lax.optimization_barrier((share, own, near))
         own, near = call(
             halo_maps_kernel,
             1.5,

time: 107 us -> 104 us (0.972)
  starting transfers between devices: 46 us -> 41.2 us
  Pallas kernels: 37.7 us -> 39 us
  waiting for transfers between devices: 19 us -> 20.2 us
    ppermute x7, starting transfers between devices: 17 us -> 8.74 us  [pair_one(): return lax.ppermute(x, 'rows', [(i, i ^ 1) for i in range(count)])]
    ppermute x4, waiting for transfers between devices: 2.02 us -> 6.66 us  [cross_swap(): lax.ppermute(x, 'cols', [(i, (i + 1 if i % 2 else i - 1) % count) for i i...]
    ppermute x6, starting transfers between devices: 7.09 us -> 11.5 us  [row_swap(): return lax.ppermute(x, 'rows', [(i, i ^ mask) for i in range(count)])]
    ppermute x3, waiting for transfers between devices: 5.87 us -> 2.37 us  [col_swap(): lax.ppermute(x, 'cols', [(i, (((i + 1) % count ^ mask) - 1) % count) for...]
    ppermute x6, waiting for transfers between devices: 8.54 us -> 7.22 us  [row_swap(): return lax.ppermute(x, 'rows', [(i, i ^ mask) for i in range(count)])]
    pallas_call x17 -> x18, Pallas kernels: 37.7 us -> 39 us  [call(): pl.pallas_call(kernel, out_shape=[jax.ShapeDtypeStruct(s, d) for s, d in...]
  transfers between devices with their start and end apart: 31 -> 31, of which waited for: 10 -> 13; matrix products, arithmetic and copies ran while one was open for 0% -> 0% of each run, Pallas kernels for 21% -> 23%
where the time goes in v5:
time: 104 us
  starting transfers between devices  41.2 us (40%)
  Pallas kernels  39 us (38%)
  waiting for transfers between devices  20.2 us (19%)
  between operations  2.01 us (2%)
  local copies, waits for them, and re-layouts  1.28 us (1%)
    pallas_call x18, Pallas kernels, call(): pl.pallas_call(kernel, out_shape=[jax.ShapeDtypeStruct(s, d) for s, d in...  39 us
    ppermute x6, starting transfers between devices, row_swap(): return lax.ppermute(x, 'rows', [(i, i ^ mask) for i in range(count)])  11.5 us
    ppermute x7, starting transfers between devices, core_swap(): return lax.ppermute(x, 'cols', [(i, i ^ 1) for i in range(count)])  9.22 us
    ppermute x7, starting transfers between devices, pair_one(): return lax.ppermute(x, 'rows', [(i, i ^ 1) for i in range(count)])  8.74 us
    ppermute x6, waiting for transfers between devices, row_swap(): return lax.ppermute(x, 'rows', [(i, i ^ mask) for i in range(count)])  7.22 us
    ppermute x4, waiting for transfers between devices, cross_swap(): lax.ppermute(x, 'cols', [(i, (i + 1 if i % 2 else i - 1) % count) for i i...  6.66 us
    ppermute x4, starting transfers between devices, cross_swap(): lax.ppermute(x, 'cols', [(i, (i + 1 if i % 2 else i - 1) % count) for i i...  5.94 us
    ppermute x7, waiting for transfers between devices, core_swap(): return lax.ppermute(x, 'cols', [(i, i ^ 1) for i in range(count)])  3.49 us
  transfers between devices with their start and end apart: 31, of which 13 were waited for; matrix products, arithmetic and copies ran while one was open for 0% of the time, Pallas kernels for 23%

profile of v5, /device:TPU:1, one launch (start us, length us, event | category | flops | bytes accessed | tf_op | source)
XLA Modules:
  0.0 104.2 jit_solution(2255288937057499635)
XLA Ops:
  3.9 2.6 %collective-permute-start.1 = (f32[72,128]{1,0:T(8,128)S(1)}, f32[72,128]{1,0:T(8,128)S(1)}, u32[]{:S(2)}, u32[]{:S(2)}) collective-permute-start(f32[72,128]{1,0:T(8,128)S(1)} %get-tuple-element.118), channel_id=1, source_target_pairs={{0,7},{1,2},{2,1},{3,4},{4,3},{5,6},{6,5},{7,0},{8,15},{9,10},{10,... | collective-permute-start | bytes 110600 | tf_op jit(solution)/shard_map/ppermute | solution.py:496
  6.6 1.6 %collective-permute-done.1 = f32[72,128]{1,0:T(8,128)S(1)} collective-permute-done((f32[72,128]{1,0:T(8,128)S(1)}, f32[72,128]{1,0:T(8,128)S(1)}, u32[]{:S(2)}, u32[]{:S(2)}) %collective-permute-start.1) | collective-permute-done | bytes 36896 | tf_op jit(solution)/shard_map/ppermute | solution.py:496
  8.2 2.3 %collective-permute-start.2 = (f32[344,128]{1,0:T(8,128)S(1)}, f32[344,128]{1,0:T(8,128)S(1)}, u32[]{:S(2)}, u32[]{:S(2)}) collective-permute-start(f32[344,128]{1,0:T(8,128)S(1)} %constant_dynamic-update-slice_fusion), channel_id=1, source_target_pairs={{0,8},{8,0},{16,24},{24,16},{1,9},{9,1},{17,25},{25,17},{2,10},{10... | collective-permute-start | bytes 528392 | tf_op jit(solution)/shard_map/ppermute | solution.py:501
  11.2 4.5 %shard_map.78 = (f32[16,448,128]{2,1,0:T(8,128)S(1)}, f32[112,128]{1,0:T(8,128)S(1)}, f32[112,128]{1,0:T(8,128)S(1)}, bf16[5,256,256]{2,1,0:T(8,128)(2,1)S(1)}, ...) custom-call(s32[1,1]{1,0:T(1,128)S(6)} %copy.28.family, ...), custom_call_target="tpu_custom_call" | custom-call | flops 3449999872 | bytes 11100000 | tf_op jit(solution)/shard_map/pallas_call | solution.py:475
  15.8 2.0 %shard_map.79 = (f32[24,64,128]{2,1,0:T(8,128)S(1)}, f32[64,256]{1,0:T(8,128)S(1)}, f32[16,64,128]{2,1,0:T(8,128)S(1)}) custom-call(f32[16,64,128]{2,1,0:T(8,128)S(1)} %get-tuple-element.114.rows_ref, f32[344,128]{1,0:T(8,128)S(1)} %collective-permute-done.2.p1, f32[344,128]{1,0:T(8,128)S(1)} %collective-permute-done.3.p2, ...), custom_call_target="tpu_custom_call" | custom-call | flops 2300000000 | bytes 7400000 | tf_op jit(solution)/shard_map/pallas_call | solution.py:475
  17.8 3.5 %shard_map.80 = (f32[112,128]{1,0:T(8,128)S(1)}, f32[176,128]{1,0:T(8,128)S(1)}, f32[8,64,128]{2,1,0:T(8,128)S(1)}, f32[8,64,128]{2,1,0:T(8,128)S(1)}, f32[64,12...) custom-call(f32[16,448,128]{2,1,0:T(8,128)S(1)} %get-tuple-element.139.obs_ref, f32[16,128]{1,0:T(8,128)S(1)} %copy-done.4, ...), custom_call_target="tpu_custom_call" | custom-call | flops 5750000128 | bytes 18500000 | tf_op jit(solution)/shard_map/pallas_call | solution.py:475
  24.6 3.9 %collective-permute-start.9 = (f32[8,64,128]{2,1,0:T(8,128)S(1)}, f32[8,64,128]{2,1,0:T(8,128)S(1)}, u32[]{:S(2)}, u32[]{:S(2)}) collective-permute-start(f32[8,64,128]{2,1,0:T(8,128)S(1)} %get-tuple-element.162), channel_id=1, source_target_pairs={{0,8},{8,0},{16,24},{24,16},{1,9},{9,1},{17,25},{25,17},{2,10},{10... | collective-permute-start | bytes 786440 | tf_op jit(solution)/shard_map/ppermute | solution.py:501
  30.6 3.5 %shard_map.81 = (bf16[2,5,256,256]{3,2,1,0:T(8,128)(2,1)S(1)}, bf16[2,5,256,256]{3,2,1,0:T(8,128)(2,1)S(1)}, bf16[768,512]{1,0:T(8,128)(2,1)S(1)}, bf16[768,512]{1,0:T(8,128)(2,1)S(1)}) custom-call(f32[24,128]{1,0:T(8,128)S(1)} %get-tuple-element.241.marks_up, f32[24,128]{1,0:T(8,128)S(1)} %pad_maximum_fusion.9.marks, ...), custom_call_target="tpu_custom_call" | custom-call | flops 3449999872 | bytes 11100000 | tf_op jit(solution)/shard_map/pallas_call | solution.py:475
  34.3 3.8 %collective-permute-start.11 = (f32[112,128]{1,0:T(8,128)S(1)}, f32[112,128]{1,0:T(8,128)S(1)}, u32[]{:S(2)}, u32[]{:S(2)}) collective-permute-start(f32[112,128]{1,0:T(8,128)S(1)} %add.76), channel_id=1, source_target_pairs={{0,16},{8,24},{16,0},{24,8},{1,17},{9,25},{17,1},{25,9},{2,18},{10... | collective-permute-start | bytes 172040 | tf_op jit(solution)/shard_map/ppermute | solution.py:516
  38.1 1.8 %shard_map.82 = (bf16[5,256,256]{2,1,0:T(8,128)(2,1)S(1)}, bf16[5,256,256]{2,1,0:T(8,128)(2,1)S(1)}) custom-call(f32[24,128]{1,0:T(8,128)S(1)} %pad_maximum_fusion.9.marks, f32[9,8,9]{2,1,0:T(8,128)S(1)} %bitcast.15), custom_call_target="tpu_custom_call" | custom-call | flops 1150000000 | bytes 3700000 | tf_op jit(solution)/shard_map/pallas_call | solution.py:475
  39.9 1.6 %collective-permute-start.8 = (f32[176,128]{1,0:T(8,128)S(1)}, f32[176,128]{1,0:T(8,128)S(1)}, u32[]{:S(2)}, u32[]{:S(2)}) collective-permute-start(f32[176,128]{1,0:T(8,128)S(1)} %get-tuple-element.254), channel_id=1, source_target_pairs={{0,24},{8,16},{16,8},{24,0},{1,25},{9,17},{17,9},{25,1},{2,26},{10... | collective-permute-start | bytes 270344 | tf_op jit(solution)/shard_map/ppermute | solution.py:516
  45.7 2.3 %collective-permute-start.12 = (f32[112,128]{1,0:T(8,128)S(1)}, f32[112,128]{1,0:T(8,128)S(1)}, u32[]{:S(2)}, u32[]{:S(2)}) collective-permute-start(f32[112,128]{1,0:T(8,128)S(1)} %subtract_maximum_fusion.2.mine), channel_id=1, source_target_pairs={{0,1},{1,0},{2,3},{3,2},{4,5},{5,4},{6,7},{7,6},{8,9},{9,8},{10,11... | collective-permute-start | bytes 172040 | tf_op jit(solution)/shard_map/ppermute | solution.py:491
  48.0 2.4 %shard_map.85 = (f32[24,64,128]{2,1,0:T(8,128)S(1)}, f32[64,256]{1,0:T(8,128)S(1)}, f32[16,64,128]{2,1,0:T(8,128)S(1)}) custom-call(f32[24,64,128]{2,1,0:T(8,128)S(1)} %get-tuple-element.137.ext_ref, f32[64,256]{1,0:T(8,128)S(1)} %get-tuple-element.138.side_ref, f32[12,64,256]{2,1,0:T(8,128)S(1)} %get-tuple-element.168.acc, ...), custom_call_target="tpu_custom_call" | custom-call | flops 2875000064 | bytes 9250000 | tf_op jit(solution)/shard_map/pallas_call | solution.py:475
  50.3 3.5 %shard_map.86 = (f32[112,128]{1,0:T(8,128)S(1)}, f32[176,128]{1,0:T(8,128)S(1)}, f32[8,64,128]{2,1,0:T(8,128)S(1)}, f32[8,64,128]{2,1,0:T(8,128)S(1)}, f32[64,12...) custom-call(f32[16,448,128]{2,1,0:T(8,128)S(1)} %get-tuple-element.139.obs_ref, f32[16,128]{1,0:T(8,128)S(1)} %copy-done.4, ...), custom_call_target="tpu_custom_call" | custom-call | flops 5750000128 | bytes 18500000 | tf_op jit(solution)/shard_map/pallas_call | solution.py:475
  58.4 1.7 %collective-permute-done.14 = f32[176,128]{1,0:T(8,128)S(1)} collective-permute-done((f32[176,128]{1,0:T(8,128)S(1)}, f32[176,128]{1,0:T(8,128)S(1)}, u32[]{:S(2)}, u32[]{:S(2)}) %collective-permute-start.14) | collective-permute-done | bytes 90144 | tf_op jit(solution)/shard_map/ppermute | solution.py:496
  68.8 3.2 %collective-permute-done.17 = f32[176,128]{1,0:T(8,128)S(1)} collective-permute-done((f32[176,128]{1,0:T(8,128)S(1)}, f32[176,128]{1,0:T(8,128)S(1)}, u32[]{:S(2)}, u32[]{:S(2)}) %collective-permute-start.17) | collective-permute-done | bytes 90144 | tf_op jit(solution)/shard_map/ppermute | solution.py:516
  72.1 2.5 %collective-permute-start.21 = (f32[112,128]{1,0:T(8,128)S(1)}, f32[112,128]{1,0:T(8,128)S(1)}, u32[]{:S(2)}, u32[]{:S(2)}) collective-permute-start(f32[112,128]{1,0:T(8,128)S(1)} %subtract_maximum_fusion.1.mine), channel_id=1, source_target_pairs={{0,1},{1,0},{2,3},{3,2},{4,5},{5,4},{6,7},{7,6},{8,9},{9,8},{10,11... | collective-permute-start | bytes 172040 | tf_op jit(solution)/shard_map/ppermute | solution.py:491
  74.6 2.4 %shard_map.89 = (f32[24,64,128]{2,1,0:T(8,128)S(1)}, f32[64,256]{1,0:T(8,128)S(1)}, f32[16,64,128]{2,1,0:T(8,128)S(1)}) custom-call(f32[24,64,128]{2,1,0:T(8,128)S(1)} %get-tuple-element.174.ext_ref, f32[64,256]{1,0:T(8,128)S(1)} %get-tuple-element.175.side_ref, f32[12,64,256]{2,1,0:T(8,128)S(1)} %get-tuple-element.194.acc, ...), custom_call_target="tpu_custom_call" | custom-call | flops 2875000064 | bytes 9250000 | tf_op jit(solution)/shard_map/pallas_call | solution.py:475
  77.0 3.5 %shard_map.90 = (f32[112,128]{1,0:T(8,128)S(1)}, f32[176,128]{1,0:T(8,128)S(1)}, f32[4,64,128]{2,1,0:T(8,128)S(1)}, f32[4,64,128]{2,1,0:T(8,128)S(1)}, f32[64,12...) custom-call(f32[16,448,128]{2,1,0:T(8,128)S(1)} %get-tuple-element.139.obs_ref, f32[16,128]{1,0:T(8,128)S(1)} %copy-done.4, ...), custom_call_target="tpu_custom_call" | custom-call | flops 5750000128 | bytes 18500000 | tf_op jit(solution)/shard_map/pallas_call | solution.py:475
  83.5 3.4 %collective-permute-done.23 = f32[176,128]{1,0:T(8,128)S(1)} collective-permute-done((f32[176,128]{1,0:T(8,128)S(1)}, f32[176,128]{1,0:T(8,128)S(1)}, u32[]{:S(2)}, u32[]{:S(2)}) %collective-permute-start.23) | collective-permute-done | bytes 90144 | tf_op jit(solution)/shard_map/ppermute | solution.py:496
  91.7 2.1 %collective-permute-start.26 = (f32[176,128]{1,0:T(8,128)S(1)}, f32[176,128]{1,0:T(8,128)S(1)}, u32[]{:S(2)}, u32[]{:S(2)}) collective-permute-start(f32[176,128]{1,0:T(8,128)S(1)} %get-tuple-element.250), channel_id=1, source_target_pairs={{0,24},{8,16},{16,8},{24,0},{1,25},{9,17},{17,9},{25,1},{2,26},{10... | collective-permute-start | bytes 270344 | tf_op jit(solution)/shard_map/ppermute | solution.py:516
  95.0 2.5 %collective-permute-done.26 = f32[176,128]{1,0:T(8,128)S(1)} collective-permute-done((f32[176,128]{1,0:T(8,128)S(1)}, f32[176,128]{1,0:T(8,128)S(1)}, u32[]{:S(2)}, u32[]{:S(2)}) %collective-permute-start.26) | collective-permute-done | bytes 90144 | tf_op jit(solution)/shard_map/ppermute | solution.py:516
  97.6 3.2 %collective-permute-start.30 = (f32[112,128]{1,0:T(8,128)S(1)}, f32[112,128]{1,0:T(8,128)S(1)}, u32[]{:S(2)}, u32[]{:S(2)}) collective-permute-start(f32[112,128]{1,0:T(8,128)S(1)} %subtract_maximum_fusion.mine), channel_id=1, source_target_pairs={{0,1},{1,0},{2,3},{3,2},{4,5},{5,4},{6,7},{7,6},{8,9},{9,8},{10,11... | collective-permute-start | bytes 172040 | tf_op jit(solution)/shard_map/ppermute | solution.py:491
  100.8 2.0 %shard_map.93 = f32[64,16,128]{2,1,0:T(8,128)} custom-call(f32[24,64,128]{2,1,0:T(8,128)S(1)} %get-tuple-element.198.ext_ref, f32[64,256]{1,0:T(8,128)S(1)} %get-tuple-element.199.side_ref, f32[12,64,256]{2,1,0:T(8,128)S(1)} %get-tuple-element.218.acc, f32[64,256]{1,0:T(8,128)S(1)} %get-tuple-element.219.near_ref, f32[64,128]{1,0:T(8,128)S(1)} %get-tuple-element.224.left, ...), custom_call_target="tpu_custom_call" | custom-call | flops 1724999936 | bytes 5550000 | tf_op jit(solution)/shard_map/pallas_call | solution.py:475
  (108 shorter events, 36.4 us)
Async XLA Ops:
  3.9 4.3 %collective-permute-start.1 = (f32[72,128]{1,0:T(8,128)S(1)}, f32[72,128]{1,0:T(8,128)S(1)}, u32[]{:S(2)}, u32[]{:S(2)}) collective-permute-start(f32[72,128]{1,0:T(8,128)S(1)} %get-tuple-element.118), channel_id=1, source_target_pairs={{0,7},{1,2},{2,1},{3,4},{4,3},{5,6},{6,5},{7,0},{8,15},{9,10},{10,... | collective-permute-start | bytes 110600 | tf_op jit(solution)/shard_map/ppermute | solution.py:496
  8.2 7.5 %collective-permute-start.2 = (f32[344,128]{1,0:T(8,128)S(1)}, f32[344,128]{1,0:T(8,128)S(1)}, u32[]{:S(2)}, u32[]{:S(2)}) collective-permute-start(f32[344,128]{1,0:T(8,128)S(1)} %constant_dynamic-update-slice_fusion), channel_id=1, source_target_pairs={{0,8},{8,0},{16,24},{24,16},{1,9},{9,1},{17,25},{25,17},{2,10},{10... | collective-permute-start | bytes 528392 | tf_op jit(solution)/shard_map/ppermute | solution.py:501
  10.5 5.2 %collective-permute-start.3 = (f32[344,128]{1,0:T(8,128)S(1)}, f32[344,128]{1,0:T(8,128)S(1)}, u32[]{:S(2)}, u32[]{:S(2)}) collective-permute-start(f32[344,128]{1,0:T(8,128)S(1)} %get-tuple-element.231), channel_id=1, source_target_pairs={{0,0},{8,16},{16,8},{24,24},{1,1},{9,17},{17,9},{25,25},{2,2},{10,... | collective-permute-start | bytes 528392 | tf_op jit(solution)/shard_map/ppermute | solution.py:506
  23.2 6.1 %collective-permute-start.5 = (f32[176,128]{1,0:T(8,128)S(1)}, f32[176,128]{1,0:T(8,128)S(1)}, u32[]{:S(2)}, u32[]{:S(2)}) collective-permute-start(f32[176,128]{1,0:T(8,128)S(1)} %pad_maximum_fusion.6), channel_id=1, source_target_pairs={{0,7},{1,2},{2,1},{3,4},{4,3},{5,6},{6,5},{7,0},{8,15},{9,10},{10,... | collective-permute-start | bytes 270344 | tf_op jit(solution)/shard_map/ppermute | solution.py:496
  24.6 18.3 %collective-permute-start.9 = (f32[8,64,128]{2,1,0:T(8,128)S(1)}, f32[8,64,128]{2,1,0:T(8,128)S(1)}, u32[]{:S(2)}, u32[]{:S(2)}) collective-permute-start(f32[8,64,128]{2,1,0:T(8,128)S(1)} %get-tuple-element.162), channel_id=1, source_target_pairs={{0,8},{8,0},{16,24},{24,16},{1,9},{9,1},{17,25},{25,17},{2,10},{10... | collective-permute-start | bytes 786440 | tf_op jit(solution)/shard_map/ppermute | solution.py:501
  28.5 14.4 %collective-permute-start.10 = (f32[8,64,128]{2,1,0:T(8,128)S(1)}, f32[8,64,128]{2,1,0:T(8,128)S(1)}, u32[]{:S(2)}, u32[]{:S(2)}) collective-permute-start(f32[8,64,128]{2,1,0:T(8,128)S(1)} %get-tuple-element.163), channel_id=1, source_target_pairs={{0,0},{8,16},{16,8},{24,24},{1,1},{9,17},{17,9},{25,25},{2,2},{10,... | collective-permute-start | bytes 786440 | tf_op jit(solution)/shard_map/ppermute | solution.py:506
  29.3 4.9 %collective-permute-start.6 = (f32[112,128]{1,0:T(8,128)S(1)}, f32[112,128]{1,0:T(8,128)S(1)}, u32[]{:S(2)}, u32[]{:S(2)}) collective-permute-start(f32[112,128]{1,0:T(8,128)S(1)} %slice_add_fusion.4), channel_id=1, source_target_pairs={{0,4},{1,5},{2,6},{3,7},{4,0},{5,1},{6,2},{7,3},{8,12},{9,13},{10,... | collective-permute-start | bytes 172040 | tf_op jit(solution)/shard_map/ppermute | solution.py:511
  34.3 11.4 %collective-permute-start.11 = (f32[112,128]{1,0:T(8,128)S(1)}, f32[112,128]{1,0:T(8,128)S(1)}, u32[]{:S(2)}, u32[]{:S(2)}) collective-permute-start(f32[112,128]{1,0:T(8,128)S(1)} %add.76), channel_id=1, source_target_pairs={{0,16},{8,24},{16,0},{24,8},{1,17},{9,25},{17,1},{25,9},{2,18},{10... | collective-permute-start | bytes 172040 | tf_op jit(solution)/shard_map/ppermute | solution.py:516
  39.9 4.3 %collective-permute-start.7 = (f32[176,128]{1,0:T(8,128)S(1)}, f32[176,128]{1,0:T(8,128)S(1)}, u32[]{:S(2)}, u32[]{:S(2)}) collective-permute-start(f32[176,128]{1,0:T(8,128)S(1)} %get-tuple-element.255), channel_id=1, source_target_pairs={{0,8},{8,0},{16,24},{24,16},{1,9},{9,1},{17,25},{25,17},{2,10},{10... | collective-permute-start | bytes 270344 | tf_op jit(solution)/shard_map/ppermute | solution.py:501
  39.9 5.7 %collective-permute-start.8 = (f32[176,128]{1,0:T(8,128)S(1)}, f32[176,128]{1,0:T(8,128)S(1)}, u32[]{:S(2)}, u32[]{:S(2)}) collective-permute-start(f32[176,128]{1,0:T(8,128)S(1)} %get-tuple-element.254), channel_id=1, source_target_pairs={{0,24},{8,16},{16,8},{24,0},{1,25},{9,17},{17,9},{25,1},{2,26},{10... | collective-permute-start | bytes 270344 | tf_op jit(solution)/shard_map/ppermute | solution.py:516
  45.7 4.6 %collective-permute-start.12 = (f32[112,128]{1,0:T(8,128)S(1)}, f32[112,128]{1,0:T(8,128)S(1)}, u32[]{:S(2)}, u32[]{:S(2)}) collective-permute-start(f32[112,128]{1,0:T(8,128)S(1)} %subtract_maximum_fusion.2.mine), channel_id=1, source_target_pairs={{0,1},{1,0},{2,3},{3,2},{4,5},{5,4},{6,7},{7,6},{8,9},{9,8},{10,11... | collective-permute-start | bytes 172040 | tf_op jit(solution)/shard_map/ppermute | solution.py:491
  55.2 4.8 %collective-permute-start.14 = (f32[176,128]{1,0:T(8,128)S(1)}, f32[176,128]{1,0:T(8,128)S(1)}, u32[]{:S(2)}, u32[]{:S(2)}) collective-permute-start(f32[176,128]{1,0:T(8,128)S(1)} %pad_maximum_fusion.7), channel_id=1, source_target_pairs={{0,7},{1,2},{2,1},{3,4},{4,3},{5,6},{6,5},{7,0},{8,15},{9,10},{10,... | collective-permute-start | bytes 270344 | tf_op jit(solution)/shard_map/ppermute | solution.py:496
  56.2 10.9 %collective-permute-start.18 = (f32[8,64,128]{2,1,0:T(8,128)S(1)}, f32[8,64,128]{2,1,0:T(8,128)S(1)}, u32[]{:S(2)}, u32[]{:S(2)}) collective-permute-start(f32[8,64,128]{2,1,0:T(8,128)S(1)} %get-tuple-element.190), channel_id=1, source_target_pairs={{0,8},{8,0},{16,24},{24,16},{1,9},{9,1},{17,25},{25,17},{2,10},{10... | collective-permute-start | bytes 786440 | tf_op jit(solution)/shard_map/ppermute | solution.py:501
  57.5 9.7 %collective-permute-start.19 = (f32[8,64,128]{2,1,0:T(8,128)S(1)}, f32[8,64,128]{2,1,0:T(8,128)S(1)}, u32[]{:S(2)}, u32[]{:S(2)}) collective-permute-start(f32[8,64,128]{2,1,0:T(8,128)S(1)} %get-tuple-element.191), channel_id=1, source_target_pairs={{0,0},{8,16},{16,8},{24,24},{1,1},{9,17},{17,9},{25,25},{2,2},{10,... | collective-permute-start | bytes 786440 | tf_op jit(solution)/shard_map/ppermute | solution.py:506
  63.5 8.5 %collective-permute-start.20 = (f32[112,128]{1,0:T(8,128)S(1)}, f32[112,128]{1,0:T(8,128)S(1)}, u32[]{:S(2)}, u32[]{:S(2)}) collective-permute-start(f32[112,128]{1,0:T(8,128)S(1)} %add.82), channel_id=1, source_target_pairs={{0,16},{8,24},{16,0},{24,8},{1,17},{9,25},{17,1},{25,9},{2,18},{10... | collective-permute-start | bytes 172040 | tf_op jit(solution)/shard_map/ppermute | solution.py:516
  65.8 6.2 %collective-permute-start.17 = (f32[176,128]{1,0:T(8,128)S(1)}, f32[176,128]{1,0:T(8,128)S(1)}, u32[]{:S(2)}, u32[]{:S(2)}) collective-permute-start(f32[176,128]{1,0:T(8,128)S(1)} %get-tuple-element.252), channel_id=1, source_target_pairs={{0,24},{8,16},{16,8},{24,0},{1,25},{9,17},{17,9},{25,1},{2,26},{10... | collective-permute-start | bytes 270344 | tf_op jit(solution)/shard_map/ppermute | solution.py:516
  72.1 4.9 %collective-permute-start.21 = (f32[112,128]{1,0:T(8,128)S(1)}, f32[112,128]{1,0:T(8,128)S(1)}, u32[]{:S(2)}, u32[]{:S(2)}) collective-permute-start(f32[112,128]{1,0:T(8,128)S(1)} %subtract_maximum_fusion.1.mine), channel_id=1, source_target_pairs={{0,1},{1,0},{2,3},{3,2},{4,5},{5,4},{6,7},{7,6},{8,9},{9,8},{10,11... | collective-permute-start | bytes 172040 | tf_op jit(solution)/shard_map/ppermute | solution.py:491
  81.9 5.1 %collective-permute-start.23 = (f32[176,128]{1,0:T(8,128)S(1)}, f32[176,128]{1,0:T(8,128)S(1)}, u32[]{:S(2)}, u32[]{:S(2)}) collective-permute-start(f32[176,128]{1,0:T(8,128)S(1)} %pad_maximum_fusion.8), channel_id=1, source_target_pairs={{0,7},{1,2},{2,1},{3,4},{4,3},{5,6},{6,5},{7,0},{8,15},{9,10},{10,... | collective-permute-start | bytes 270344 | tf_op jit(solution)/shard_map/ppermute | solution.py:496
  82.9 10.9 %collective-permute-start.27 = (f32[4,64,128]{2,1,0:T(8,128)S(1)}, f32[4,64,128]{2,1,0:T(8,128)S(1)}, u32[]{:S(2)}, u32[]{:S(2)}) collective-permute-start(f32[4,64,128]{2,1,0:T(8,128)S(1)} %get-tuple-element.214), channel_id=1, source_target_pairs={{0,8},{8,0},{16,24},{24,16},{1,9},{9,1},{17,25},{25,17},{2,10},{10... | collective-permute-start | bytes 393224 | tf_op jit(solution)/shard_map/ppermute | solution.py:501
  82.9 10.9 %collective-permute-start.28 = (f32[4,64,128]{2,1,0:T(8,128)S(1)}, f32[4,64,128]{2,1,0:T(8,128)S(1)}, u32[]{:S(2)}, u32[]{:S(2)}) collective-permute-start(f32[4,64,128]{2,1,0:T(8,128)S(1)} %get-tuple-element.215), channel_id=1, source_target_pairs={{0,0},{8,16},{16,8},{24,24},{1,1},{9,17},{17,9},{25,25},{2,2},{10,... | collective-permute-start | bytes 393224 | tf_op jit(solution)/shard_map/ppermute | solution.py:506
  90.1 7.5 %collective-permute-start.29 = (f32[112,128]{1,0:T(8,128)S(1)}, f32[112,128]{1,0:T(8,128)S(1)}, u32[]{:S(2)}, u32[]{:S(2)}) collective-permute-start(f32[112,128]{1,0:T(8,128)S(1)} %add.88), channel_id=1, source_target_pairs={{0,16},{8,24},{16,0},{24,8},{1,17},{9,25},{17,1},{25,9},{2,18},{10... | collective-permute-start | bytes 172040 | tf_op jit(solution)/shard_map/ppermute | solution.py:516
  91.2 3.8 %collective-permute-start.25 = (f32[176,128]{1,0:T(8,128)S(1)}, f32[176,128]{1,0:T(8,128)S(1)}, u32[]{:S(2)}, u32[]{:S(2)}) collective-permute-start(f32[176,128]{1,0:T(8,128)S(1)} %get-tuple-element.251), channel_id=1, source_target_pairs={{0,8},{8,0},{16,24},{24,16},{1,9},{9,1},{17,25},{25,17},{2,10},{10... | collective-permute-start | bytes 270344 | tf_op jit(solution)/shard_map/ppermute | solution.py:501
  91.7 5.9 %collective-permute-start.26 = (f32[176,128]{1,0:T(8,128)S(1)}, f32[176,128]{1,0:T(8,128)S(1)}, u32[]{:S(2)}, u32[]{:S(2)}) collective-permute-start(f32[176,128]{1,0:T(8,128)S(1)} %get-tuple-element.250), channel_id=1, source_target_pairs={{0,24},{8,16},{16,8},{24,0},{1,25},{9,17},{17,9},{25,1},{2,26},{10... | collective-permute-start | bytes 270344 | tf_op jit(solution)/shard_map/ppermute | solution.py:516
  97.6 5.1 %collective-permute-start.30 = (f32[112,128]{1,0:T(8,128)S(1)}, f32[112,128]{1,0:T(8,128)S(1)}, u32[]{:S(2)}, u32[]{:S(2)}) collective-permute-start(f32[112,128]{1,0:T(8,128)S(1)} %subtract_maximum_fusion.mine), channel_id=1, source_target_pairs={{0,1},{1,0},{2,3},{3,2},{4,5},{5,4},{6,7},{7,6},{8,9},{9,8},{10,11... | collective-permute-start | bytes 172040 | tf_op jit(solution)/shard_map/ppermute | solution.py:491
  (12 other events, 48.3 us)

commit v6 on v5

--- a/solution.py
+++ b/solution.py
@@ -462,13 +462,11 @@
     blur_into(b_ref, a2_high, a2_low, side, wf_high, wf_low, sf_high, sf_low, acc_b)
 
 
-def spectra_kernel(mine, other, place, out_ref):
-    channels, depth = out_ref.shape
-    second = place[HALF] == 1
-    first = jnp.where(second, other[...], mine[...])
-    last = jnp.where(second, mine[...], other[...])
-    parts = [first[:, :channels], first[:, channels:], last[:, :channels], last[:, channels:]]
-    out_ref[...] = jnp.concatenate(parts, axis=0).T[:, :depth]
+def turn_kernel(half_ref, out_ref):
+    channels, width = out_ref.shape
+    half = jnp.concatenate([half_ref[:, :channels], half_ref[:, channels:]], axis=0)
+    rest = jnp.zeros((width - half.shape[0], channels), F32)
+    out_ref[...] = jnp.concatenate([half, rest], axis=0).T
 
 
 def call(kernel, micros, outs, scratch, specs, *args, aliases=None):
@@ -534,8 +532,9 @@
     has_up = (row_at > 0).astype(F32)
     has_down = (row_at < n_rows - 1).astype(F32)
     table = jnp.transpose(kernels, (1, 0, 2))
-    place, abundance, row_odd, col_odd, has_left, has_right, has_up, has_down = lax.optimization_barrier(
-        (place, abundance, row_odd, col_odd, has_left, has_right, has_up, has_down)
+    second_half = half_of == 1
+    place, abundance, second_half, row_odd, col_odd, has_left, has_right, has_up, has_down = lax.optimization_barrier(
+        (place, abundance, second_half, row_odd, col_odd, has_left, has_right, has_up, has_down)
     )
     tile = (channels, width)
 
@@ -646,8 +645,15 @@
         share = g_mine + got_core[:quarter]
         main2, share = lax.optimization_barrier((main2, share))
         p2 = pair_two(main2)
-        got_cross = cross_swap(jnp.concatenate([share, e_cross]))
-        share = share + got_cross[:quarter]
+        message = jnp.concatenate([share, e_cross])
+        got_cross = cross_swap(message)
+        at_once = last and n_cols >= 8
+        if at_once:
+            got_four = col_swap(message, 4)
+            got_five = col_swap(message, 5)
+            share = (share + got_cross[:quarter]) + (got_four[:quarter] + got_five[:quarter])
+        else:
+            share = share + got_cross[:quarter]
         if step == 0:
             share, marks = lax.optimization_barrier((share, marks))
             wa = halo_weights(marks)
@@ -655,16 +661,21 @@
             share, g_rows = lax.optimization_barrier((share, g_rows))
             own, near = own_part(g_rows)
         left, right, side1, side2 = sides(got_core[quarter:], got_cross[quarter:])
-        step_size = 4
+        step_size = 8 if at_once else 4
         while step_size < n_cols:
             share = share + col_swap(share, step_size)
             step_size *= 2
         if step == 0:
-            share, g_rows, marks, *wa = lax.optimization_barrier((share, g_rows, marks, *wa))
+            share, *wa = lax.optimization_barrier((share, *wa))
+            got1 = pair_one(jnp.concatenate([share, side1]))
+            g_rows, marks, p1 = lax.optimization_barrier((g_rows, marks, p1))
+            got1, p2 = lax.optimization_barrier((got1, p2))
             w_own = call(own_weights_kernel, 1, [main_w, main_w], [], [VMEM, SMEM], marks, table)
             own, near = own_part(g_rows)
         else:
-            share, own, near = lax.optimization_barrier((share, own, near))
+            if not at_once:
+                share, own, near = lax.optimization_barrier((share, own, near))
+            got1 = pair_one(jnp.concatenate([share, side1]))
         own, near = call(
             halo_maps_kernel,
             1.5,
@@ -674,7 +685,6 @@
             own, near, p1, p2, place, wa[0], wa[1],
             aliases={0: 0, 1: 1},
         )
-        got1 = pair_one(jnp.concatenate([share, side1]))
         if n_rows == 4:
             got2 = row_swap(jnp.concatenate([share, side2]), 3)
             got3 = row_swap(share, 2)
@@ -711,13 +721,15 @@
                 *gathered, *wf,
             )
         mine = jnp.maximum(mine - rate * share, 0.0)
-        other = core_swap(mine)
         if last:
             (out,) = made
-        else:
+            (mine,) = call(turn_kernel, 0.5, [((channels, -(-2 * quarter // 128) * 128), F32)], [], [VMEM], mine)
+        other = core_swap(mine)
+        if not last:
             ext, side, blurred = made
-    (result,) = call(spectra_kernel, 1, [((channels, bands), F32)], [], [VMEM, VMEM, SMEM], mine, other, place)
-    return out, result.T
+    low = jnp.where(second_half, other, mine)[:, : 2 * quarter]
+    high = jnp.where(second_half, mine, other)[:, : bands - 2 * quarter]
+    return out, jnp.concatenate([low, high], axis=1).T
 
 
 def solution(mesh):

time: 104 us -> 102 us (0.981)
  waiting for transfers between devices: 20.2 us -> 15.7 us
  starting transfers between devices: 41.2 us -> 43.4 us
  Pallas kernels: 39 us -> 37.8 us
    ppermute x3 -> x4, starting transfers between devices: 2.8 us -> 5.79 us  [col_swap(): lax.ppermute(x, 'cols', [(i, (((i + 1) % count ^ mask) - 1) % count) for...]
    ppermute x4, waiting for transfers between devices: 6.66 us -> 4.06 us  [cross_swap(): lax.ppermute(x, 'cols', [(i, (i + 1 if i % 2 else i - 1) % count) for i i...]
    ppermute x6, waiting for transfers between devices: 7.22 us -> 5.01 us  [row_swap(): return lax.ppermute(x, 'rows', [(i, i ^ mask) for i in range(count)])]
    pallas_call x18, Pallas kernels: 39 us -> 37.8 us  [call(): pl.pallas_call(kernel, out_shape=[jax.ShapeDtypeStruct(s, d) for s, d in...]
    ppermute x3 -> x4, waiting for transfers between devices: 2.37 us -> 2.82 us  [col_swap(): lax.ppermute(x, 'cols', [(i, (((i + 1) % count ^ mask) - 1) % count) for...]
  transfers between devices with their start and end apart: 31 -> 32, of which waited for: 13 -> 12; matrix products, arithmetic and copies ran while one was open for 0% -> 0% of each run, Pallas kernels for 23% -> 24%
where the time goes in v6:
time: 102 us; the launch traced here: 101 us
  starting transfers between devices  43.4 us (43%)
  Pallas kernels  37.8 us (37%)
  waiting for transfers between devices  15.7 us (15%)
  between operations  2.06 us (2%)
  local copies, waits for them, and re-layouts  1.29 us (1%)
  other arithmetic  1.16 us (1%)
    pallas_call x18, Pallas kernels, call(): pl.pallas_call(kernel, out_shape=[jax.ShapeDtypeStruct(s, d) for s, d in...  37.8 us
    ppermute x6, starting transfers between devices, row_swap(): return lax.ppermute(x, 'rows', [(i, i ^ mask) for i in range(count)])  10.9 us
    ppermute x7, starting transfers between devices, pair_one(): return lax.ppermute(x, 'rows', [(i, i ^ 1) for i in range(count)])  9.27 us
    ppermute x7, starting transfers between devices, core_swap(): return lax.ppermute(x, 'cols', [(i, i ^ 1) for i in range(count)])  8.65 us
    ppermute x4, starting transfers between devices, col_swap(): lax.ppermute(x, 'cols', [(i, (((i + 1) % count ^ mask) - 1) % count) for...  5.79 us
    ppermute x4, starting transfers between devices, cross_swap(): lax.ppermute(x, 'cols', [(i, (i + 1 if i % 2 else i - 1) % count) for i i...  5.71 us
    ppermute x6, waiting for transfers between devices, row_swap(): return lax.ppermute(x, 'rows', [(i, i ^ mask) for i in range(count)])  5.01 us
    ppermute x4, waiting for transfers between devices, cross_swap(): lax.ppermute(x, 'cols', [(i, (i + 1 if i % 2 else i - 1) % count) for i i...  4.06 us
  transfers between devices with their start and end apart: 32, of which 12 were waited for; matrix products, arithmetic and copies ran while one was open for 0% of the time, Pallas kernels for 24%

profile of v6, /device:TPU:1, one launch (start us, length us, event | category | flops | bytes accessed | tf_op | source)
XLA Modules:
  0.0 101.4 jit_solution(6229202436214210057)
XLA Ops:
  3.9 2.6 %collective-permute-start.1 = (f32[72,128]{1,0:T(8,128)S(1)}, f32[72,128]{1,0:T(8,128)S(1)}, u32[]{:S(2)}, u32[]{:S(2)}) collective-permute-start(f32[72,128]{1,0:T(8,128)S(1)} %get-tuple-element.119), channel_id=1, source_target_pairs={{0,7},{1,2},{2,1},{3,4},{4,3},{5,6},{6,5},{7,0},{8,15},{9,10},{10,... | collective-permute-start | bytes 110600 | tf_op jit(solution)/shard_map/ppermute | solution.py:494
  8.2 2.3 %collective-permute-start.2 = (f32[344,128]{1,0:T(8,128)S(1)}, f32[344,128]{1,0:T(8,128)S(1)}, u32[]{:S(2)}, u32[]{:S(2)}) collective-permute-start(f32[344,128]{1,0:T(8,128)S(1)} %constant_dynamic-update-slice_fusion), channel_id=1, source_target_pairs={{0,8},{8,0},{16,24},{24,16},{1,9},{9,1},{17,25},{25,17},{2,10},{10... | collective-permute-start | bytes 528392 | tf_op jit(solution)/shard_map/ppermute | solution.py:499
  11.2 4.5 %shard_map.78 = (f32[16,448,128]{2,1,0:T(8,128)S(1)}, f32[112,128]{1,0:T(8,128)S(1)}, f32[112,128]{1,0:T(8,128)S(1)}, bf16[5,256,256]{2,1,0:T(8,128)(2,1)S(1)}, ...) custom-call(s32[1,1]{1,0:T(1,128)S(6)} %copy.29.family, ...), custom_call_target="tpu_custom_call" | custom-call | flops 3449999872 | bytes 11100000 | tf_op jit(solution)/shard_map/pallas_call | solution.py:473
  15.8 2.0 %shard_map.79 = (f32[24,64,128]{2,1,0:T(8,128)S(1)}, f32[64,256]{1,0:T(8,128)S(1)}, f32[16,64,128]{2,1,0:T(8,128)S(1)}) custom-call(f32[16,64,128]{2,1,0:T(8,128)S(1)} %get-tuple-element.115.rows_ref, f32[344,128]{1,0:T(8,128)S(1)} %collective-permute-done.2.p1, f32[344,128]{1,0:T(8,128)S(1)} %collective-permute-done.3.p2, ...), custom_call_target="tpu_custom_call" | custom-call | flops 2300000000 | bytes 7400000 | tf_op jit(solution)/shard_map/pallas_call | solution.py:473
  17.8 3.5 %shard_map.80 = (f32[112,128]{1,0:T(8,128)S(1)}, f32[176,128]{1,0:T(8,128)S(1)}, f32[8,64,128]{2,1,0:T(8,128)S(1)}, f32[8,64,128]{2,1,0:T(8,128)S(1)}, f32[64,12...) custom-call(f32[16,448,128]{2,1,0:T(8,128)S(1)} %get-tuple-element.140.obs_ref, f32[16,128]{1,0:T(8,128)S(1)} %copy-done.4, ...), custom_call_target="tpu_custom_call" | custom-call | flops 5750000128 | bytes 18500000 | tf_op jit(solution)/shard_map/pallas_call | solution.py:473
  24.6 3.9 %collective-permute-start.10 = (f32[8,64,128]{2,1,0:T(8,128)S(1)}, f32[8,64,128]{2,1,0:T(8,128)S(1)}, u32[]{:S(2)}, u32[]{:S(2)}) collective-permute-start(f32[8,64,128]{2,1,0:T(8,128)S(1)} %get-tuple-element.159), channel_id=1, source_target_pairs={{0,8},{8,0},{16,24},{24,16},{1,9},{9,1},{17,25},{25,17},{2,10},{10... | collective-permute-start | bytes 786440 | tf_op jit(solution)/shard_map/ppermute | solution.py:499
  30.6 3.5 %shard_map.81 = (bf16[2,5,256,256]{3,2,1,0:T(8,128)(2,1)S(1)}, bf16[2,5,256,256]{3,2,1,0:T(8,128)(2,1)S(1)}, bf16[768,512]{1,0:T(8,128)(2,1)S(1)}, bf16[768,512]{1,0:T(8,128)(2,1)S(1)}) custom-call(f32[24,128]{1,0:T(8,128)S(1)} %get-tuple-element.243.marks_up, f32[24,128]{1,0:T(8,128)S(1)} %pad_maximum_fusion.8.marks, ...), custom_call_target="tpu_custom_call" | custom-call | flops 3449999872 | bytes 11100000 | tf_op jit(solution)/shard_map/pallas_call | solution.py:473
  34.3 3.8 %collective-permute-start.11 = (f32[112,128]{1,0:T(8,128)S(1)}, f32[112,128]{1,0:T(8,128)S(1)}, u32[]{:S(2)}, u32[]{:S(2)}) collective-permute-start(f32[112,128]{1,0:T(8,128)S(1)} %add.79), channel_id=1, source_target_pairs={{0,16},{8,24},{16,0},{24,8},{1,17},{9,25},{17,1},{25,9},{2,18},{10... | collective-permute-start | bytes 172040 | tf_op jit(solution)/shard_map/ppermute | solution.py:514
  38.2 1.6 %collective-permute-start.9 = (f32[176,128]{1,0:T(8,128)S(1)}, f32[176,128]{1,0:T(8,128)S(1)}, u32[]{:S(2)}, u32[]{:S(2)}) collective-permute-start(f32[176,128]{1,0:T(8,128)S(1)} %get-tuple-element.256), channel_id=1, source_target_pairs={{0,24},{8,16},{16,8},{24,0},{1,25},{9,17},{17,9},{25,1},{2,26},{10... | collective-permute-start | bytes 270344 | tf_op jit(solution)/shard_map/ppermute | solution.py:514
  39.7 1.8 %shard_map.82 = (bf16[5,256,256]{2,1,0:T(8,128)(2,1)S(1)}, bf16[5,256,256]{2,1,0:T(8,128)(2,1)S(1)}) custom-call(f32[24,128]{1,0:T(8,128)S(1)} %pad_maximum_fusion.8.marks, f32[9,8,9]{2,1,0:T(8,128)S(1)} %bitcast.16), custom_call_target="tpu_custom_call" | custom-call | flops 1150000000 | bytes 3700000 | tf_op jit(solution)/shard_map/pallas_call | solution.py:473
  44.4 2.0 %collective-permute-start.12 = (f32[112,128]{1,0:T(8,128)S(1)}, f32[112,128]{1,0:T(8,128)S(1)}, u32[]{:S(2)}, u32[]{:S(2)}) collective-permute-start(f32[112,128]{1,0:T(8,128)S(1)} %subtract_maximum_fusion.2.mine), channel_id=1, source_target_pairs={{0,1},{1,0},{2,3},{3,2},{4,5},{5,4},{6,7},{7,6},{8,9},{9,8},{10,11... | collective-permute-start | bytes 172040 | tf_op jit(solution)/shard_map/ppermute | solution.py:489
  46.5 2.4 %shard_map.85 = (f32[24,64,128]{2,1,0:T(8,128)S(1)}, f32[64,256]{1,0:T(8,128)S(1)}, f32[16,64,128]{2,1,0:T(8,128)S(1)}) custom-call(f32[24,64,128]{2,1,0:T(8,128)S(1)} %get-tuple-element.138.ext_ref, f32[64,256]{1,0:T(8,128)S(1)} %get-tuple-element.139.side_ref, f32[12,64,256]{2,1,0:T(8,128)S(1)} %get-tuple-element.172.acc, ...), custom_call_target="tpu_custom_call" | custom-call | flops 2875000064 | bytes 9250000 | tf_op jit(solution)/shard_map/pallas_call | solution.py:473
  48.9 3.5 %shard_map.86 = (f32[112,128]{1,0:T(8,128)S(1)}, f32[176,128]{1,0:T(8,128)S(1)}, f32[8,64,128]{2,1,0:T(8,128)S(1)}, f32[8,64,128]{2,1,0:T(8,128)S(1)}, f32[64,12...) custom-call(f32[16,448,128]{2,1,0:T(8,128)S(1)} %get-tuple-element.140.obs_ref, f32[16,128]{1,0:T(8,128)S(1)} %copy-done.4, ...), custom_call_target="tpu_custom_call" | custom-call | flops 5750000128 | bytes 18500000 | tf_op jit(solution)/shard_map/pallas_call | solution.py:473
  56.7 2.3 %collective-permute-done.14 = f32[176,128]{1,0:T(8,128)S(1)} collective-permute-done((f32[176,128]{1,0:T(8,128)S(1)}, f32[176,128]{1,0:T(8,128)S(1)}, u32[]{:S(2)}, u32[]{:S(2)}) %collective-permute-start.14) | collective-permute-done | bytes 90144 | tf_op jit(solution)/shard_map/ppermute | solution.py:494
  62.4 1.6 %collective-permute-start.20 = (f32[112,128]{1,0:T(8,128)S(1)}, f32[112,128]{1,0:T(8,128)S(1)}, u32[]{:S(2)}, u32[]{:S(2)}) collective-permute-start(f32[112,128]{1,0:T(8,128)S(1)} %add.85), channel_id=1, source_target_pairs={{0,16},{8,24},{16,0},{24,8},{1,17},{9,25},{17,1},{25,9},{2,18},{10... | collective-permute-start | bytes 172040 | tf_op jit(solution)/shard_map/ppermute | solution.py:514
  64.3 1.8 %collective-permute-start.17 = (f32[176,128]{1,0:T(8,128)S(1)}, f32[176,128]{1,0:T(8,128)S(1)}, u32[]{:S(2)}, u32[]{:S(2)}) collective-permute-start(f32[176,128]{1,0:T(8,128)S(1)} %get-tuple-element.254), channel_id=1, source_target_pairs={{0,24},{8,16},{16,8},{24,0},{1,25},{9,17},{17,9},{25,1},{2,26},{10... | collective-permute-start | bytes 270344 | tf_op jit(solution)/shard_map/ppermute | solution.py:514
  67.8 2.0 %collective-permute-done.17 = f32[176,128]{1,0:T(8,128)S(1)} collective-permute-done((f32[176,128]{1,0:T(8,128)S(1)}, f32[176,128]{1,0:T(8,128)S(1)}, u32[]{:S(2)}, u32[]{:S(2)}) %collective-permute-start.17) | collective-permute-done | bytes 90144 | tf_op jit(solution)/shard_map/ppermute | solution.py:514
  69.8 4.2 %collective-permute-start.21 = (f32[112,128]{1,0:T(8,128)S(1)}, f32[112,128]{1,0:T(8,128)S(1)}, u32[]{:S(2)}, u32[]{:S(2)}) collective-permute-start(f32[112,128]{1,0:T(8,128)S(1)} %subtract_maximum_fusion.1.mine), channel_id=1, source_target_pairs={{0,1},{1,0},{2,3},{3,2},{4,5},{5,4},{6,7},{7,6},{8,9},{9,8},{10,11... | collective-permute-start | bytes 172040 | tf_op jit(solution)/shard_map/ppermute | solution.py:489
  73.9 2.4 %shard_map.89 = (f32[24,64,128]{2,1,0:T(8,128)S(1)}, f32[64,256]{1,0:T(8,128)S(1)}, f32[16,64,128]{2,1,0:T(8,128)S(1)}) custom-call(f32[24,64,128]{2,1,0:T(8,128)S(1)} %get-tuple-element.178.ext_ref, f32[64,256]{1,0:T(8,128)S(1)} %get-tuple-element.179.side_ref, f32[12,64,256]{2,1,0:T(8,128)S(1)} %get-tuple-element.198.acc, ...), custom_call_target="tpu_custom_call" | custom-call | flops 2875000064 | bytes 9250000 | tf_op jit(solution)/shard_map/pallas_call | solution.py:473
  76.3 3.5 %shard_map.90 = (f32[112,128]{1,0:T(8,128)S(1)}, f32[176,128]{1,0:T(8,128)S(1)}, f32[4,64,128]{2,1,0:T(8,128)S(1)}, f32[4,64,128]{2,1,0:T(8,128)S(1)}, f32[64,12...) custom-call(f32[16,448,128]{2,1,0:T(8,128)S(1)} %get-tuple-element.140.obs_ref, f32[16,128]{1,0:T(8,128)S(1)} %copy-done.4, ...), custom_call_target="tpu_custom_call" | custom-call | flops 5750000128 | bytes 18500000 | tf_op jit(solution)/shard_map/pallas_call | solution.py:473
  82.5 2.0 %collective-permute-start.25 = (f32[176,128]{1,0:T(8,128)S(1)}, f32[176,128]{1,0:T(8,128)S(1)}, u32[]{:S(2)}, u32[]{:S(2)}) collective-permute-start(f32[176,128]{1,0:T(8,128)S(1)} %constant_dynamic-update-slice_fusion.8), channel_id=1, source_target_pairs={{0,3},{1,6},{2,5},{3,0},{4,7},{5,2},{6,1},{7,4},{8,11},{9,14},{10,... | collective-permute-start | bytes 270344 | tf_op jit(solution)/shard_map/ppermute | solution.py:509
  86.2 2.2 %collective-permute-done.25 = f32[176,128]{1,0:T(8,128)S(1)} collective-permute-done((f32[176,128]{1,0:T(8,128)S(1)}, f32[176,128]{1,0:T(8,128)S(1)}, u32[]{:S(2)}, u32[]{:S(2)}) %collective-permute-start.25) | collective-permute-done | bytes 90144 | tf_op jit(solution)/shard_map/ppermute | solution.py:509
  94.5 2.8 %collective-permute-done.27 = f32[176,128]{1,0:T(8,128)S(1)} collective-permute-done((f32[176,128]{1,0:T(8,128)S(1)}, f32[176,128]{1,0:T(8,128)S(1)}, u32[]{:S(2)}, u32[]{:S(2)}) %collective-permute-start.27) | collective-permute-done | bytes 90144 | tf_op jit(solution)/shard_map/ppermute | solution.py:514
  98.7 2.0 %shard_map.93 = f32[64,16,128]{2,1,0:T(8,128)} custom-call(f32[24,64,128]{2,1,0:T(8,128)S(1)} %get-tuple-element.202.ext_ref, f32[64,256]{1,0:T(8,128)S(1)} %get-tuple-element.203.side_ref, f32[12,64,256]{2,1,0:T(8,128)S(1)} %get-tuple-element.219.acc, f32[64,256]{1,0:T(8,128)S(1)} %get-tuple-element.220.near_ref, f32[64,128]{1,0:T(8,128)S(1)} %get-tuple-element.226.left, ...), custom_call_target="tpu_custom_call" | custom-call | flops 1724999936 | bytes 5550000 | tf_op jit(solution)/shard_map/pallas_call | solution.py:473
  (113 shorter events, 35.4 us)
Async XLA Ops:
  8.2 7.5 %collective-permute-start.2 = (f32[344,128]{1,0:T(8,128)S(1)}, f32[344,128]{1,0:T(8,128)S(1)}, u32[]{:S(2)}, u32[]{:S(2)}) collective-permute-start(f32[344,128]{1,0:T(8,128)S(1)} %constant_dynamic-update-slice_fusion), channel_id=1, source_target_pairs={{0,8},{8,0},{16,24},{24,16},{1,9},{9,1},{17,25},{25,17},{2,10},{10... | collective-permute-start | bytes 528392 | tf_op jit(solution)/shard_map/ppermute | solution.py:499
  10.5 5.2 %collective-permute-start.3 = (f32[344,128]{1,0:T(8,128)S(1)}, f32[344,128]{1,0:T(8,128)S(1)}, u32[]{:S(2)}, u32[]{:S(2)}) collective-permute-start(f32[344,128]{1,0:T(8,128)S(1)} %get-tuple-element.233), channel_id=1, source_target_pairs={{0,0},{8,16},{16,8},{24,24},{1,1},{9,17},{17,9},{25,25},{2,2},{10,... | collective-permute-start | bytes 528392 | tf_op jit(solution)/shard_map/ppermute | solution.py:504
  23.2 6.1 %collective-permute-start.5 = (f32[176,128]{1,0:T(8,128)S(1)}, f32[176,128]{1,0:T(8,128)S(1)}, u32[]{:S(2)}, u32[]{:S(2)}) collective-permute-start(f32[176,128]{1,0:T(8,128)S(1)} %pad_maximum_fusion.6), channel_id=1, source_target_pairs={{0,7},{1,2},{2,1},{3,4},{4,3},{5,6},{6,5},{7,0},{8,15},{9,10},{10,... | collective-permute-start | bytes 270344 | tf_op jit(solution)/shard_map/ppermute | solution.py:494
  24.6 15.2 %collective-permute-start.10 = (f32[8,64,128]{2,1,0:T(8,128)S(1)}, f32[8,64,128]{2,1,0:T(8,128)S(1)}, u32[]{:S(2)}, u32[]{:S(2)}) collective-permute-start(f32[8,64,128]{2,1,0:T(8,128)S(1)} %get-tuple-element.159), channel_id=1, source_target_pairs={{0,8},{8,0},{16,24},{24,16},{1,9},{9,1},{17,25},{25,17},{2,10},{10... | collective-permute-start | bytes 786440 | tf_op jit(solution)/shard_map/ppermute | solution.py:499
  28.5 14.4 %collective-permute-start.8 = (f32[8,64,128]{2,1,0:T(8,128)S(1)}, f32[8,64,128]{2,1,0:T(8,128)S(1)}, u32[]{:S(2)}, u32[]{:S(2)}) collective-permute-start(f32[8,64,128]{2,1,0:T(8,128)S(1)} %get-tuple-element.156), channel_id=1, source_target_pairs={{0,0},{8,16},{16,8},{24,24},{1,1},{9,17},{17,9},{25,25},{2,2},{10,... | collective-permute-start | bytes 786440 | tf_op jit(solution)/shard_map/ppermute | solution.py:504
  29.3 4.9 %collective-permute-start.6 = (f32[112,128]{1,0:T(8,128)S(1)}, f32[112,128]{1,0:T(8,128)S(1)}, u32[]{:S(2)}, u32[]{:S(2)}) collective-permute-start(f32[112,128]{1,0:T(8,128)S(1)} %slice_add_fusion.5), channel_id=1, source_target_pairs={{0,4},{1,5},{2,6},{3,7},{4,0},{5,1},{6,2},{7,3},{8,12},{9,13},{10,... | collective-permute-start | bytes 172040 | tf_op jit(solution)/shard_map/ppermute | solution.py:509
  34.3 10.1 %collective-permute-start.11 = (f32[112,128]{1,0:T(8,128)S(1)}, f32[112,128]{1,0:T(8,128)S(1)}, u32[]{:S(2)}, u32[]{:S(2)}) collective-permute-start(f32[112,128]{1,0:T(8,128)S(1)} %add.79), channel_id=1, source_target_pairs={{0,16},{8,24},{16,0},{24,8},{1,17},{9,25},{17,1},{25,9},{2,18},{10... | collective-permute-start | bytes 172040 | tf_op jit(solution)/shard_map/ppermute | solution.py:514
  38.1 4.8 %collective-permute-start.7 = (f32[176,128]{1,0:T(8,128)S(1)}, f32[176,128]{1,0:T(8,128)S(1)}, u32[]{:S(2)}, u32[]{:S(2)}) collective-permute-start(f32[176,128]{1,0:T(8,128)S(1)} %get-tuple-element.257), channel_id=1, source_target_pairs={{0,8},{8,0},{16,24},{24,16},{1,9},{9,1},{17,25},{25,17},{2,10},{10... | collective-permute-start | bytes 270344 | tf_op jit(solution)/shard_map/ppermute | solution.py:499
  38.2 6.2 %collective-permute-start.9 = (f32[176,128]{1,0:T(8,128)S(1)}, f32[176,128]{1,0:T(8,128)S(1)}, u32[]{:S(2)}, u32[]{:S(2)}) collective-permute-start(f32[176,128]{1,0:T(8,128)S(1)} %get-tuple-element.256), channel_id=1, source_target_pairs={{0,24},{8,16},{16,8},{24,0},{1,25},{9,17},{17,9},{25,1},{2,26},{10... | collective-permute-start | bytes 270344 | tf_op jit(solution)/shard_map/ppermute | solution.py:514
  44.4 4.4 %collective-permute-start.12 = (f32[112,128]{1,0:T(8,128)S(1)}, f32[112,128]{1,0:T(8,128)S(1)}, u32[]{:S(2)}, u32[]{:S(2)}) collective-permute-start(f32[112,128]{1,0:T(8,128)S(1)} %subtract_maximum_fusion.2.mine), channel_id=1, source_target_pairs={{0,1},{1,0},{2,3},{3,2},{4,5},{5,4},{6,7},{7,6},{8,9},{9,8},{10,11... | collective-permute-start | bytes 172040 | tf_op jit(solution)/shard_map/ppermute | solution.py:489
  53.8 5.2 %collective-permute-start.14 = (f32[176,128]{1,0:T(8,128)S(1)}, f32[176,128]{1,0:T(8,128)S(1)}, u32[]{:S(2)}, u32[]{:S(2)}) collective-permute-start(f32[176,128]{1,0:T(8,128)S(1)} %pad_maximum_fusion.7), channel_id=1, source_target_pairs={{0,7},{1,2},{2,1},{3,4},{4,3},{5,6},{6,5},{7,0},{8,15},{9,10},{10,... | collective-permute-start | bytes 270344 | tf_op jit(solution)/shard_map/ppermute | solution.py:494
  55.4 10.7 %collective-permute-start.18 = (f32[8,64,128]{2,1,0:T(8,128)S(1)}, f32[8,64,128]{2,1,0:T(8,128)S(1)}, u32[]{:S(2)}, u32[]{:S(2)}) collective-permute-start(f32[8,64,128]{2,1,0:T(8,128)S(1)} %get-tuple-element.194), channel_id=1, source_target_pairs={{0,8},{8,0},{16,24},{24,16},{1,9},{9,1},{17,25},{25,17},{2,10},{10... | collective-permute-start | bytes 786440 | tf_op jit(solution)/shard_map/ppermute | solution.py:499
  55.8 10.3 %collective-permute-start.19 = (f32[8,64,128]{2,1,0:T(8,128)S(1)}, f32[8,64,128]{2,1,0:T(8,128)S(1)}, u32[]{:S(2)}, u32[]{:S(2)}) collective-permute-start(f32[8,64,128]{2,1,0:T(8,128)S(1)} %get-tuple-element.195), channel_id=1, source_target_pairs={{0,0},{8,16},{16,8},{24,24},{1,1},{9,17},{17,9},{25,25},{2,2},{10,... | collective-permute-start | bytes 786440 | tf_op jit(solution)/shard_map/ppermute | solution.py:504
  62.4 7.4 %collective-permute-start.20 = (f32[112,128]{1,0:T(8,128)S(1)}, f32[112,128]{1,0:T(8,128)S(1)}, u32[]{:S(2)}, u32[]{:S(2)}) collective-permute-start(f32[112,128]{1,0:T(8,128)S(1)} %add.85), channel_id=1, source_target_pairs={{0,16},{8,24},{16,0},{24,8},{1,17},{9,25},{17,1},{25,9},{2,18},{10... | collective-permute-start | bytes 172040 | tf_op jit(solution)/shard_map/ppermute | solution.py:514
  64.3 5.5 %collective-permute-start.17 = (f32[176,128]{1,0:T(8,128)S(1)}, f32[176,128]{1,0:T(8,128)S(1)}, u32[]{:S(2)}, u32[]{:S(2)}) collective-permute-start(f32[176,128]{1,0:T(8,128)S(1)} %get-tuple-element.254), channel_id=1, source_target_pairs={{0,24},{8,16},{16,8},{24,0},{1,25},{9,17},{17,9},{25,1},{2,26},{10... | collective-permute-start | bytes 270344 | tf_op jit(solution)/shard_map/ppermute | solution.py:514
  69.8 6.5 %collective-permute-start.21 = (f32[112,128]{1,0:T(8,128)S(1)}, f32[112,128]{1,0:T(8,128)S(1)}, u32[]{:S(2)}, u32[]{:S(2)}) collective-permute-start(f32[112,128]{1,0:T(8,128)S(1)} %subtract_maximum_fusion.1.mine), channel_id=1, source_target_pairs={{0,1},{1,0},{2,3},{3,2},{4,5},{5,4},{6,7},{7,6},{8,9},{9,8},{10,11... | collective-permute-start | bytes 172040 | tf_op jit(solution)/shard_map/ppermute | solution.py:489
  81.2 4.9 %collective-permute-start.23 = (f32[176,128]{1,0:T(8,128)S(1)}, f32[176,128]{1,0:T(8,128)S(1)}, u32[]{:S(2)}, u32[]{:S(2)}) collective-permute-start(f32[176,128]{1,0:T(8,128)S(1)} %constant_dynamic-update-slice_fusion.8), channel_id=1, source_target_pairs={{0,7},{1,2},{2,1},{3,4},{4,3},{5,6},{6,5},{7,0},{8,15},{9,10},{10,... | collective-permute-start | bytes 270344 | tf_op jit(solution)/shard_map/ppermute | solution.py:494
  81.4 4.7 %collective-permute-start.24 = (f32[176,128]{1,0:T(8,128)S(1)}, f32[176,128]{1,0:T(8,128)S(1)}, u32[]{:S(2)}, u32[]{:S(2)}) collective-permute-start(f32[176,128]{1,0:T(8,128)S(1)} %constant_dynamic-update-slice_fusion.8), channel_id=1, source_target_pairs={{0,4},{1,5},{2,6},{3,7},{4,0},{5,1},{6,2},{7,3},{8,12},{9,13},{10,... | collective-permute-start | bytes 270344 | tf_op jit(solution)/shard_map/ppermute | solution.py:509
  82.5 5.8 %collective-permute-start.25 = (f32[176,128]{1,0:T(8,128)S(1)}, f32[176,128]{1,0:T(8,128)S(1)}, u32[]{:S(2)}, u32[]{:S(2)}) collective-permute-start(f32[176,128]{1,0:T(8,128)S(1)} %constant_dynamic-update-slice_fusion.8), channel_id=1, source_target_pairs={{0,3},{1,6},{2,5},{3,0},{4,7},{5,2},{6,1},{7,4},{8,11},{9,14},{10,... | collective-permute-start | bytes 270344 | tf_op jit(solution)/shard_map/ppermute | solution.py:509
  84.5 8.8 %collective-permute-start.28 = (f32[4,64,128]{2,1,0:T(8,128)S(1)}, f32[4,64,128]{2,1,0:T(8,128)S(1)}, u32[]{:S(2)}, u32[]{:S(2)}) collective-permute-start(f32[4,64,128]{2,1,0:T(8,128)S(1)} %get-tuple-element.215), channel_id=1, source_target_pairs={{0,8},{8,0},{16,24},{24,16},{1,9},{9,1},{17,25},{25,17},{2,10},{10... | collective-permute-start | bytes 393224 | tf_op jit(solution)/shard_map/ppermute | solution.py:499
  85.2 8.1 %collective-permute-start.29 = (f32[4,64,128]{2,1,0:T(8,128)S(1)}, f32[4,64,128]{2,1,0:T(8,128)S(1)}, u32[]{:S(2)}, u32[]{:S(2)}) collective-permute-start(f32[4,64,128]{2,1,0:T(8,128)S(1)} %get-tuple-element.216), channel_id=1, source_target_pairs={{0,0},{8,16},{16,8},{24,24},{1,1},{9,17},{17,9},{25,25},{2,2},{10,... | collective-permute-start | bytes 393224 | tf_op jit(solution)/shard_map/ppermute | solution.py:504
  88.3 9.0 %collective-permute-start.30 = (f32[112,128]{1,0:T(8,128)S(1)}, f32[112,128]{1,0:T(8,128)S(1)}, u32[]{:S(2)}, u32[]{:S(2)}) collective-permute-start(f32[112,128]{1,0:T(8,128)S(1)} %fusion), channel_id=1, source_target_pairs={{0,16},{8,24},{16,0},{24,8},{1,17},{9,25},{17,1},{25,9},{2,18},{10... | collective-permute-start | bytes 172040 | tf_op jit(solution)/shard_map/ppermute | solution.py:514
  89.2 5.3 %collective-permute-start.26 = (f32[176,128]{1,0:T(8,128)S(1)}, f32[176,128]{1,0:T(8,128)S(1)}, u32[]{:S(2)}, u32[]{:S(2)}) collective-permute-start(f32[176,128]{1,0:T(8,128)S(1)} %get-tuple-element.253), channel_id=1, source_target_pairs={{0,8},{8,0},{16,24},{24,16},{1,9},{9,1},{17,25},{25,17},{2,10},{10... | collective-permute-start | bytes 270344 | tf_op jit(solution)/shard_map/ppermute | solution.py:499
  90.8 6.5 %collective-permute-start.27 = (f32[176,128]{1,0:T(8,128)S(1)}, f32[176,128]{1,0:T(8,128)S(1)}, u32[]{:S(2)}, u32[]{:S(2)}) collective-permute-start(f32[176,128]{1,0:T(8,128)S(1)} %get-tuple-element.252), channel_id=1, source_target_pairs={{0,24},{8,16},{16,8},{24,0},{1,25},{9,17},{17,9},{25,1},{2,26},{10... | collective-permute-start | bytes 270344 | tf_op jit(solution)/shard_map/ppermute | solution.py:514
  (13 other events, 52.6 us)

commit v7 on v6

--- a/solution.py
+++ b/solution.py
@@ -119,13 +119,23 @@
     return total
 
 
+def toeplitz(taps, delta):
+    height, width = delta.shape
+    lane = lanes((8, width))
+    line = jnp.zeros((8, width), F32)
+    for v in range(KS):
+        line = jnp.where(lane == (RADIUS - v) % width, taps[v], line)
+    rolled = pltpu.roll(jnp.concatenate([line] * (height // 8), axis=0), 0, 1, stride=1, stride_axis=0)
+    return jnp.where((delta >= 0) & (delta < KS), rolled, 0.0)
+
+
 def build_main(taps, w_high, w_low, index, width):
     shape = (width, width)
     delta = lax.broadcasted_iota(jnp.int32, shape, 0) - lax.broadcasted_iota(jnp.int32, shape, 1) + RADIUS
     blank = jnp.zeros(shape, BF16)
     for u in range(-1, KS + 1):
         if 0 <= u < KS:
-            high, low = split(band_sum([taps(u, v) for v in range(KS)], delta))
+            high, low = split(toeplitz([taps(u, v) for v in range(KS)], delta))
         else:
             high, low = blank, blank
         for r in range(2):

time: 102 us -> 100 us (0.980)
  Pallas kernels: 37.8 us -> 36.6 us
  starting transfers between devices: 43.4 us -> 42.3 us
  waiting for transfers between devices: 15.7 us -> 16.8 us
    pallas_call x18, Pallas kernels: 37.8 us -> 36.6 us  [call(): pl.pallas_call(kernel, out_shape=[jax.ShapeDtypeStruct(s, d) for s, d in...]
    ppermute x4, waiting for transfers between devices: 4.06 us -> 5.13 us  [cross_swap(): lax.ppermute(x, 'cols', [(i, (i + 1 if i % 2 else i - 1) % count) for i i...]
  transfers between devices with their start and end apart: 32 -> 32, of which waited for: 12 -> 12; matrix products, arithmetic and copies ran while one was open for 0% -> 0% of each run, Pallas kernels for 24% -> 23%
where the time goes in v7:
time: 100 us
  starting transfers between devices  42.3 us (42%)
  Pallas kernels  36.6 us (37%)
  waiting for transfers between devices  16.8 us (17%)
  between operations  2.06 us (2%)
  local copies, waits for them, and re-layouts  1.29 us (1%)
  other arithmetic  1.16 us (1%)
    pallas_call x18, Pallas kernels, call(): pl.pallas_call(kernel, out_shape=[jax.ShapeDtypeStruct(s, d) for s, d in...  36.6 us
    ppermute x6, starting transfers between devices, row_swap(): return lax.ppermute(x, 'rows', [(i, i ^ mask) for i in range(count)])  11.2 us
    ppermute x7, starting transfers between devices, pair_one(): return lax.ppermute(x, 'rows', [(i, i ^ 1) for i in range(count)])  9.03 us
    ppermute x7, starting transfers between devices, core_swap(): return lax.ppermute(x, 'cols', [(i, i ^ 1) for i in range(count)])  8.84 us
    ppermute x4, starting transfers between devices, cross_swap(): lax.ppermute(x, 'cols', [(i, (i + 1 if i % 2 else i - 1) % count) for i i...  5.19 us
    ppermute x4, waiting for transfers between devices, cross_swap(): lax.ppermute(x, 'cols', [(i, (i + 1 if i % 2 else i - 1) % count) for i i...  5.13 us
    ppermute x4, starting transfers between devices, col_swap(): lax.ppermute(x, 'cols', [(i, (((i + 1) % count ^ mask) - 1) % count) for...  4.92 us
    ppermute x6, waiting for transfers between devices, row_swap(): return lax.ppermute(x, 'rows', [(i, i ^ mask) for i in range(count)])  4.73 us
  transfers between devices with their start and end apart: 32, of which 12 were waited for; matrix products, arithmetic and copies ran while one was open for 0% of the time, Pallas kernels for 23%

profile of v7, /device:TPU:1, one launch (start us, length us, event | category | flops | bytes accessed | tf_op | source)
XLA Modules:
  0.0 100.2 jit_solution(6711245616134057495)
XLA Ops:
  3.9 2.6 %collective-permute-start.1 = (f32[72,128]{1,0:T(8,128)S(1)}, f32[72,128]{1,0:T(8,128)S(1)}, u32[]{:S(2)}, u32[]{:S(2)}) collective-permute-start(f32[72,128]{1,0:T(8,128)S(1)} %get-tuple-element.119), channel_id=1, source_target_pairs={{0,7},{1,2},{2,1},{3,4},{4,3},{5,6},{6,5},{7,0},{8,15},{9,10},{10,... | collective-permute-start | bytes 110600 | tf_op jit(solution)/shard_map/ppermute | solution.py:504
  8.2 2.3 %collective-permute-start.2 = (f32[344,128]{1,0:T(8,128)S(1)}, f32[344,128]{1,0:T(8,128)S(1)}, u32[]{:S(2)}, u32[]{:S(2)}) collective-permute-start(f32[344,128]{1,0:T(8,128)S(1)} %constant_dynamic-update-slice_fusion), channel_id=1, source_target_pairs={{0,8},{8,0},{16,24},{24,16},{1,9},{9,1},{17,25},{25,17},{2,10},{10... | collective-permute-start | bytes 528392 | tf_op jit(solution)/shard_map/ppermute | solution.py:509
  11.2 4.2 %shard_map.78 = (f32[16,448,128]{2,1,0:T(8,128)S(1)}, f32[112,128]{1,0:T(8,128)S(1)}, f32[112,128]{1,0:T(8,128)S(1)}, bf16[5,256,256]{2,1,0:T(8,128)(2,1)S(1)}, ...) custom-call(s32[1,1]{1,0:T(1,128)S(6)} %copy.29.family, ...), custom_call_target="tpu_custom_call" | custom-call | flops 3449999872 | bytes 11100000 | tf_op jit(solution)/shard_map/pallas_call | solution.py:483
  15.4 2.0 %shard_map.79 = (f32[24,64,128]{2,1,0:T(8,128)S(1)}, f32[64,256]{1,0:T(8,128)S(1)}, f32[16,64,128]{2,1,0:T(8,128)S(1)}) custom-call(f32[16,64,128]{2,1,0:T(8,128)S(1)} %get-tuple-element.115.rows_ref, f32[344,128]{1,0:T(8,128)S(1)} %collective-permute-done.2.p1, f32[344,128]{1,0:T(8,128)S(1)} %collective-permute-done.3.p2, ...), custom_call_target="tpu_custom_call" | custom-call | flops 2300000000 | bytes 7400000 | tf_op jit(solution)/shard_map/pallas_call | solution.py:483
  17.5 3.5 %shard_map.80 = (f32[112,128]{1,0:T(8,128)S(1)}, f32[176,128]{1,0:T(8,128)S(1)}, f32[8,64,128]{2,1,0:T(8,128)S(1)}, f32[8,64,128]{2,1,0:T(8,128)S(1)}, f32[64,12...) custom-call(f32[16,448,128]{2,1,0:T(8,128)S(1)} %get-tuple-element.140.obs_ref, f32[16,128]{1,0:T(8,128)S(1)} %copy-done.4, ...), custom_call_target="tpu_custom_call" | custom-call | flops 5750000128 | bytes 18500000 | tf_op jit(solution)/shard_map/pallas_call | solution.py:483
  24.2 4.2 %collective-permute-start.10 = (f32[8,64,128]{2,1,0:T(8,128)S(1)}, f32[8,64,128]{2,1,0:T(8,128)S(1)}, u32[]{:S(2)}, u32[]{:S(2)}) collective-permute-start(f32[8,64,128]{2,1,0:T(8,128)S(1)} %get-tuple-element.159), channel_id=1, source_target_pairs={{0,8},{8,0},{16,24},{24,16},{1,9},{9,1},{17,25},{25,17},{2,10},{10... | collective-permute-start | bytes 786440 | tf_op jit(solution)/shard_map/ppermute | solution.py:509
  30.7 3.0 %shard_map.81 = (bf16[2,5,256,256]{3,2,1,0:T(8,128)(2,1)S(1)}, bf16[2,5,256,256]{3,2,1,0:T(8,128)(2,1)S(1)}, bf16[768,512]{1,0:T(8,128)(2,1)S(1)}, bf16[768,512]{1,0:T(8,128)(2,1)S(1)}) custom-call(f32[24,128]{1,0:T(8,128)S(1)} %get-tuple-element.243.marks_up, f32[24,128]{1,0:T(8,128)S(1)} %pad_maximum_fusion.8.marks, ...), custom_call_target="tpu_custom_call" | custom-call | flops 3449999872 | bytes 11100000 | tf_op jit(solution)/shard_map/pallas_call | solution.py:483
  33.7 3.8 %collective-permute-start.11 = (f32[112,128]{1,0:T(8,128)S(1)}, f32[112,128]{1,0:T(8,128)S(1)}, u32[]{:S(2)}, u32[]{:S(2)}) collective-permute-start(f32[112,128]{1,0:T(8,128)S(1)} %add.79), channel_id=1, source_target_pairs={{0,16},{8,24},{16,0},{24,8},{1,17},{9,25},{17,1},{25,9},{2,18},{10... | collective-permute-start | bytes 172040 | tf_op jit(solution)/shard_map/ppermute | solution.py:524
  37.6 1.6 %collective-permute-start.9 = (f32[176,128]{1,0:T(8,128)S(1)}, f32[176,128]{1,0:T(8,128)S(1)}, u32[]{:S(2)}, u32[]{:S(2)}) collective-permute-start(f32[176,128]{1,0:T(8,128)S(1)} %get-tuple-element.256), channel_id=1, source_target_pairs={{0,24},{8,16},{16,8},{24,0},{1,25},{9,17},{17,9},{25,1},{2,26},{10... | collective-permute-start | bytes 270344 | tf_op jit(solution)/shard_map/ppermute | solution.py:524
  43.9 2.3 %collective-permute-start.12 = (f32[112,128]{1,0:T(8,128)S(1)}, f32[112,128]{1,0:T(8,128)S(1)}, u32[]{:S(2)}, u32[]{:S(2)}) collective-permute-start(f32[112,128]{1,0:T(8,128)S(1)} %subtract_maximum_fusion.2.mine), channel_id=1, source_target_pairs={{0,1},{1,0},{2,3},{3,2},{4,5},{5,4},{6,7},{7,6},{8,9},{9,8},{10,11... | collective-permute-start | bytes 172040 | tf_op jit(solution)/shard_map/ppermute | solution.py:499
  46.2 2.4 %shard_map.85 = (f32[24,64,128]{2,1,0:T(8,128)S(1)}, f32[64,256]{1,0:T(8,128)S(1)}, f32[16,64,128]{2,1,0:T(8,128)S(1)}) custom-call(f32[24,64,128]{2,1,0:T(8,128)S(1)} %get-tuple-element.138.ext_ref, f32[64,256]{1,0:T(8,128)S(1)} %get-tuple-element.139.side_ref, f32[12,64,256]{2,1,0:T(8,128)S(1)} %get-tuple-element.172.acc, ...), custom_call_target="tpu_custom_call" | custom-call | flops 2875000064 | bytes 9250000 | tf_op jit(solution)/shard_map/pallas_call | solution.py:483
  48.6 3.5 %shard_map.86 = (f32[112,128]{1,0:T(8,128)S(1)}, f32[176,128]{1,0:T(8,128)S(1)}, f32[8,64,128]{2,1,0:T(8,128)S(1)}, f32[8,64,128]{2,1,0:T(8,128)S(1)}, f32[64,12...) custom-call(f32[16,448,128]{2,1,0:T(8,128)S(1)} %get-tuple-element.140.obs_ref, f32[16,128]{1,0:T(8,128)S(1)} %copy-done.4, ...), custom_call_target="tpu_custom_call" | custom-call | flops 5750000128 | bytes 18500000 | tf_op jit(solution)/shard_map/pallas_call | solution.py:483
  56.2 2.2 %collective-permute-done.14 = f32[176,128]{1,0:T(8,128)S(1)} collective-permute-done((f32[176,128]{1,0:T(8,128)S(1)}, f32[176,128]{1,0:T(8,128)S(1)}, u32[]{:S(2)}, u32[]{:S(2)}) %collective-permute-start.14) | collective-permute-done | bytes 90144 | tf_op jit(solution)/shard_map/ppermute | solution.py:504
  63.8 1.7 %collective-permute-start.17 = (f32[176,128]{1,0:T(8,128)S(1)}, f32[176,128]{1,0:T(8,128)S(1)}, u32[]{:S(2)}, u32[]{:S(2)}) collective-permute-start(f32[176,128]{1,0:T(8,128)S(1)} %get-tuple-element.254), channel_id=1, source_target_pairs={{0,24},{8,16},{16,8},{24,0},{1,25},{9,17},{17,9},{25,1},{2,26},{10... | collective-permute-start | bytes 270344 | tf_op jit(solution)/shard_map/ppermute | solution.py:524
  66.9 2.4 %collective-permute-done.17 = f32[176,128]{1,0:T(8,128)S(1)} collective-permute-done((f32[176,128]{1,0:T(8,128)S(1)}, f32[176,128]{1,0:T(8,128)S(1)}, u32[]{:S(2)}, u32[]{:S(2)}) %collective-permute-start.17) | collective-permute-done | bytes 90144 | tf_op jit(solution)/shard_map/ppermute | solution.py:524
  69.4 3.3 %collective-permute-start.21 = (f32[112,128]{1,0:T(8,128)S(1)}, f32[112,128]{1,0:T(8,128)S(1)}, u32[]{:S(2)}, u32[]{:S(2)}) collective-permute-start(f32[112,128]{1,0:T(8,128)S(1)} %subtract_maximum_fusion.1.mine), channel_id=1, source_target_pairs={{0,1},{1,0},{2,3},{3,2},{4,5},{5,4},{6,7},{7,6},{8,9},{9,8},{10,11... | collective-permute-start | bytes 172040 | tf_op jit(solution)/shard_map/ppermute | solution.py:499
  72.7 2.4 %shard_map.89 = (f32[24,64,128]{2,1,0:T(8,128)S(1)}, f32[64,256]{1,0:T(8,128)S(1)}, f32[16,64,128]{2,1,0:T(8,128)S(1)}) custom-call(f32[24,64,128]{2,1,0:T(8,128)S(1)} %get-tuple-element.178.ext_ref, f32[64,256]{1,0:T(8,128)S(1)} %get-tuple-element.179.side_ref, f32[12,64,256]{2,1,0:T(8,128)S(1)} %get-tuple-element.198.acc, ...), custom_call_target="tpu_custom_call" | custom-call | flops 2875000064 | bytes 9250000 | tf_op jit(solution)/shard_map/pallas_call | solution.py:483
  75.1 3.5 %shard_map.90 = (f32[112,128]{1,0:T(8,128)S(1)}, f32[176,128]{1,0:T(8,128)S(1)}, f32[4,64,128]{2,1,0:T(8,128)S(1)}, f32[4,64,128]{2,1,0:T(8,128)S(1)}, f32[64,12...) custom-call(f32[16,448,128]{2,1,0:T(8,128)S(1)} %get-tuple-element.140.obs_ref, f32[16,128]{1,0:T(8,128)S(1)} %copy-done.4, ...), custom_call_target="tpu_custom_call" | custom-call | flops 5750000128 | bytes 18500000 | tf_op jit(solution)/shard_map/pallas_call | solution.py:483
  81.4 1.8 %collective-permute-start.25 = (f32[176,128]{1,0:T(8,128)S(1)}, f32[176,128]{1,0:T(8,128)S(1)}, u32[]{:S(2)}, u32[]{:S(2)}) collective-permute-start(f32[176,128]{1,0:T(8,128)S(1)} %constant_dynamic-update-slice_fusion.8), channel_id=1, source_target_pairs={{0,3},{1,6},{2,5},{3,0},{4,7},{5,2},{6,1},{7,4},{8,11},{9,14},{10,... | collective-permute-start | bytes 270344 | tf_op jit(solution)/shard_map/ppermute | solution.py:519
  85.3 2.0 %collective-permute-done.25 = f32[176,128]{1,0:T(8,128)S(1)} collective-permute-done((f32[176,128]{1,0:T(8,128)S(1)}, f32[176,128]{1,0:T(8,128)S(1)}, u32[]{:S(2)}, u32[]{:S(2)}) %collective-permute-start.25) | collective-permute-done | bytes 90144 | tf_op jit(solution)/shard_map/ppermute | solution.py:519
  89.3 1.7 %collective-permute-start.27 = (f32[176,128]{1,0:T(8,128)S(1)}, f32[176,128]{1,0:T(8,128)S(1)}, u32[]{:S(2)}, u32[]{:S(2)}) collective-permute-start(f32[176,128]{1,0:T(8,128)S(1)} %get-tuple-element.252), channel_id=1, source_target_pairs={{0,24},{8,16},{16,8},{24,0},{1,25},{9,17},{17,9},{25,1},{2,26},{10... | collective-permute-start | bytes 270344 | tf_op jit(solution)/shard_map/ppermute | solution.py:524
  93.4 1.8 %collective-permute-done.27 = f32[176,128]{1,0:T(8,128)S(1)} collective-permute-done((f32[176,128]{1,0:T(8,128)S(1)}, f32[176,128]{1,0:T(8,128)S(1)}, u32[]{:S(2)}, u32[]{:S(2)}) %collective-permute-start.27) | collective-permute-done | bytes 90144 | tf_op jit(solution)/shard_map/ppermute | solution.py:524
  95.4 2.0 %collective-permute-start.31 = (f32[64,256]{1,0:T(8,128)S(1)}, f32[64,256]{1,0:T(8,128)S(1)}, u32[]{:S(2)}, u32[]{:S(2)}) collective-permute-start(f32[64,256]{1,0:T(8,128)S(1)} %shard_map.94), channel_id=1, source_target_pairs={{0,1},{1,0},{2,3},{3,2},{4,5},{5,4},{6,7},{7,6},{8,9},{9,8},{10,11... | collective-permute-start | bytes 196616 | tf_op jit(solution)/shard_map/ppermute | solution.py:499
  97.4 2.0 %shard_map.93 = f32[64,16,128]{2,1,0:T(8,128)} custom-call(f32[24,64,128]{2,1,0:T(8,128)S(1)} %get-tuple-element.202.ext_ref, f32[64,256]{1,0:T(8,128)S(1)} %get-tuple-element.203.side_ref, f32[12,64,256]{2,1,0:T(8,128)S(1)} %get-tuple-element.219.acc, f32[64,256]{1,0:T(8,128)S(1)} %get-tuple-element.220.near_ref, f32[64,128]{1,0:T(8,128)S(1)} %get-tuple-element.226.left, ...), custom_call_target="tpu_custom_call" | custom-call | flops 1724999936 | bytes 5550000 | tf_op jit(solution)/shard_map/pallas_call | solution.py:483
  (113 shorter events, 36.0 us)
Async XLA Ops:
  8.2 7.1 %collective-permute-start.2 = (f32[344,128]{1,0:T(8,128)S(1)}, f32[344,128]{1,0:T(8,128)S(1)}, u32[]{:S(2)}, u32[]{:S(2)}) collective-permute-start(f32[344,128]{1,0:T(8,128)S(1)} %constant_dynamic-update-slice_fusion), channel_id=1, source_target_pairs={{0,8},{8,0},{16,24},{24,16},{1,9},{9,1},{17,25},{25,17},{2,10},{10... | collective-permute-start | bytes 528392 | tf_op jit(solution)/shard_map/ppermute | solution.py:509
  10.5 4.9 %collective-permute-start.3 = (f32[344,128]{1,0:T(8,128)S(1)}, f32[344,128]{1,0:T(8,128)S(1)}, u32[]{:S(2)}, u32[]{:S(2)}) collective-permute-start(f32[344,128]{1,0:T(8,128)S(1)} %get-tuple-element.233), channel_id=1, source_target_pairs={{0,0},{8,16},{16,8},{24,24},{1,1},{9,17},{17,9},{25,25},{2,2},{10,... | collective-permute-start | bytes 528392 | tf_op jit(solution)/shard_map/ppermute | solution.py:514
  22.9 6.4 %collective-permute-start.5 = (f32[176,128]{1,0:T(8,128)S(1)}, f32[176,128]{1,0:T(8,128)S(1)}, u32[]{:S(2)}, u32[]{:S(2)}) collective-permute-start(f32[176,128]{1,0:T(8,128)S(1)} %pad_maximum_fusion.6), channel_id=1, source_target_pairs={{0,7},{1,2},{2,1},{3,4},{4,3},{5,6},{6,5},{7,0},{8,15},{9,10},{10,... | collective-permute-start | bytes 270344 | tf_op jit(solution)/shard_map/ppermute | solution.py:504
  24.2 14.9 %collective-permute-start.10 = (f32[8,64,128]{2,1,0:T(8,128)S(1)}, f32[8,64,128]{2,1,0:T(8,128)S(1)}, u32[]{:S(2)}, u32[]{:S(2)}) collective-permute-start(f32[8,64,128]{2,1,0:T(8,128)S(1)} %get-tuple-element.159), channel_id=1, source_target_pairs={{0,8},{8,0},{16,24},{24,16},{1,9},{9,1},{17,25},{25,17},{2,10},{10... | collective-permute-start | bytes 786440 | tf_op jit(solution)/shard_map/ppermute | solution.py:509
  28.5 13.5 %collective-permute-start.8 = (f32[8,64,128]{2,1,0:T(8,128)S(1)}, f32[8,64,128]{2,1,0:T(8,128)S(1)}, u32[]{:S(2)}, u32[]{:S(2)}) collective-permute-start(f32[8,64,128]{2,1,0:T(8,128)S(1)} %get-tuple-element.156), channel_id=1, source_target_pairs={{0,0},{8,16},{16,8},{24,24},{1,1},{9,17},{17,9},{25,25},{2,2},{10,... | collective-permute-start | bytes 786440 | tf_op jit(solution)/shard_map/ppermute | solution.py:514
  29.3 4.3 %collective-permute-start.6 = (f32[112,128]{1,0:T(8,128)S(1)}, f32[112,128]{1,0:T(8,128)S(1)}, u32[]{:S(2)}, u32[]{:S(2)}) collective-permute-start(f32[112,128]{1,0:T(8,128)S(1)} %slice_add_fusion.5), channel_id=1, source_target_pairs={{0,4},{1,5},{2,6},{3,7},{4,0},{5,1},{6,2},{7,3},{8,12},{9,13},{10,... | collective-permute-start | bytes 172040 | tf_op jit(solution)/shard_map/ppermute | solution.py:519
  33.7 10.2 %collective-permute-start.11 = (f32[112,128]{1,0:T(8,128)S(1)}, f32[112,128]{1,0:T(8,128)S(1)}, u32[]{:S(2)}, u32[]{:S(2)}) collective-permute-start(f32[112,128]{1,0:T(8,128)S(1)} %add.79), channel_id=1, source_target_pairs={{0,16},{8,24},{16,0},{24,8},{1,17},{9,25},{17,1},{25,9},{2,18},{10... | collective-permute-start | bytes 172040 | tf_op jit(solution)/shard_map/ppermute | solution.py:524
  37.5 4.5 %collective-permute-start.7 = (f32[176,128]{1,0:T(8,128)S(1)}, f32[176,128]{1,0:T(8,128)S(1)}, u32[]{:S(2)}, u32[]{:S(2)}) collective-permute-start(f32[176,128]{1,0:T(8,128)S(1)} %get-tuple-element.257), channel_id=1, source_target_pairs={{0,8},{8,0},{16,24},{24,16},{1,9},{9,1},{17,25},{25,17},{2,10},{10... | collective-permute-start | bytes 270344 | tf_op jit(solution)/shard_map/ppermute | solution.py:509
  37.6 6.3 %collective-permute-start.9 = (f32[176,128]{1,0:T(8,128)S(1)}, f32[176,128]{1,0:T(8,128)S(1)}, u32[]{:S(2)}, u32[]{:S(2)}) collective-permute-start(f32[176,128]{1,0:T(8,128)S(1)} %get-tuple-element.256), channel_id=1, source_target_pairs={{0,24},{8,16},{16,8},{24,0},{1,25},{9,17},{17,9},{25,1},{2,26},{10... | collective-permute-start | bytes 270344 | tf_op jit(solution)/shard_map/ppermute | solution.py:524
  43.9 4.7 %collective-permute-start.12 = (f32[112,128]{1,0:T(8,128)S(1)}, f32[112,128]{1,0:T(8,128)S(1)}, u32[]{:S(2)}, u32[]{:S(2)}) collective-permute-start(f32[112,128]{1,0:T(8,128)S(1)} %subtract_maximum_fusion.2.mine), channel_id=1, source_target_pairs={{0,1},{1,0},{2,3},{3,2},{4,5},{5,4},{6,7},{7,6},{8,9},{9,8},{10,11... | collective-permute-start | bytes 172040 | tf_op jit(solution)/shard_map/ppermute | solution.py:499
  53.5 4.9 %collective-permute-start.14 = (f32[176,128]{1,0:T(8,128)S(1)}, f32[176,128]{1,0:T(8,128)S(1)}, u32[]{:S(2)}, u32[]{:S(2)}) collective-permute-start(f32[176,128]{1,0:T(8,128)S(1)} %pad_maximum_fusion.7), channel_id=1, source_target_pairs={{0,7},{1,2},{2,1},{3,4},{4,3},{5,6},{6,5},{7,0},{8,15},{9,10},{10,... | collective-permute-start | bytes 270344 | tf_op jit(solution)/shard_map/ppermute | solution.py:504
  54.3 11.2 %collective-permute-start.18 = (f32[8,64,128]{2,1,0:T(8,128)S(1)}, f32[8,64,128]{2,1,0:T(8,128)S(1)}, u32[]{:S(2)}, u32[]{:S(2)}) collective-permute-start(f32[8,64,128]{2,1,0:T(8,128)S(1)} %get-tuple-element.194), channel_id=1, source_target_pairs={{0,8},{8,0},{16,24},{24,16},{1,9},{9,1},{17,25},{25,17},{2,10},{10... | collective-permute-start | bytes 786440 | tf_op jit(solution)/shard_map/ppermute | solution.py:509
  55.3 10.2 %collective-permute-start.19 = (f32[8,64,128]{2,1,0:T(8,128)S(1)}, f32[8,64,128]{2,1,0:T(8,128)S(1)}, u32[]{:S(2)}, u32[]{:S(2)}) collective-permute-start(f32[8,64,128]{2,1,0:T(8,128)S(1)} %get-tuple-element.195), channel_id=1, source_target_pairs={{0,0},{8,16},{16,8},{24,24},{1,1},{9,17},{17,9},{25,25},{2,2},{10,... | collective-permute-start | bytes 786440 | tf_op jit(solution)/shard_map/ppermute | solution.py:514
  61.8 7.6 %collective-permute-start.20 = (f32[112,128]{1,0:T(8,128)S(1)}, f32[112,128]{1,0:T(8,128)S(1)}, u32[]{:S(2)}, u32[]{:S(2)}) collective-permute-start(f32[112,128]{1,0:T(8,128)S(1)} %add.85), channel_id=1, source_target_pairs={{0,16},{8,24},{16,0},{24,8},{1,17},{9,25},{17,1},{25,9},{2,18},{10... | collective-permute-start | bytes 172040 | tf_op jit(solution)/shard_map/ppermute | solution.py:524
  63.8 5.6 %collective-permute-start.17 = (f32[176,128]{1,0:T(8,128)S(1)}, f32[176,128]{1,0:T(8,128)S(1)}, u32[]{:S(2)}, u32[]{:S(2)}) collective-permute-start(f32[176,128]{1,0:T(8,128)S(1)} %get-tuple-element.254), channel_id=1, source_target_pairs={{0,24},{8,16},{16,8},{24,0},{1,25},{9,17},{17,9},{25,1},{2,26},{10... | collective-permute-start | bytes 270344 | tf_op jit(solution)/shard_map/ppermute | solution.py:524
  69.4 5.7 %collective-permute-start.21 = (f32[112,128]{1,0:T(8,128)S(1)}, f32[112,128]{1,0:T(8,128)S(1)}, u32[]{:S(2)}, u32[]{:S(2)}) collective-permute-start(f32[112,128]{1,0:T(8,128)S(1)} %subtract_maximum_fusion.1.mine), channel_id=1, source_target_pairs={{0,1},{1,0},{2,3},{3,2},{4,5},{5,4},{6,7},{7,6},{8,9},{9,8},{10,11... | collective-permute-start | bytes 172040 | tf_op jit(solution)/shard_map/ppermute | solution.py:499
  80.0 5.3 %collective-permute-start.23 = (f32[176,128]{1,0:T(8,128)S(1)}, f32[176,128]{1,0:T(8,128)S(1)}, u32[]{:S(2)}, u32[]{:S(2)}) collective-permute-start(f32[176,128]{1,0:T(8,128)S(1)} %constant_dynamic-update-slice_fusion.8), channel_id=1, source_target_pairs={{0,7},{1,2},{2,1},{3,4},{4,3},{5,6},{6,5},{7,0},{8,15},{9,10},{10,... | collective-permute-start | bytes 270344 | tf_op jit(solution)/shard_map/ppermute | solution.py:504
  80.4 4.9 %collective-permute-start.24 = (f32[176,128]{1,0:T(8,128)S(1)}, f32[176,128]{1,0:T(8,128)S(1)}, u32[]{:S(2)}, u32[]{:S(2)}) collective-permute-start(f32[176,128]{1,0:T(8,128)S(1)} %constant_dynamic-update-slice_fusion.8), channel_id=1, source_target_pairs={{0,4},{1,5},{2,6},{3,7},{4,0},{5,1},{6,2},{7,3},{8,12},{9,13},{10,... | collective-permute-start | bytes 270344 | tf_op jit(solution)/shard_map/ppermute | solution.py:519
  81.4 5.8 %collective-permute-start.25 = (f32[176,128]{1,0:T(8,128)S(1)}, f32[176,128]{1,0:T(8,128)S(1)}, u32[]{:S(2)}, u32[]{:S(2)}) collective-permute-start(f32[176,128]{1,0:T(8,128)S(1)} %constant_dynamic-update-slice_fusion.8), channel_id=1, source_target_pairs={{0,3},{1,6},{2,5},{3,0},{4,7},{5,2},{6,1},{7,4},{8,11},{9,14},{10,... | collective-permute-start | bytes 270344 | tf_op jit(solution)/shard_map/ppermute | solution.py:519
  83.3 9.0 %collective-permute-start.28 = (f32[4,64,128]{2,1,0:T(8,128)S(1)}, f32[4,64,128]{2,1,0:T(8,128)S(1)}, u32[]{:S(2)}, u32[]{:S(2)}) collective-permute-start(f32[4,64,128]{2,1,0:T(8,128)S(1)} %get-tuple-element.215), channel_id=1, source_target_pairs={{0,8},{8,0},{16,24},{24,16},{1,9},{9,1},{17,25},{25,17},{2,10},{10... | collective-permute-start | bytes 393224 | tf_op jit(solution)/shard_map/ppermute | solution.py:509
  83.3 9.0 %collective-permute-start.29 = (f32[4,64,128]{2,1,0:T(8,128)S(1)}, f32[4,64,128]{2,1,0:T(8,128)S(1)}, u32[]{:S(2)}, u32[]{:S(2)}) collective-permute-start(f32[4,64,128]{2,1,0:T(8,128)S(1)} %get-tuple-element.216), channel_id=1, source_target_pairs={{0,0},{8,16},{16,8},{24,24},{1,1},{9,17},{17,9},{25,25},{2,2},{10,... | collective-permute-start | bytes 393224 | tf_op jit(solution)/shard_map/ppermute | solution.py:514
  87.3 8.0 %collective-permute-start.30 = (f32[112,128]{1,0:T(8,128)S(1)}, f32[112,128]{1,0:T(8,128)S(1)}, u32[]{:S(2)}, u32[]{:S(2)}) collective-permute-start(f32[112,128]{1,0:T(8,128)S(1)} %fusion), channel_id=1, source_target_pairs={{0,16},{8,24},{16,0},{24,8},{1,17},{9,25},{17,1},{25,9},{2,18},{10... | collective-permute-start | bytes 172040 | tf_op jit(solution)/shard_map/ppermute | solution.py:524
  88.6 4.8 %collective-permute-start.26 = (f32[176,128]{1,0:T(8,128)S(1)}, f32[176,128]{1,0:T(8,128)S(1)}, u32[]{:S(2)}, u32[]{:S(2)}) collective-permute-start(f32[176,128]{1,0:T(8,128)S(1)} %get-tuple-element.253), channel_id=1, source_target_pairs={{0,8},{8,0},{16,24},{24,16},{1,9},{9,1},{17,25},{25,17},{2,10},{10... | collective-permute-start | bytes 270344 | tf_op jit(solution)/shard_map/ppermute | solution.py:509
  89.3 5.9 %collective-permute-start.27 = (f32[176,128]{1,0:T(8,128)S(1)}, f32[176,128]{1,0:T(8,128)S(1)}, u32[]{:S(2)}, u32[]{:S(2)}) collective-permute-start(f32[176,128]{1,0:T(8,128)S(1)} %get-tuple-element.252), channel_id=1, source_target_pairs={{0,24},{8,16},{16,8},{24,0},{1,25},{9,17},{17,9},{25,1},{2,26},{10... | collective-permute-start | bytes 270344 | tf_op jit(solution)/shard_map/ppermute | solution.py:524
  (13 other events, 53.7 us)
